TPU v7x, 128 devices: a whole 4x4x4 slice. The times are simulated.
128 devices in a mesh: section: 16 (over z, y), dp: 8 (over x, core).
Axes of the slice: x: 4, y: 4, z: 4, core: 2. Of those that a mesh axis runs over, the one named last changes fastest.
Arguments:
- acts: bfloat16 [16, 3, 384, 8192], P('section', None, 'dp'), may hold values from -6 to 6
- out_grad: bfloat16 [3, 384, 8192], P(None, 'dp'), may hold values from -6 to 6
- w_value: bfloat16 [16, 8192, 512], P('section', 'dp'), may hold values from -0.0625 to 0.0625
- w_output: bfloat16 [16, 512, 8192], P('section', None, 'dp'), may hold values from -0.109375 to 0.109375
- order: int32 [8, 3], P('dp'), may hold values from 0 to 2, each once within a row
- alive: int32 [8], replicated, may hold values from 0 to 1, as said below
- flags: int32 [16, 8], P('section', 'dp'), may hold values 0 or 1
- clip_rms: float32 [1], replicated, may hold values from 0.1 to 0.5
- master: float32 [16, 8192, 1024], P('section', 'dp'), may hold values from -3 to 3
- moment_one: bfloat16 [16, 8192, 1024], P('section', 'dp'), may hold values from -2 to 2
- moment_two: bfloat16 [16, 8192, 1024], P('section', 'dp'), may hold values from 0.0099487305 to 0.5
Outputs:
- new_master: float32 [16, 8192, 1024], P('section', 'dp')
- new_moment_one: bfloat16 [16, 8192, 1024], P('section', 'dp')
- new_moment_two: bfloat16 [16, 8192, 1024], P('section', 'dp')
Inputs may be any that keep to these rules, and one draw needn't show every extreme that they name: Each row of order names each of the 3 micro-batches once. `alive`: 1 marks a surviving replica; at least one replica survives and at least one is lost. `flags`: 1 marks an overflow.
All inputs are finite; a program needn't handle non-finite values. No bound on the sum of `flags` on one device may be relied on, other than what follows from the above.
Results may differ from a plain program's by a relative error of at most 0.009.
Values may be sent and summed in bfloat16 or wider, within the bound.
No kernel may reach another device: no remote copies, remote signals or barrier semaphores. Data moves between devices by JAX's collectives and lax.ppermute only.
A program may use at most 128 MiB of HBM per device.

v0:
```python
import math

import jax
import jax.numpy as jnp
from jax import lax
from jax.sharding import PartitionSpec as P

beta_one = 0.9
beta_two = 0.95
adam_eps = 1e-08
learn_rate = 0.01
weight_decay = 0.1
step_count = 100


def shifted(value, axis, steps):
    count = lax.axis_size(axis)
    leading, last = (max(0, -steps), min(count, count - steps))
    return lax.ppermute(value, axis, [(source, source + steps) for source in range(leading, last)])


def contract_rows(left, right):
    return lax.dot_general(
        left, right, (((1,), (1,)), ((), ())), preferred_element_type=jnp.float32
    )


def contract_tokens(left, right):
    return lax.dot_general(
        left, right, (((0,), (0,)), ((), ())), preferred_element_type=jnp.float32
    )


def shards(
    acts, out_grad, w_value, w_output, order, alive, flags, clip_rms, master, moment_one, moment_two
):
    sections = lax.axis_size("section")
    section_place = lax.axis_index("section")
    value_full, output_full = (
        lax.all_gather(w_value, "dp", axis=1, tiled=True),
        lax.all_gather(w_output, "dp", axis=2, tiled=True),
    )
    value_weight = value_full[0]
    output_weight = output_full[0]
    stash = acts[0]
    micro, tok_rows, width = stash.shape
    head_size = value_weight.shape[1]
    pieces = 1
    piece_rows = tok_rows // pieces
    slots = micro * pieces
    at_end = section_place == sections - 1

    def backward_step(step, received, kept_grad, kept_back):
        slot = step - (sections - 1 - section_place)
        usable = jnp.logical_and(slot >= 0, slot < slots)
        where_to = jnp.clip(slot, 0, slots - 1)
        fresh = lax.dynamic_index_in_dim(out_grad, where_to, 0, keepdims=False)
        gradient = jnp.where(at_end, fresh, received)
        back = contract_rows(gradient, output_weight).astype(jnp.bfloat16)
        lower = (gradient.astype(jnp.float32) + contract_rows(back, value_weight)).astype(
            jnp.bfloat16
        )
        prior_grad = lax.dynamic_index_in_dim(kept_grad, where_to, 0, keepdims=False)
        prior_back = lax.dynamic_index_in_dim(kept_back, where_to, 0, keepdims=False)
        kept_grad = lax.dynamic_update_index_in_dim(
            kept_grad, jnp.where(usable, gradient, prior_grad), where_to, 0
        )
        kept_back = lax.dynamic_update_index_in_dim(
            kept_back, jnp.where(usable, back, prior_back), where_to, 0
        )
        return (lower, kept_grad, kept_back)

    def loop_body(step, carry):
        received, kept_grad, kept_back = carry
        lower, kept_grad, kept_back = backward_step(step, received, kept_grad, kept_back)
        received = shifted(lower, "section", -1)
        return (received, kept_grad, kept_back)

    start_state = (
        jnp.zeros((piece_rows, width), jnp.bfloat16),
        jnp.zeros((slots, piece_rows, width), jnp.bfloat16),
        jnp.zeros((slots, piece_rows, head_size), jnp.bfloat16),
    )
    received, kept_grad, kept_back = lax.fori_loop(0, sections + slots - 2, loop_body, start_state)
    unused, kept_grad, kept_back = backward_step(
        sections + slots - 2, received, kept_grad, kept_back
    )
    grad_rows = kept_grad.reshape(micro * tok_rows, width)
    back_rows = kept_back.reshape(micro * tok_rows, head_size)
    picked = jnp.take(stash, order[0], axis=0).reshape(micro * tok_rows, width)
    hidden = jnp.dot(picked, value_weight, preferred_element_type=jnp.float32).astype(jnp.bfloat16)
    keep = (alive[lax.axis_index("dp")] * (1 - flags[0, 0])).astype(jnp.float32)
    value_part = contract_tokens(picked, back_rows)
    output_part = contract_tokens(grad_rows, hidden)
    summed = lax.psum_scatter(
        (keep * jnp.concatenate([value_part, output_part], axis=1)).astype(jnp.bfloat16),
        "dp",
        scatter_dimension=0,
        tiled=True,
    ).astype(jnp.float32)
    contributors = jnp.maximum(lax.psum(keep, "dp"), 1.0)
    grad_share = summed / contributors
    total_square = lax.psum(jnp.sum(grad_share * grad_share), ("section", "dp"))
    norm = jnp.sqrt(total_square)
    threshold = clip_rms[0] * math.sqrt(2 * width * head_size * sections)
    factor = jnp.minimum(1.0, threshold / (norm + 1e-06))
    scaled = factor * grad_share
    new_one = beta_one * moment_one[0].astype(jnp.float32) + (1.0 - beta_one) * scaled
    new_two = beta_two * moment_two[0].astype(jnp.float32) + (1.0 - beta_two) * scaled * scaled
    hat_one = new_one / (1.0 - beta_one**step_count)
    hat_two = new_two / (1.0 - beta_two**step_count)
    old_master = master[0]
    new_master = old_master - learn_rate * (
        hat_one / (jnp.sqrt(hat_two) + adam_eps) + weight_decay * old_master
    )
    return (
        new_master[None],
        new_one.astype(jnp.bfloat16)[None],
        new_two.astype(jnp.bfloat16)[None],
    )


def solution(mesh):
    in_specs = (
        P("section", None, "dp", None),
        P(None, "dp", None),
        P("section", "dp", None),
        P("section", None, "dp"),
        P("dp", None),
        P(),
        P("section", "dp"),
        P(),
        P("section", "dp", None),
        P("section", "dp", None),
        P("section", "dp", None),
    )
    out_specs = (P("section", "dp", None), P("section", "dp", None), P("section", "dp", None))
    return jax.shard_map(shards, mesh=mesh, in_specs=in_specs, out_specs=out_specs, check_vma=False)
```

profile of v0, /device:TPU:0, one launch (start us, length us, event | category | flops | bytes accessed | tf_op | source)
XLA Modules:
  0.0 862.1 jit_solution(17811035409244809523)
XLA Ops:
  14.2 3.4 broadcast_select_fusion
  17.6 44.3 %all-gather.3.cloned.1.call-done = bf16[1,512,8192]{2,1,0:T(8,128)(2,1)} async-done(((bf16[1,512,1024]{2,1,0:T(8,128)(2,1)}), bf16[1,512,8192]{2,1,0:T(8,128)(2,1)}) %all-gather.3.cloned.1.call-update) | async-done | bytes 8388624 | tf_op jit(solution)/shard_map/all_gather | solution.py:41
  61.9 51.6 %all-gather.5.cloned.1.call-done = bf16[1,8192,512]{2,1,0:T(8,128)(2,1)} async-done(((bf16[1,1024,512]{2,1,0:T(8,128)(2,1)}), bf16[1,8192,512]{2,1,0:T(8,128)(2,1)}) %all-gather.5.cloned.1.call-update) | async-done | bytes 8388624 | tf_op jit(solution)/shard_map/all_gather | solution.py:40
  115.2 510.9 %while.19 = (s32[]{:T(128)}, bf16[48,8192]{1,0:T(8,128)(2,1)S(1)}, bf16[3,48,8192]{2,1,0:T(8,128)(2,1)}, bf16[3,48,512]{2,1,0:T(8,128)(2,1)S(1)}, pred[]{:T(512)...) while((s32[]{:T(128)}, bf16[48,8192]{1,0:T(8,128)(2,1)S(1)}, ...), condition=%wide.region_1.2_spmd, body=%wide.region_0.1_spmd.sunk | while | flops 807321600 | bytes 61637388 | solution.py:84
  118.9 6.2 bitcast_dynamic-update-slice_fusion.6
  125.0 2.6 fusion.34
  128.9 20.3 %collective-permute-done = bf16[48,8192]{1,0:T(8,128)(2,1)S(1)} collective-permute-done((bf16[48,8192]{1,0:T(8,128)(2,1)S(1)}, bf16[48,8192]{1,0:T(8,128)(2,1)S(1)}, u32[]{:S(2)}, u32[]{:S(2)}) %collective-permute-start) | collective-permute-done | bytes 786464 | tf_op jit(solution)/shard_map/while/body/eval_jaxpr/ppermute | solution.py:19
  152.8 6.2 bitcast_dynamic-update-slice_fusion.6
  159.0 2.6 fusion.34
  162.9 19.5 %collective-permute-done = bf16[48,8192]{1,0:T(8,128)(2,1)S(1)} collective-permute-done((bf16[48,8192]{1,0:T(8,128)(2,1)S(1)}, bf16[48,8192]{1,0:T(8,128)(2,1)S(1)}, u32[]{:S(2)}, u32[]{:S(2)}) %collective-permute-start) | collective-permute-done | bytes 786464 | tf_op jit(solution)/shard_map/while/body/eval_jaxpr/ppermute | solution.py:19
  185.9 6.2 bitcast_dynamic-update-slice_fusion.6
  192.1 2.6 fusion.34
  196.0 18.6 %collective-permute-done = bf16[48,8192]{1,0:T(8,128)(2,1)S(1)} collective-permute-done((bf16[48,8192]{1,0:T(8,128)(2,1)S(1)}, bf16[48,8192]{1,0:T(8,128)(2,1)S(1)}, u32[]{:S(2)}, u32[]{:S(2)}) %collective-permute-start) | collective-permute-done | bytes 786464 | tf_op jit(solution)/shard_map/while/body/eval_jaxpr/ppermute | solution.py:19
  218.2 6.2 bitcast_dynamic-update-slice_fusion.6
  224.3 2.6 fusion.34
  228.2 19.7 %collective-permute-done = bf16[48,8192]{1,0:T(8,128)(2,1)S(1)} collective-permute-done((bf16[48,8192]{1,0:T(8,128)(2,1)S(1)}, bf16[48,8192]{1,0:T(8,128)(2,1)S(1)}, u32[]{:S(2)}, u32[]{:S(2)}) %collective-permute-start) | collective-permute-done | bytes 786464 | tf_op jit(solution)/shard_map/while/body/eval_jaxpr/ppermute | solution.py:19
  251.5 6.2 bitcast_dynamic-update-slice_fusion.6
  261.6 18.8 %collective-permute-done = bf16[48,8192]{1,0:T(8,128)(2,1)S(1)} collective-permute-done((bf16[48,8192]{1,0:T(8,128)(2,1)S(1)}, bf16[48,8192]{1,0:T(8,128)(2,1)S(1)}, u32[]{:S(2)}, u32[]{:S(2)}) %collective-permute-start) | collective-permute-done | bytes 786464 | tf_op jit(solution)/shard_map/while/body/eval_jaxpr/ppermute | solution.py:19
  283.9 6.2 bitcast_dynamic-update-slice_fusion.6
  294.0 17.9 %collective-permute-done = bf16[48,8192]{1,0:T(8,128)(2,1)S(1)} collective-permute-done((bf16[48,8192]{1,0:T(8,128)(2,1)S(1)}, bf16[48,8192]{1,0:T(8,128)(2,1)S(1)}, u32[]{:S(2)}, u32[]{:S(2)}) %collective-permute-start) | collective-permute-done | bytes 786464 | tf_op jit(solution)/shard_map/while/body/eval_jaxpr/ppermute | solution.py:19
  315.5 6.2 bitcast_dynamic-update-slice_fusion.6
  325.6 17.0 %collective-permute-done = bf16[48,8192]{1,0:T(8,128)(2,1)S(1)} collective-permute-done((bf16[48,8192]{1,0:T(8,128)(2,1)S(1)}, bf16[48,8192]{1,0:T(8,128)(2,1)S(1)}, u32[]{:S(2)}, u32[]{:S(2)}) %collective-permute-start) | collective-permute-done | bytes 786464 | tf_op jit(solution)/shard_map/while/body/eval_jaxpr/ppermute | solution.py:19
  346.1 6.2 bitcast_dynamic-update-slice_fusion.6
  356.2 16.0 %collective-permute-done = bf16[48,8192]{1,0:T(8,128)(2,1)S(1)} collective-permute-done((bf16[48,8192]{1,0:T(8,128)(2,1)S(1)}, bf16[48,8192]{1,0:T(8,128)(2,1)S(1)}, u32[]{:S(2)}, u32[]{:S(2)}) %collective-permute-start) | collective-permute-done | bytes 786464 | tf_op jit(solution)/shard_map/while/body/eval_jaxpr/ppermute | solution.py:19
  375.8 6.2 bitcast_dynamic-update-slice_fusion.6
  382.0 2.6 fusion.34
  385.9 15.2 %collective-permute-done = bf16[48,8192]{1,0:T(8,128)(2,1)S(1)} collective-permute-done((bf16[48,8192]{1,0:T(8,128)(2,1)S(1)}, bf16[48,8192]{1,0:T(8,128)(2,1)S(1)}, u32[]{:S(2)}, u32[]{:S(2)}) %collective-permute-start) | collective-permute-done | bytes 786464 | tf_op jit(solution)/shard_map/while/body/eval_jaxpr/ppermute | solution.py:19
  404.7 6.2 bitcast_dynamic-update-slice_fusion.6
  410.8 2.6 fusion.34
  414.7 14.2 %collective-permute-done = bf16[48,8192]{1,0:T(8,128)(2,1)S(1)} collective-permute-done((bf16[48,8192]{1,0:T(8,128)(2,1)S(1)}, bf16[48,8192]{1,0:T(8,128)(2,1)S(1)}, u32[]{:S(2)}, u32[]{:S(2)}) %collective-permute-start) | collective-permute-done | bytes 786464 | tf_op jit(solution)/shard_map/while/body/eval_jaxpr/ppermute | solution.py:19
  432.5 6.2 bitcast_dynamic-update-slice_fusion.6
  442.6 13.8 %collective-permute-done = bf16[48,8192]{1,0:T(8,128)(2,1)S(1)} collective-permute-done((bf16[48,8192]{1,0:T(8,128)(2,1)S(1)}, bf16[48,8192]{1,0:T(8,128)(2,1)S(1)}, u32[]{:S(2)}, u32[]{:S(2)}) %collective-permute-start) | collective-permute-done | bytes 786464 | tf_op jit(solution)/shard_map/while/body/eval_jaxpr/ppermute | solution.py:19
  460.0 6.2 bitcast_dynamic-update-slice_fusion.6
  466.2 2.6 fusion.34
  470.1 14.3 %collective-permute-done = bf16[48,8192]{1,0:T(8,128)(2,1)S(1)} collective-permute-done((bf16[48,8192]{1,0:T(8,128)(2,1)S(1)}, bf16[48,8192]{1,0:T(8,128)(2,1)S(1)}, u32[]{:S(2)}, u32[]{:S(2)}) %collective-permute-start) | collective-permute-done | bytes 786464 | tf_op jit(solution)/shard_map/while/body/eval_jaxpr/ppermute | solution.py:19
  488.0 6.2 bitcast_dynamic-update-slice_fusion.6
  494.2 2.6 fusion.34
  498.1 14.7 %collective-permute-done = bf16[48,8192]{1,0:T(8,128)(2,1)S(1)} collective-permute-done((bf16[48,8192]{1,0:T(8,128)(2,1)S(1)}, bf16[48,8192]{1,0:T(8,128)(2,1)S(1)}, u32[]{:S(2)}, u32[]{:S(2)}) %collective-permute-start) | collective-permute-done | bytes 786464 | tf_op jit(solution)/shard_map/while/body/eval_jaxpr/ppermute | solution.py:19
  516.4 6.2 bitcast_dynamic-update-slice_fusion.6
  522.5 2.6 fusion.34
  526.4 14.7 %collective-permute-done = bf16[48,8192]{1,0:T(8,128)(2,1)S(1)} collective-permute-done((bf16[48,8192]{1,0:T(8,128)(2,1)S(1)}, bf16[48,8192]{1,0:T(8,128)(2,1)S(1)}, u32[]{:S(2)}, u32[]{:S(2)}) %collective-permute-start) | collective-permute-done | bytes 786464 | tf_op jit(solution)/shard_map/while/body/eval_jaxpr/ppermute | solution.py:19
  544.7 6.2 bitcast_dynamic-update-slice_fusion.6
  550.9 2.6 fusion.34
  554.8 14.7 %collective-permute-done = bf16[48,8192]{1,0:T(8,128)(2,1)S(1)} collective-permute-done((bf16[48,8192]{1,0:T(8,128)(2,1)S(1)}, bf16[48,8192]{1,0:T(8,128)(2,1)S(1)}, u32[]{:S(2)}, u32[]{:S(2)}) %collective-permute-start) | collective-permute-done | bytes 786464 | tf_op jit(solution)/shard_map/while/body/eval_jaxpr/ppermute | solution.py:19
  573.0 6.2 bitcast_dynamic-update-slice_fusion.6
  579.2 2.6 fusion.34
  583.1 14.7 %collective-permute-done = bf16[48,8192]{1,0:T(8,128)(2,1)S(1)} collective-permute-done((bf16[48,8192]{1,0:T(8,128)(2,1)S(1)}, bf16[48,8192]{1,0:T(8,128)(2,1)S(1)}, u32[]{:S(2)}, u32[]{:S(2)}) %collective-permute-start) | collective-permute-done | bytes 786464 | tf_op jit(solution)/shard_map/while/body/eval_jaxpr/ppermute | solution.py:19
  601.4 6.2 bitcast_dynamic-update-slice_fusion.6
  607.6 2.6 fusion.34
  611.5 14.7 %collective-permute-done = bf16[48,8192]{1,0:T(8,128)(2,1)S(1)} collective-permute-done((bf16[48,8192]{1,0:T(8,128)(2,1)S(1)}, bf16[48,8192]{1,0:T(8,128)(2,1)S(1)}, u32[]{:S(2)}, u32[]{:S(2)}) %collective-permute-start) | collective-permute-done | bytes 786464 | tf_op jit(solution)/shard_map/while/body/eval_jaxpr/ppermute | solution.py:19
  629.7 6.4 fusion.10
  636.1 8.2 convolution_bitcast_fusion
  648.4 15.3 %fusion.1 = bf16[8192,1024]{0,1:T(8,128)(2,1)} fusion(f32[8192,512]{0,1:T(8,128)S(1)} %fusion.15, f32[8192,512]{0,1:T(8,128)} %convolution_bitcast_fusion, f32[]{:T(128)S(6)} %convert_element_type.57), kind=kLoop, calls=%fused_computation.12 | loop fusion | flops 25165824 | bytes 50331652 | tf_op jit(solution)/shard_map/convert_element_type | solution.py:96
  663.7 13.1 %psum.14 = f32[]{:T(128)} all-reduce(f32[]{:T(128)S(6)} %convert_element_type.57), channel_id=1, replica_groups=mesh['section'=16,'dp'=8] {'dp'}, use_global_device_ids=true, to_apply=%region_3.4 | all-reduce | flops 1 | bytes 8 | tf_op jit(solution)/shard_map/psum | solution.py:101
  677.4 5.4 copy.14
  682.9 2.9 copy.15
  685.7 4.0 copy.16
  690.4 73.1 %reduce-scatter.2.cloned.1.call-done = bf16[1024,1024]{0,1:T(8,128)(2,1)} async-done(((bf16[8192,1024]{0,1:T(8,128)(2,1)}), bf16[1024,1024]{0,1:T(8,128)(2,1)}) %reduce-scatter.2.cloned.1.call-update) | async-done | bytes 2097168 | tf_op jit(solution)/shard_map/reduce_scatter | solution.py:95
  763.5 3.3 multiply_reduce_fusion
  766.8 65.0 %psum.15 = f32[]{:T(128)} all-reduce(f32[]{:T(128)} %multiply_reduce_fusion), channel_id=1, replica_groups=mesh['section'=16,'dp'=8] {'section','dp'}, use_global_device_ids=true, to_apply=%region_5.6 | all-reduce | flops 1 | bytes 8 | tf_op jit(solution)/shard_map/psum | solution.py:103
  832.6 9.6 %convert_bitcast_fusion = (bf16[1,1024,1024]{1,2,0:T(8,128)(2,1)}, f32[1,1024,1024]{1,2,0:T(8,128)}, bf16[1,1024,1024]{1,2,0:T(8,128)(2,1)}) fusion(bf16[1,1024,1024]{1,2,0:T(8,128)(2,1)} %copy.16, f32[]{:T(128)S(6)} %min.17, f32[]{:T(128)S(6)} %max.17, bf16[1024,1024]{0,1:T(8,128)(2,1)} %reduce-scatter.2.cloned.1.call-done, ...), kind=kLoop, calls=%fused_computation.27 | loop fusion | flops 23068672 | bytes 18874376 | tf_op jit(solution)/shard_map/broadcast_in_dim | solution.py:119
  842.2 5.3 copy.17
  847.5 4.1 copy.18
  851.6 3.9 copy.19
  (141 shorter events, 110.5 us)
Async XLA Ops:
  7.2 4.8 copy-start
  7.2 7.0 copy-start.5
  7.2 54.7 %all-gather.3.cloned.1.call-start = ((), (), s32[]{:S(2)}) async-start(), calls=%async_computation.1 | async-start | bytes 9437184 | tf_op jit(solution)/shard_map/all_gather | solution.py:41
  7.9 105.6 %all-gather.5.cloned.1.call-start = ((), (), s32[]{:S(2)}) async-start(), calls=%async_computation.2 | async-start | bytes 9437184 | tf_op jit(solution)/shard_map/all_gather | solution.py:40
  8.7 754.8 %reduce-scatter.2.cloned.1.call-start = ((), (), s32[]{:S(2)}) async-start(), calls=%async_computation.3 | async-start | bytes 18874368 | tf_op jit(solution)/shard_map/reduce_scatter | solution.py:95
  118.9 6.2 copy-start.2
  127.6 21.6 %collective-permute-start = (bf16[48,8192]{1,0:T(8,128)(2,1)S(1)}, bf16[48,8192]{1,0:T(8,128)(2,1)S(1)}, u32[]{:S(2)}, u32[]{:S(2)}) collective-permute-start(bf16[48,8192]{1,0:T(8,128)(2,1)S(1)} %fusion.34), channel_id=1, source_target_pairs={{8,0},{16,8},{24,16},{32,24},{40,32},{48,40},{56,48},{64,56},{72,6... | collective-permute-start | bytes 2359304 | tf_op jit(solution)/shard_map/while/body/eval_jaxpr/ppermute | solution.py:19
  152.8 6.2 copy-start.2
  161.6 20.8 %collective-permute-start = (bf16[48,8192]{1,0:T(8,128)(2,1)S(1)}, bf16[48,8192]{1,0:T(8,128)(2,1)S(1)}, u32[]{:S(2)}, u32[]{:S(2)}) collective-permute-start(bf16[48,8192]{1,0:T(8,128)(2,1)S(1)} %fusion.34), channel_id=1, source_target_pairs={{8,0},{16,8},{24,16},{32,24},{40,32},{48,40},{56,48},{64,56},{72,6... | collective-permute-start | bytes 2359304 | tf_op jit(solution)/shard_map/while/body/eval_jaxpr/ppermute | solution.py:19
  185.9 6.2 copy-start.2
  194.7 19.9 %collective-permute-start = (bf16[48,8192]{1,0:T(8,128)(2,1)S(1)}, bf16[48,8192]{1,0:T(8,128)(2,1)S(1)}, u32[]{:S(2)}, u32[]{:S(2)}) collective-permute-start(bf16[48,8192]{1,0:T(8,128)(2,1)S(1)} %fusion.34), channel_id=1, source_target_pairs={{8,0},{16,8},{24,16},{32,24},{40,32},{48,40},{56,48},{64,56},{72,6... | collective-permute-start | bytes 2359304 | tf_op jit(solution)/shard_map/while/body/eval_jaxpr/ppermute | solution.py:19
  218.2 6.2 copy-start.2
  226.9 21.0 %collective-permute-start = (bf16[48,8192]{1,0:T(8,128)(2,1)S(1)}, bf16[48,8192]{1,0:T(8,128)(2,1)S(1)}, u32[]{:S(2)}, u32[]{:S(2)}) collective-permute-start(bf16[48,8192]{1,0:T(8,128)(2,1)S(1)} %fusion.34), channel_id=1, source_target_pairs={{8,0},{16,8},{24,16},{32,24},{40,32},{48,40},{56,48},{64,56},{72,6... | collective-permute-start | bytes 2359304 | tf_op jit(solution)/shard_map/while/body/eval_jaxpr/ppermute | solution.py:19
  251.5 6.2 copy-start.2
  260.3 20.1 %collective-permute-start = (bf16[48,8192]{1,0:T(8,128)(2,1)S(1)}, bf16[48,8192]{1,0:T(8,128)(2,1)S(1)}, u32[]{:S(2)}, u32[]{:S(2)}) collective-permute-start(bf16[48,8192]{1,0:T(8,128)(2,1)S(1)} %fusion.34), channel_id=1, source_target_pairs={{8,0},{16,8},{24,16},{32,24},{40,32},{48,40},{56,48},{64,56},{72,6... | collective-permute-start | bytes 2359304 | tf_op jit(solution)/shard_map/while/body/eval_jaxpr/ppermute | solution.py:19
  283.9 6.2 copy-start.2
  292.7 19.2 %collective-permute-start = (bf16[48,8192]{1,0:T(8,128)(2,1)S(1)}, bf16[48,8192]{1,0:T(8,128)(2,1)S(1)}, u32[]{:S(2)}, u32[]{:S(2)}) collective-permute-start(bf16[48,8192]{1,0:T(8,128)(2,1)S(1)} %fusion.34), channel_id=1, source_target_pairs={{8,0},{16,8},{24,16},{32,24},{40,32},{48,40},{56,48},{64,56},{72,6... | collective-permute-start | bytes 2359304 | tf_op jit(solution)/shard_map/while/body/eval_jaxpr/ppermute | solution.py:19
  315.5 6.2 copy-start.2
  324.3 18.3 %collective-permute-start = (bf16[48,8192]{1,0:T(8,128)(2,1)S(1)}, bf16[48,8192]{1,0:T(8,128)(2,1)S(1)}, u32[]{:S(2)}, u32[]{:S(2)}) collective-permute-start(bf16[48,8192]{1,0:T(8,128)(2,1)S(1)} %fusion.34), channel_id=1, source_target_pairs={{8,0},{16,8},{24,16},{32,24},{40,32},{48,40},{56,48},{64,56},{72,6... | collective-permute-start | bytes 2359304 | tf_op jit(solution)/shard_map/while/body/eval_jaxpr/ppermute | solution.py:19
  346.1 6.2 copy-start.2
  354.9 17.3 %collective-permute-start = (bf16[48,8192]{1,0:T(8,128)(2,1)S(1)}, bf16[48,8192]{1,0:T(8,128)(2,1)S(1)}, u32[]{:S(2)}, u32[]{:S(2)}) collective-permute-start(bf16[48,8192]{1,0:T(8,128)(2,1)S(1)} %fusion.34), channel_id=1, source_target_pairs={{8,0},{16,8},{24,16},{32,24},{40,32},{48,40},{56,48},{64,56},{72,6... | collective-permute-start | bytes 2359304 | tf_op jit(solution)/shard_map/while/body/eval_jaxpr/ppermute | solution.py:19
  375.8 6.2 copy-start.2
  384.6 16.5 %collective-permute-start = (bf16[48,8192]{1,0:T(8,128)(2,1)S(1)}, bf16[48,8192]{1,0:T(8,128)(2,1)S(1)}, u32[]{:S(2)}, u32[]{:S(2)}) collective-permute-start(bf16[48,8192]{1,0:T(8,128)(2,1)S(1)} %fusion.34), channel_id=1, source_target_pairs={{8,0},{16,8},{24,16},{32,24},{40,32},{48,40},{56,48},{64,56},{72,6... | collective-permute-start | bytes 2359304 | tf_op jit(solution)/shard_map/while/body/eval_jaxpr/ppermute | solution.py:19
  404.6 6.2 copy-start.2
  413.4 15.5 %collective-permute-start = (bf16[48,8192]{1,0:T(8,128)(2,1)S(1)}, bf16[48,8192]{1,0:T(8,128)(2,1)S(1)}, u32[]{:S(2)}, u32[]{:S(2)}) collective-permute-start(bf16[48,8192]{1,0:T(8,128)(2,1)S(1)} %fusion.34), channel_id=1, source_target_pairs={{8,0},{16,8},{24,16},{32,24},{40,32},{48,40},{56,48},{64,56},{72,6... | collective-permute-start | bytes 2359304 | tf_op jit(solution)/shard_map/while/body/eval_jaxpr/ppermute | solution.py:19
  432.5 6.2 copy-start.2
  441.3 15.1 %collective-permute-start = (bf16[48,8192]{1,0:T(8,128)(2,1)S(1)}, bf16[48,8192]{1,0:T(8,128)(2,1)S(1)}, u32[]{:S(2)}, u32[]{:S(2)}) collective-permute-start(bf16[48,8192]{1,0:T(8,128)(2,1)S(1)} %fusion.34), channel_id=1, source_target_pairs={{8,0},{16,8},{24,16},{32,24},{40,32},{48,40},{56,48},{64,56},{72,6... | collective-permute-start | bytes 2359304 | tf_op jit(solution)/shard_map/while/body/eval_jaxpr/ppermute | solution.py:19
  460.0 6.2 copy-start.2
  468.8 15.6 %collective-permute-start = (bf16[48,8192]{1,0:T(8,128)(2,1)S(1)}, bf16[48,8192]{1,0:T(8,128)(2,1)S(1)}, u32[]{:S(2)}, u32[]{:S(2)}) collective-permute-start(bf16[48,8192]{1,0:T(8,128)(2,1)S(1)} %fusion.34), channel_id=1, source_target_pairs={{8,0},{16,8},{24,16},{32,24},{40,32},{48,40},{56,48},{64,56},{72,6... | collective-permute-start | bytes 2359304 | tf_op jit(solution)/shard_map/while/body/eval_jaxpr/ppermute | solution.py:19
  488.0 6.2 copy-start.2
  496.8 16.0 %collective-permute-start = (bf16[48,8192]{1,0:T(8,128)(2,1)S(1)}, bf16[48,8192]{1,0:T(8,128)(2,1)S(1)}, u32[]{:S(2)}, u32[]{:S(2)}) collective-permute-start(bf16[48,8192]{1,0:T(8,128)(2,1)S(1)} %fusion.34), channel_id=1, source_target_pairs={{8,0},{16,8},{24,16},{32,24},{40,32},{48,40},{56,48},{64,56},{72,6... | collective-permute-start | bytes 2359304 | tf_op jit(solution)/shard_map/while/body/eval_jaxpr/ppermute | solution.py:19
  516.4 6.2 copy-start.2
  525.1 16.0 %collective-permute-start = (bf16[48,8192]{1,0:T(8,128)(2,1)S(1)}, bf16[48,8192]{1,0:T(8,128)(2,1)S(1)}, u32[]{:S(2)}, u32[]{:S(2)}) collective-permute-start(bf16[48,8192]{1,0:T(8,128)(2,1)S(1)} %fusion.34), channel_id=1, source_target_pairs={{8,0},{16,8},{24,16},{32,24},{40,32},{48,40},{56,48},{64,56},{72,6... | collective-permute-start | bytes 2359304 | tf_op jit(solution)/shard_map/while/body/eval_jaxpr/ppermute | solution.py:19
  544.7 6.2 copy-start.2
  553.5 16.0 %collective-permute-start = (bf16[48,8192]{1,0:T(8,128)(2,1)S(1)}, bf16[48,8192]{1,0:T(8,128)(2,1)S(1)}, u32[]{:S(2)}, u32[]{:S(2)}) collective-permute-start(bf16[48,8192]{1,0:T(8,128)(2,1)S(1)} %fusion.34), channel_id=1, source_target_pairs={{8,0},{16,8},{24,16},{32,24},{40,32},{48,40},{56,48},{64,56},{72,6... | collective-permute-start | bytes 2359304 | tf_op jit(solution)/shard_map/while/body/eval_jaxpr/ppermute | solution.py:19
  573.0 6.2 copy-start.2
  581.8 16.0 %collective-permute-start = (bf16[48,8192]{1,0:T(8,128)(2,1)S(1)}, bf16[48,8192]{1,0:T(8,128)(2,1)S(1)}, u32[]{:S(2)}, u32[]{:S(2)}) collective-permute-start(bf16[48,8192]{1,0:T(8,128)(2,1)S(1)} %fusion.34), channel_id=1, source_target_pairs={{8,0},{16,8},{24,16},{32,24},{40,32},{48,40},{56,48},{64,56},{72,6... | collective-permute-start | bytes 2359304 | tf_op jit(solution)/shard_map/while/body/eval_jaxpr/ppermute | solution.py:19
  601.4 6.2 copy-start.2
  610.2 16.0 %collective-permute-start = (bf16[48,8192]{1,0:T(8,128)(2,1)S(1)}, bf16[48,8192]{1,0:T(8,128)(2,1)S(1)}, u32[]{:S(2)}, u32[]{:S(2)}) collective-permute-start(bf16[48,8192]{1,0:T(8,128)(2,1)S(1)} %fusion.34), channel_id=1, source_target_pairs={{8,0},{16,8},{24,16},{32,24},{40,32},{48,40},{56,48},{64,56},{72,6... | collective-permute-start | bytes 2359304 | tf_op jit(solution)/shard_map/while/body/eval_jaxpr/ppermute | solution.py:19
  629.6 6.4 copy-start.4
  629.6 14.6 %slice-start = ((s8[8388608]{0:T(1024)(128)(4,1)}), s8[4194304]{0:T(1024)(128)(4,1)S(1)}, s32[]{:S(2)}) async-start(s8[8388608]{0:T(1024)(128)(4,1)} %bitcast.110), calls=%async_computation.4 | async-start | bytes 8388608
  636.1 8.2 slice-start.1
  644.3 1.7 copy-start.3
  847.5 8.0 copy-start.1
Sparse Core Ops, SparseCore 0:
  9.7 52.1 all-gather.2
  63.6 49.8 all-gather.4
  663.8 99.6 reduce-scatter.1
where the time goes:
time: 866 us; the launch traced here: 862 us
  waiting for transfers between devices  449 us (52%)
  matrix products  167 us (19%)
  blocking collectives  78.1 us (9%)
  other arithmetic  74.8 us (9%)
  local copies, waits for them, and re-layouts  52.7 us (6%)
  starting transfers between devices  22.1 us (3%)
  between operations  17.2 us (2%)
    ppermute x17, waiting for transfers between devices, shifted(): lax.ppermute(value, axis, [(source, source + steps) for source in range(l...  279 us
    dot_general x35, matrix products, contract_rows(): lax.dot_general(left, right, (((1,), (1,)), ((), ())), preferred_element_...  155 us
    reduce_scatter x1, waiting for transfers between devices, shards(): lax.psum_scatter((keep * jnp.concatenate([value_part, output_part], axis=...  73.1 us
    psum x1, blocking collectives, shards(): total_square = lax.psum(jnp.sum(grad_share * grad_share), ('section', 'dp'))  65 us
    all_gather x1, waiting for transfers between devices, shards(): lax.all_gather(w_value, 'dp', axis=1, tiled=True)  51.6 us
    all_gather x1, waiting for transfers between devices, shards(): lax.all_gather(w_output, 'dp', axis=2, tiled=True)  44.3 us
    dynamic_update_slice x18, other arithmetic, backward_step(): lax.dynamic_update_index_in_dim(kept_grad, jnp.where(usable, gradient, pr...  42.5 us
    unnamed x20, local copies, waits for them, and re-layouts  26 us
  transfers between devices with their start and end apart: 20, of which 20 were waited for; matrix products, arithmetic and copies ran while one was open for 2% of the time, Pallas kernels for 0%

commit v1 on v0

v1 whole, which is shorter than its diff:
```python
import math

import jax
import jax.numpy as jnp
from jax import lax
from jax.sharding import Mesh
from jax.sharding import PartitionSpec as P

beta_one = 0.9
beta_two = 0.95
adam_eps = 1e-08
learn_rate = 0.01
weight_decay = 0.1
step_count = 100

SECTION = ("z", "y")
DP = ("x", "core")
PLANE = ("y", "core")


def dot(left, right, dims):
    return lax.dot_general(left, right, (dims, ((), ())), preferred_element_type=jnp.float32)


def swap(value, axis, mask):
    return lax.ppermute(value, axis, [(i, i ^ mask) for i in range(lax.axis_size(axis))])


def sum_over_x(part):
    part = part.astype(jnp.bfloat16)
    rows = part.shape[0] // 2
    halves = (part[:rows], part[rows:])
    masks = ((1, 3), (3, 1))
    for turn in range(2):
        got = [swap(half, "x", masks[i][turn]) for i, half in enumerate(halves)]
        halves = [
            (half.astype(jnp.float32) + other.astype(jnp.float32)).astype(jnp.bfloat16)
            for half, other in zip(halves, got)
        ]
    return jnp.concatenate(halves, axis=0)


def sum_over_all(value):
    for axis, masks in (("core", (1,)), ("x", (1, 3)), ("y", (1, 3)), ("z", (1, 3))):
        for mask in masks:
            value = value + swap(value, axis, mask)
    return value


def shards(
    acts, out_grad, w_value, w_output, order, alive, flags, clip_rms, master, moment_one, moment_two
):
    z, y, x, core = (lax.axis_index(axis) for axis in ("z", "y", "x", "core"))
    planes, columns, across = (lax.axis_size(axis) for axis in ("z", "y", "x"))
    replicas = across * lax.axis_size("core")
    own_value, own_output = w_value[0], w_output[0]
    share, head_size = own_value.shape
    micro, tok_rows, width = out_grad.shape
    rows = micro * tok_rows
    chip_width = 2 * share

    output_weight = lax.all_gather(own_output, PLANE, axis=0)
    value_weight = lax.all_gather(own_value, PLANE, axis=0)
    flag_row = lax.all_gather(flags[0, 0], DP)

    top = out_grad.reshape(rows, width)
    own_slice = lax.dynamic_slice(top, (0, x * chip_width), (rows, chip_width))
    gradient = jnp.where(jnp.logical_and(z == planes - 1, x == y), own_slice, jnp.zeros_like(own_slice))
    for turn in range(1, across):
        other = lax.rem(x + turn, across)
        piece = lax.dynamic_slice(top, (0, other * chip_width), (rows, chip_width))
        base = (planes - 1) * columns * across
        pairs = [
            (base + i * across + i, base + i * across + (i + turn) % across) for i in range(columns)
        ]
        gradient = gradient + lax.ppermute(piece, ("z", "y", "x"), pairs)

    keep = alive * (1 - flag_row)
    replica = lax.axis_index(DP)
    own_keep = (alive[replica] * (1 - flags[0, 0])).astype(jnp.bfloat16)
    picked = jnp.take(acts[0], order[0], axis=0).reshape(rows, width) * own_keep
    picked = lax.all_to_all(picked, DP, split_axis=1, concat_axis=0, tiled=True)
    hidden_part = dot(picked, own_value, ((1,), (0,))).astype(jnp.bfloat16)
    hidden_part = lax.all_to_all(
        hidden_part.reshape(replicas, rows, head_size), DP, split_axis=0, concat_axis=0, tiled=True
    )
    hidden = jnp.sum(hidden_part.astype(jnp.float32), axis=0).astype(jnp.bfloat16)
    hidden = lax.all_gather(hidden, DP, axis=0, tiled=True)

    kept_gradient = jnp.zeros((rows, chip_width), jnp.bfloat16)
    kept_back = [jnp.zeros((rows, head_size), jnp.bfloat16) for _ in range(columns)]
    for turn in range(planes):
        kept_gradient = kept_gradient + gradient
        for at in reversed(range(columns)):
            part = dot(gradient[:, :share], output_weight[2 * at], ((1,), (1,))) + dot(
                gradient[:, share:], output_weight[2 * at + 1], ((1,), (1,))
            )
            back = sum_over_x(part)
            kept_back[at] = kept_back[at] + back
            if turn < planes - 1 or at > 0:
                weight = value_weight[2 * at : 2 * at + 2].reshape(chip_width, head_size)
                gradient = (gradient.astype(jnp.float32) + dot(back, weight, ((1,), (1,)))).astype(
                    jnp.bfloat16
                )
        if turn < planes - 1:
            gradient = lax.ppermute(gradient, "z", [(i, i - 1) for i in range(1, planes)])

    gradients = [None] * columns
    gradient = kept_gradient
    for at in reversed(range(columns)):
        gradients[at] = gradient
        if at > 0:
            weight = value_weight[2 * at : 2 * at + 2].reshape(chip_width, head_size)
            gradient = (
                gradient.astype(jnp.float32) + dot(kept_back[at], weight, ((1,), (1,)))
            ).astype(jnp.bfloat16)
    sent = jnp.stack(
        [piece[:, half * share : (half + 1) * share] for piece in gradients for half in range(2)]
    )
    grad_rows = lax.all_to_all(sent, PLANE, split_axis=0, concat_axis=0, tiled=True)
    grad_rows = grad_rows.reshape(replicas * rows, share)
    backs = lax.all_to_all(jnp.stack(kept_back), "y", split_axis=0, concat_axis=0, tiled=True)
    others = swap(backs, "core", 1)
    back_rows = jnp.stack(
        [jnp.where(core == 0, backs, others), jnp.where(core == 0, others, backs)], axis=1
    ).reshape(replicas * rows, head_size)

    value_part = dot(picked, back_rows, ((0,), (0,)))
    output_part = dot(grad_rows, hidden, ((0,), (0,)))
    contributors = jnp.maximum(jnp.sum(keep).astype(jnp.float32), 1.0)
    grad_share = jnp.concatenate([value_part, output_part], axis=1) / contributors
    total_square = sum_over_all(jnp.full((8, 128), jnp.sum(grad_share * grad_share)))[0, 0]
    norm = jnp.sqrt(total_square)
    sections = planes * columns
    threshold = clip_rms[0] * math.sqrt(2 * width * head_size * sections)
    factor = jnp.minimum(1.0, threshold / (norm + 1e-06))
    scaled = factor * grad_share
    new_one = beta_one * moment_one[0].astype(jnp.float32) + (1.0 - beta_one) * scaled
    new_two = beta_two * moment_two[0].astype(jnp.float32) + (1.0 - beta_two) * scaled * scaled
    hat_one = new_one / (1.0 - beta_one**step_count)
    hat_two = new_two / (1.0 - beta_two**step_count)
    old_master = master[0]
    new_master = old_master - learn_rate * (
        hat_one / (jnp.sqrt(hat_two) + adam_eps) + weight_decay * old_master
    )
    return (
        new_master[None],
        new_one.astype(jnp.bfloat16)[None],
        new_two.astype(jnp.bfloat16)[None],
    )


def solution(mesh):
    physical = Mesh(mesh.devices.reshape(4, 4, 4, 2), ("z", "y", "x", "core"))
    in_specs = (
        P(SECTION, None, DP, None),
        P(None, DP, None),
        P(SECTION, DP, None),
        P(SECTION, None, DP),
        P(DP, None),
        P(),
        P(SECTION, DP),
        P(),
        P(SECTION, DP, None),
        P(SECTION, DP, None),
        P(SECTION, DP, None),
    )
    out_specs = (P(SECTION, DP, None), P(SECTION, DP, None), P(SECTION, DP, None))
    return jax.shard_map(
        shards, mesh=physical, in_specs=in_specs, out_specs=out_specs, check_vma=False
    )
```

time: 866 us -> 596 us (0.69)
  waiting for transfers between devices: 449 us -> 288 us
  starting transfers between devices: 22.1 us -> 121 us
  matrix products: 167 us -> 69.3 us
  blocking collectives: 78.1 us -> 8.12 us
  other arithmetic: 74.8 us -> 24.4 us
    ppermute x17 -> x78, waiting for transfers between devices: 279 us -> 178 us  [the longest x72 153 us: swap(): lax.ppermute(value, axis, [(i, i ^ mask) for i in range(lax.axis_size(axi...]
    dot_general x38 -> x53, matrix products: 167 us -> 69.3 us  [dot(): lax.dot_general(left, right, (dims, ((), ())), preferred_element_type=jnp...]
    ppermute x17 -> x78, starting transfers between devices: 22 us -> 104 us  [the longest x72 96.6 us: swap(): lax.ppermute(value, axis, [(i, i ^ mask) for i in range(lax.axis_size(axi...]
    psum x2 -> x0, blocking collectives: 78.1 us -> none  [the longest x1 65 us: shards(): total_square = lax.psum(jnp.sum(grad_share * grad_share), ('section', 'dp'))]
    reduce_scatter x1 -> x0, waiting for transfers between devices: 73.1 us -> none  [shards(): lax.psum_scatter((keep * jnp.concatenate([value_part, output_part], axis=...]
    dynamic_update_slice x18 -> x0, other arithmetic: 42.5 us -> none  [backward_step(): lax.dynamic_update_index_in_dim(kept_grad, jnp.where(usable, gradient, pr...]
    all_to_all x0 -> x4, waiting for transfers between devices: none -> 22.3 us  [the longest x1 15.3 us: shards(): lax.all_to_all(sent, PLANE, split_axis=0, concat_axis=0, tiled=True)]
    dynamic_slice x37 -> x2, local copies, waits for them, and re-layouts: 22.8 us -> 3.2 us  [the longest x1 2.61 us: shards(): piece = lax.dynamic_slice(top, (0, other * chip_width), (rows, chip_width))]
  transfers between devices with their start and end apart: 20 -> 85, of which waited for: 20 -> 73; matrix products, arithmetic and copies ran while one was open for 2% -> 14% of each run, Pallas kernels for 0% -> 0%
where the time goes in v1:
time: 596 us; the launch traced here: 586 us
  waiting for transfers between devices  288 us (48%)
  starting transfers between devices  121 us (20%)
  matrix products  69.3 us (12%)
  local copies, waits for them, and re-layouts  54.4 us (9%)
  other arithmetic  24.4 us (4%)
  between operations  21.1 us (4%)
  blocking collectives  8.12 us (1%)
    ppermute x72, waiting for transfers between devices, swap(): lax.ppermute(value, axis, [(i, i ^ mask) for i in range(lax.axis_size(axi...  153 us
    ppermute x72, starting transfers between devices, swap(): lax.ppermute(value, axis, [(i, i ^ mask) for i in range(lax.axis_size(axi...  96.6 us
    dot_general x53, matrix products, dot(): lax.dot_general(left, right, (dims, ((), ())), preferred_element_type=jnp...  69.3 us
    all_gather x1, waiting for transfers between devices, shards(): output_weight = lax.all_gather(own_output, PLANE, axis=0)  45.2 us
    all_gather x1, waiting for transfers between devices, shards(): value_weight = lax.all_gather(own_value, PLANE, axis=0)  40.9 us
    unnamed x163, local copies, waits for them, and re-layouts  39.5 us
    ppermute x3, waiting for transfers between devices, shards(): lax.ppermute(gradient, 'z', [(i, i - 1) for i in range(1, planes)])  25.3 us
    all_to_all x1, waiting for transfers between devices, shards(): lax.all_to_all(sent, PLANE, split_axis=0, concat_axis=0, tiled=True)  15.3 us
  transfers between devices with their start and end apart: 85, of which 73 were waited for; matrix products, arithmetic and copies ran while one was open for 14% of the time, Pallas kernels for 0%

profile of v1, /device:TPU:0, one launch (start us, length us, event | category | flops | bytes accessed | tf_op | source)
XLA Modules:
  0.0 586.0 jit_solution(15261721585324565758)
XLA Ops:
  9.5 2.6 constant_dynamic-slice_fusion.2
  17.6 45.2 %all-gather.5.cloned.1.call-done = bf16[8,512,1024]{2,1,0:T(8,128)(2,1)} async-done(((bf16[1,512,1024]{2,1,0:T(8,128)(2,1)}), bf16[8,512,1024]{2,1,0:T(8,128)(2,1)}) %all-gather.5.cloned.1.call-update) | async-done | bytes 8388624 | tf_op jit(solution)/shard_map/all_gather | solution.py:62
  70.8 2.6 collective-permute-done.5
  73.5 40.9 %all-gather.7.cloned.1.call-done = bf16[8,1024,512]{2,1,0:T(8,128)(2,1)} async-done(((bf16[1,1024,512]{2,1,0:T(8,128)(2,1)}), bf16[8,1024,512]{2,1,0:T(8,128)(2,1)}) %all-gather.7.cloned.1.call-update) | async-done | bytes 8388624 | tf_op jit(solution)/shard_map/all_gather | solution.py:63
  114.4 3.8 fusion.150
  118.2 2.8 collective-permute-start.4
  121.1 2.9 collective-permute-done.4
  128.8 2.5 collective-permute-start.9
  135.1 2.6 collective-permute-start.8
  145.5 2.5 collective-permute-start.13
  152.3 2.9 collective-permute-start.12
  160.0 2.9 collective-permute-start.17
  166.7 2.6 collective-permute-start.16
  174.4 10.5 %collective-permute-done.19 = bf16[144,2048]{1,0:T(8,128)(2,1)S(1)} collective-permute-done((bf16[144,2048]{1,0:T(8,128)(2,1)S(1)}, bf16[144,2048]{1,0:T(8,128)(2,1)S(1)}, u32[]{:S(2)}, u32[]{:S(2)}) %collective-permute-start.19) | collective-permute-done | bytes 589856 | tf_op jit(solution)/shard_map/ppermute | solution.py:106
  186.1 3.0 collective-permute-start.22
  193.2 2.8 collective-permute-start.21
  201.0 2.8 collective-permute-start.26
  207.5 2.6 collective-permute-start.25
  215.2 2.6 collective-permute-start.30
  229.9 2.6 collective-permute-start.34
  244.6 10.5 %collective-permute-done.36 = bf16[144,2048]{1,0:T(8,128)(2,1)S(1)} collective-permute-done((bf16[144,2048]{1,0:T(8,128)(2,1)S(1)}, bf16[144,2048]{1,0:T(8,128)(2,1)S(1)}, u32[]{:S(2)}, u32[]{:S(2)}) %collective-permute-start.36) | collective-permute-done | bytes 589856 | tf_op jit(solution)/shard_map/ppermute | solution.py:106
  256.3 2.6 collective-permute-start.39
  270.7 2.6 collective-permute-start.43
  277.7 2.6 collective-permute-start.42
  280.8 2.7 collective-permute-done.42
  283.6 2.6 add_convert_fusion.4
  291.1 2.6 collective-permute-start.47
  295.9 3.3 copy.47
  303.8 2.7 copy.39
  306.5 4.5 all-to-all-start
  311.0 3.1 collective-permute-start.46
  315.1 27.1 %collective-permute-done.46 = bf16[72,512]{1,0:T(8,128)(2,1)S(1)} collective-permute-done((bf16[72,512]{1,0:T(8,128)(2,1)S(1)}, bf16[72,512]{1,0:T(8,128)(2,1)S(1)}, u32[]{:S(2)}, u32[]{:S(2)}) %collective-permute-start.46) | collective-permute-done | bytes 73760 | tf_op jit(solution)/shard_map/ppermute | solution.py:26
  347.9 3.2 collective-permute-done.49
  353.9 3.2 collective-permute-done.52
  361.8 4.3 convolution_convert_fusion
  366.2 4.3 all-to-all-start.3
  370.5 4.3 collective-permute-done.53
  379.8 8.0 %collective-permute-done.54 = bf16[72,512]{1,0:T(8,128)(2,1)S(1)} collective-permute-done((bf16[72,512]{1,0:T(8,128)(2,1)S(1)}, bf16[72,512]{1,0:T(8,128)(2,1)S(1)}, u32[]{:S(2)}, u32[]{:S(2)}) %collective-permute-start.54) | collective-permute-done | bytes 73760 | tf_op jit(solution)/shard_map/ppermute | solution.py:26
  395.3 2.6 collective-permute-done.55
  398.0 2.4 add_convert_fusion.3
  406.4 3.1 collective-permute-done.58
  424.4 3.4 collective-permute-done.62
  431.6 2.4 collective-permute-done.65
  453.1 3.1 collective-permute-done.69
  458.8 3.5 all-to-all-start.1
  463.7 6.9 %all-to-all-done.1 = bf16[4,144,512]{2,1,0:T(8,128)(2,1)S(1)} async-done(((bf16[4,144,512]{2,1,0:T(8,128)(2,1)}), bf16[4,144,512]{2,1,0:T(8,128)(2,1)S(1)}, u32[]{:S(2)}, u32[]{:S(2)}) %all-to-all-start.1) | async-done | bytes 589856 | tf_op jit(solution)/shard_map/all_to_all | solution.py:122
  470.6 4.4 all-to-all-start.2
  476.7 8.1 %all-reduce = s32[8]{0:T(128)S(1)} all-reduce(s32[8]{0:T(128)S(1)} %bitcast_dynamic-update-slice_fusion), channel_id=2, replica_groups=mesh['z'=4,'y'=4,'x'=4,'core'=2] {'x','core'}, use_global_device_ids=true, to_apply=%add | all-reduce | flops 8 | bytes 64
  486.4 3.2 fusion.167
  489.7 15.3 %all-to-all-done.2 = bf16[8,144,1024]{2,1,0:T(8,128)(2,1)} async-done(((bf16[8,144,1024]{2,1,0:T(8,128)(2,1)}), bf16[8,144,1024]{2,1,0:T(8,128)(2,1)}, u32[]{:S(2)}, u32[]{:S(2)}) %all-to-all-start.2) | async-done | bytes 2359328 | tf_op jit(solution)/shard_map/all_to_all | solution.py:120
  505.0 3.5 fusion.168
  515.0 2.8 collective-permute-done.72
  519.9 3.4 collective-permute-done.73
  523.9 3.0 collective-permute-done.74
  528.1 3.7 collective-permute-done.75
  531.8 3.1 collective-permute-start.76
  536.5 3.6 collective-permute-start.77
  540.1 3.9 copy.41
  544.7 5.3 copy.43
  550.1 4.0 copy.38
  555.4 9.4 %fusion.14 = (bf16[1,1024,1024]{1,2,0:T(8,128)(2,1)}, f32[1,1024,1024]{1,2,0:T(8,128)}, bf16[1,1024,1024]{1,2,0:T(8,128)(2,1)}) fusion(bf16[1,1024,1024]{1,2,0:T(8,128)(2,1)} %copy.41, f32[]{:T(128)S(6)} %max.3, f32[1,1024,512]{1,2,0:T(8,128)} %bitcast.198, f32[1,1024,512]{1,2,0:T(8,128)S(1)} %bitcast.197, f32[]{:T(128)S(6)} %min.3, ...), kind=kLoop, calls=%fused_computation.30 | loop fusion | flops 23068672 | bytes 20971528 | tf_op jit(solution)/shard_map/convert_element_type | solution.py:149
  564.8 5.3 copy.44
  570.1 4.1 copy.45
  574.2 3.9 copy.46
  (425 shorter events, 209.4 us)
Async XLA Ops:
  8.0 54.8 %all-gather.5.cloned.1.call-start = ((), (), s32[]{:S(2)}) async-start(), calls=%async_computation.4 | async-start | bytes 9437184 | tf_op jit(solution)/shard_map/all_gather | solution.py:62
  8.7 105.7 %all-gather.7.cloned.1.call-start = ((), (), s32[]{:S(2)}) async-start(), calls=%async_computation.5 | async-start | bytes 9437184 | tf_op jit(solution)/shard_map/all_gather | solution.py:63
  66.3 4.5 collective-permute-start.3
  67.8 5.6 collective-permute-start.5
  73.4 47.6 %collective-permute-start.6 = (bf16[72,512]{1,0:T(8,128)(2,1)S(1)}, bf16[72,512]{1,0:T(8,128)(2,1)S(1)}, u32[]{:S(2)}, u32[]{:S(2)}) collective-permute-start(bf16[72,512]{1,0:T(8,128)(2,1)S(1)} %get-tuple-element.88), channel_id=1, source_target_pairs={{0,2},{2,0},{4,6},{6,4},{1,3},{3,1},{5,7},{7,5},{8,10},{10,8},{12,... | collective-permute-start | bytes 221192 | tf_op jit(solution)/shard_map/ppermute | solution.py:26
  118.2 5.7 collective-permute-start.4
  128.8 5.6 collective-permute-start.9
  135.1 5.6 collective-permute-start.8
  145.2 4.8 collective-permute-start.11
  145.5 5.8 collective-permute-start.13
  151.4 4.4 collective-permute-start.14
  152.3 5.6 collective-permute-start.12
  159.8 4.4 collective-permute-start.15
  160.0 5.6 collective-permute-start.17
  165.6 4.4 collective-permute-start.18
  166.7 5.6 collective-permute-start.16
  173.1 11.8 %collective-permute-start.19 = (bf16[144,2048]{1,0:T(8,128)(2,1)S(1)}, bf16[144,2048]{1,0:T(8,128)(2,1)S(1)}, u32[]{:S(2)}, u32[]{:S(2)}) collective-permute-start(bf16[144,2048]{1,0:T(8,128)(2,1)S(1)} %fusion.5), channel_id=1, source_target_pairs={{32,0},{64,32},{96,64},{33,1},{65,33},{97,65},{34,2},{66,34},{98,6... | collective-permute-start | bytes 1769480 | tf_op jit(solution)/shard_map/ppermute | solution.py:106
  185.9 4.4 collective-permute-start.20
  186.1 5.9 %collective-permute-start.22 = (bf16[72,512]{1,0:T(8,128)(2,1)S(1)}, bf16[72,512]{1,0:T(8,128)(2,1)S(1)}, u32[]{:S(2)}, u32[]{:S(2)}) collective-permute-start(bf16[72,512]{1,0:T(8,128)(2,1)S(1)} %get-tuple-element.74), channel_id=1, source_target_pairs={{0,6},{2,4},{4,2},{6,0},{1,7},{3,5},{5,3},{7,1},{8,14},{10,12},{12... | collective-permute-start | bytes 221192 | tf_op jit(solution)/shard_map/ppermute | solution.py:26
  192.1 4.9 collective-permute-start.23
  193.2 5.6 collective-permute-start.21
  200.7 4.4 collective-permute-start.24
  201.0 5.6 collective-permute-start.26
  206.6 4.4 collective-permute-start.27
  207.5 5.6 collective-permute-start.25
  215.0 5.2 collective-permute-start.28
  215.2 6.2 %collective-permute-start.30 = (bf16[72,512]{1,0:T(8,128)(2,1)S(1)}, bf16[72,512]{1,0:T(8,128)(2,1)S(1)}, u32[]{:S(2)}, u32[]{:S(2)}) collective-permute-start(bf16[72,512]{1,0:T(8,128)(2,1)S(1)} %get-tuple-element.66), channel_id=1, source_target_pairs={{0,6},{2,4},{4,2},{6,0},{1,7},{3,5},{5,3},{7,1},{8,14},{10,12},{12... | collective-permute-start | bytes 221192 | tf_op jit(solution)/shard_map/ppermute | solution.py:26
  222.2 5.6 collective-permute-start.29
  229.9 5.6 collective-permute-start.34
  236.2 5.6 collective-permute-start.33
  243.3 11.8 %collective-permute-start.36 = (bf16[144,2048]{1,0:T(8,128)(2,1)S(1)}, bf16[144,2048]{1,0:T(8,128)(2,1)S(1)}, u32[]{:S(2)}, u32[]{:S(2)}) collective-permute-start(bf16[144,2048]{1,0:T(8,128)(2,1)S(1)} %fusion.7), channel_id=1, source_target_pairs={{32,0},{64,32},{96,64},{33,1},{65,33},{97,65},{34,2},{66,34},{98,6... | collective-permute-start | bytes 1769480 | tf_op jit(solution)/shard_map/ppermute | solution.py:106
  256.3 5.6 collective-permute-start.39
  262.7 5.6 collective-permute-start.38
  270.7 5.6 collective-permute-start.43
  277.7 5.8 collective-permute-start.42
  290.9 9.7 %collective-permute-start.45 = (bf16[72,512]{1,0:T(8,128)(2,1)}, bf16[72,512]{1,0:T(8,128)(2,1)}, u32[]{:S(2)}, u32[]{:S(2)}) collective-permute-start(bf16[72,512]{1,0:T(8,128)(2,1)} %get-tuple-element.49), channel_id=1, source_target_pairs={{0,2},{2,0},{4,6},{6,4},{1,3},{3,1},{5,7},{7,5},{8,10},{10,8},{12,... | collective-permute-start | bytes 221192 | tf_op jit(solution)/shard_map/ppermute | solution.py:26
  291.1 9.5 %collective-permute-start.47 = (bf16[72,512]{1,0:T(8,128)(2,1)}, bf16[72,512]{1,0:T(8,128)(2,1)}, u32[]{:S(2)}, u32[]{:S(2)}) collective-permute-start(bf16[72,512]{1,0:T(8,128)(2,1)} %get-tuple-element.50), channel_id=1, source_target_pairs={{0,6},{2,4},{4,2},{6,0},{1,7},{3,5},{5,3},{7,1},{8,14},{10,12},{12... | collective-permute-start | bytes 221192 | tf_op jit(solution)/shard_map/ppermute | solution.py:26
  302.3 11.8 %collective-permute-start.48 = (bf16[72,512]{1,0:T(8,128)(2,1)}, bf16[72,512]{1,0:T(8,128)(2,1)}, u32[]{:S(2)}, u32[]{:S(2)}) collective-permute-start(bf16[72,512]{1,0:T(8,128)(2,1)} %get-tuple-element.48), channel_id=1, source_target_pairs={{0,2},{2,0},{4,6},{6,4},{1,3},{3,1},{5,7},{7,5},{8,10},{10,8},{12,... | collective-permute-start | bytes 221192 | tf_op jit(solution)/shard_map/ppermute | solution.py:26
  306.5 55.4 %all-to-all-start = ((bf16[144,8,1024]{2,0,1:T(8,128)(2,1)}), bf16[144,8,1024]{2,0,1:T(8,128)(2,1)}, u32[]{:S(2)}, u32[]{:S(2)}) async-start(bf16[144,8,1024]{2,0,1:T(8,128)(2,1)} %copy.39), calls=%async_computation | async-start | bytes 4718592 | tf_op jit(solution)/shard_map/all_to_all | solution.py:82
  311.0 31.2 %collective-permute-start.46 = (bf16[72,512]{1,0:T(8,128)(2,1)S(1)}, bf16[72,512]{1,0:T(8,128)(2,1)S(1)}, u32[]{:S(2)}, u32[]{:S(2)}) collective-permute-start(bf16[72,512]{1,0:T(8,128)(2,1)S(1)} %copy-done.67), channel_id=1, source_target_pairs={{0,6},{2,4},{4,2},{6,0},{1,7},{3,5},{5,3},{7,1},{8,14},{10,12},{12... | collective-permute-start | bytes 221192 | tf_op jit(solution)/shard_map/ppermute | solution.py:26
  347.0 5.6 collective-permute-start.51
  353.3 5.6 collective-permute-start.50
  360.5 14.3 %collective-permute-start.53 = (bf16[144,2048]{1,0:T(8,128)(2,1)}, bf16[144,2048]{1,0:T(8,128)(2,1)S(1)}, u32[]{:S(2)}, u32[]{:S(2)}) collective-permute-start(bf16[144,2048]{1,0:T(8,128)(2,1)} %fusion.9), channel_id=1, source_target_pairs={{32,0},{64,32},{96,64},{33,1},{65,33},{97,65},{34,2},{66,34},{98,6... | collective-permute-start | bytes 1769480 | tf_op jit(solution)/shard_map/ppermute | solution.py:106
  366.2 23.9 %all-to-all-start.3 = ((bf16[8,144,512]{2,1,0:T(8,128)(2,1)}), bf16[8,144,512]{2,1,0:T(8,128)(2,1)}, u32[]{:S(2)}, u32[]{:S(2)}) async-start(bf16[8,144,512]{2,1,0:T(8,128)(2,1)} %bitcast.201), calls=%async_computation.3 | async-start | bytes 2359296 | tf_op jit(solution)/shard_map/all_to_all | solution.py:84
  370.5 119.2 %all-gather.9.cloned.1.call-start = ((), (), s32[]{:S(2)}) async-start(), calls=%async_computation.6 | async-start | bytes 1327104 | tf_op jit(solution)/shard_map/all_gather | solution.py:88
  378.5 9.3 %collective-permute-start.54 = (bf16[72,512]{1,0:T(8,128)(2,1)S(1)}, bf16[72,512]{1,0:T(8,128)(2,1)S(1)}, u32[]{:S(2)}, u32[]{:S(2)}) collective-permute-start(bf16[72,512]{1,0:T(8,128)(2,1)S(1)} %get-tuple-element.41), channel_id=1, source_target_pairs={{0,2},{2,0},{4,6},{6,4},{1,3},{3,1},{5,7},{7,5},{8,10},{10,8},{12,... | collective-permute-start | bytes 221192 | tf_op jit(solution)/shard_map/ppermute | solution.py:26
  378.9 10.1 %collective-permute-start.56 = (bf16[72,512]{1,0:T(8,128)(2,1)S(1)}, bf16[72,512]{1,0:T(8,128)(2,1)S(1)}, u32[]{:S(2)}, u32[]{:S(2)}) collective-permute-start(bf16[72,512]{1,0:T(8,128)(2,1)S(1)} %get-tuple-element.42), channel_id=1, source_target_pairs={{0,6},{2,4},{4,2},{6,0},{1,7},{3,5},{5,3},{7,1},{8,14},{10,12},{12... | collective-permute-start | bytes 221192 | tf_op jit(solution)/shard_map/ppermute | solution.py:26
  389.7 4.8 collective-permute-start.57
  392.3 5.6 collective-permute-start.55
  404.3 5.2 collective-permute-start.58
  404.9 6.8 %collective-permute-start.60 = (bf16[72,512]{1,0:T(8,128)(2,1)S(1)}, bf16[72,512]{1,0:T(8,128)(2,1)S(1)}, u32[]{:S(2)}, u32[]{:S(2)}) collective-permute-start(bf16[72,512]{1,0:T(8,128)(2,1)S(1)} %get-tuple-element.38), channel_id=1, source_target_pairs={{0,6},{2,4},{4,2},{6,0},{1,7},{3,5},{5,3},{7,1},{8,14},{10,12},{12... | collective-permute-start | bytes 221192 | tf_op jit(solution)/shard_map/ppermute | solution.py:26
  412.7 5.6 collective-permute-start.59
  422.9 4.9 collective-permute-start.62
  423.7 5.8 collective-permute-start.64
  430.6 5.6 collective-permute-start.63
  446.1 5.6 collective-permute-start.68
  452.0 5.6 collective-permute-start.67
  458.8 11.9 %all-to-all-start.1 = ((bf16[4,144,512]{2,1,0:T(8,128)(2,1)}), bf16[4,144,512]{2,1,0:T(8,128)(2,1)S(1)}, u32[]{:S(2)}, u32[]{:S(2)}) async-start(bf16[4,144,512]{2,1,0:T(8,128)(2,1)} %pad_maximum_fusion.1), calls=%async_computation.1 | async-start | bytes 1179648 | tf_op jit(solution)/shard_map/all_to_all | solution.py:122
  470.6 34.4 %all-to-all-start.2 = ((bf16[8,144,1024]{2,1,0:T(8,128)(2,1)}), bf16[8,144,1024]{2,1,0:T(8,128)(2,1)}, u32[]{:S(2)}, u32[]{:S(2)}) async-start(bf16[8,144,1024]{2,1,0:T(8,128)(2,1)} %fusion.48), calls=%async_computation.2 | async-start | bytes 4718592 | tf_op jit(solution)/shard_map/all_to_all | solution.py:120
  475.0 11.1 %collective-permute-start.70 = (bf16[4,144,512]{2,1,0:T(8,128)(2,1)S(1)}, bf16[4,144,512]{2,1,0:T(8,128)(2,1)S(1)}, u32[]{:S(2)}, u32[]{:S(2)}) collective-permute-start(bf16[4,144,512]{2,1,0:T(8,128)(2,1)S(1)} %all-to-all-done.1), channel_id=1, source_target_pairs={{0,1},{1,0},{2,3},{3,2},{4,5},{5,4},{6,7},{7,6},{8,9},{9,8},{10,11... | collective-permute-start | bytes 1769480 | tf_op jit(solution)/shard_map/ppermute | solution.py:26
  518.5 4.9 collective-permute-start.73
  527.0 4.8 collective-permute-start.75
  531.8 4.7 collective-permute-start.76
  536.5 17.5 %collective-permute-start.77 = (f32[8,128]{1,0:T(8,128)S(1)}, f32[8,128]{1,0:T(8,128)S(1)}, u32[]{:S(2)}, u32[]{:S(2)}) collective-permute-start(f32[8,128]{1,0:T(8,128)S(1)} %add.681), channel_id=1, source_target_pairs={{0,96},{32,64},{64,32},{96,0},{1,97},{33,65},{65,33},{97,1},{2,98}... | collective-permute-start | bytes 12296 | tf_op jit(solution)/shard_map/ppermute | solution.py:26
  (94 other events, 1477.1 us)
Sparse Core Ops, SparseCore 0:
  10.6 52.1 all-gather.4
  64.5 49.8 all-gather.6
Sparse Core Ops, SparseCore 1:
  392.4 24.6 all-gather.8

commit v2 on v1

v2 whole, which is shorter than its diff:
```python
import math

import jax
import jax.numpy as jnp
from jax import lax
from jax.experimental import pallas as pl
from jax.experimental.pallas import tpu as pltpu
from jax.sharding import Mesh
from jax.sharding import PartitionSpec as P

beta_one = 0.9
beta_two = 0.95
adam_eps = 1e-08
learn_rate = 0.01
weight_decay = 0.1
step_count = 100

SECTION = ("z", "y")
DP = ("x", "core")
PLANE = ("y", "core")


VMEM_LIMIT = 40 * 1024 * 1024
PAIRS = ((0, 1), (0, 2), (0, 3), (1, 2), (1, 3), (2, 3))


def dot(left, right, dims):
    return lax.dot_general(left, right, (dims, ((), ())), preferred_element_type=jnp.float32)


def dot_nt(left, right):
    return dot(left, right, ((1,), (1,)))


def call(kernel, grid, in_specs, out_specs, out_shape, scratch=(), cost=None):
    return pl.pallas_call(
        kernel,
        grid=grid,
        in_specs=in_specs,
        out_specs=out_specs,
        out_shape=out_shape,
        scratch_shapes=list(scratch),
        cost_estimate=cost,
        compiler_params=pltpu.CompilerParams(vmem_limit_bytes=VMEM_LIMIT),
    )


def whole(shape):
    return pl.BlockSpec(shape, lambda *_: (0,) * len(shape))


def swap(value, axis, mask):
    return lax.ppermute(value, axis, [(i, i ^ mask) for i in range(lax.axis_size(axis))])


def turn_by(value, axis, steps):
    count = lax.axis_size(axis)
    return lax.ppermute(value, axis, [(i, (i + steps) % count) for i in range(count)])


def addends_over_x(parts, masks=((1, 3), (3, 1))):
    pairs = []
    firsts = [swap(part, "x", masks[i][0]) for i, part in enumerate(parts)]
    halves = [
        (part.astype(jnp.float32) + other.astype(jnp.float32)).astype(jnp.bfloat16)
        for part, other in zip(parts, firsts)
    ]
    for i, half in enumerate(halves):
        pairs.append((half, swap(half, "x", masks[i][1])))
    return pairs


def sum_over_all(value):
    value = value + swap(value, "core", 1)
    for axis in ("x", "y", "z"):
        got = [turn_by(value, axis, steps) for steps in (1, 3, 2)]
        value = value + got[0] + got[1] + got[2]
    return value


def project(gradient, weights, first):
    rows, chip_width = gradient.shape
    _, head_size, share = weights.shape

    def kernel(g_ref, w_ref, out_ref):
        part = dot_nt(g_ref[:, :share], w_ref[0]) + dot_nt(g_ref[:, share:], w_ref[1])
        out_ref[...] = part.astype(jnp.bfloat16)

    return call(
        kernel,
        (2,),
        [
            whole((rows, chip_width)),
            pl.BlockSpec((2, head_size, share), lambda i: (first + i, 0, 0)),
        ],
        pl.BlockSpec((rows, head_size), lambda i: (0, i)),
        jax.ShapeDtypeStruct((rows, 2 * head_size), jnp.bfloat16),
        cost=pl.CostEstimate(
            flops=4 * rows * chip_width * head_size,
            bytes_accessed=4 * chip_width * head_size,
            transcendentals=0,
        ),
    )(gradient, weights)


def solve(addends, links, b_ref):
    low, low_got, high, high_got = addends
    head_size = links.shape[-1]
    sums = []
    for own, got in ((low, low_got), (high, high_got)):
        both = own[...].astype(jnp.float32) + got[...].astype(jnp.float32)
        sums += [both[:, :head_size], both[:, head_size:]]
    backs = [None] * 4
    for at in (3, 2, 1, 0):
        total = sums[at]
        for other in range(at + 1, 4):
            link = links[:, PAIRS.index((at, other))].reshape(head_size, head_size)
            total = total + dot_nt(backs[other], link)
        backs[at] = total.astype(jnp.bfloat16)
        b_ref[at] = backs[at]


def advance(gradient, addends, links, weights):
    rows, chip_width = gradient.shape
    count, share, head_size = weights.shape
    steps = 4
    block = chip_width // steps
    weights = weights.reshape(4, steps, block, head_size)
    flat = [array for pair in addends for array in pair]

    def kernel(g_ref, low, low_got, high, high_got, m_ref, w_ref, b_ref, out_ref):
        @pl.when(pl.program_id(0) == 0)
        def _():
            solve((low, low_got, high, high_got), m_ref, b_ref)

        total = g_ref[...].astype(jnp.float32)
        for at in range(4):
            total = total + dot_nt(b_ref[at], w_ref[at, 0])
        out_ref[...] = total.astype(jnp.bfloat16)

    return call(
        kernel,
        (steps,),
        [pl.BlockSpec((rows, block), lambda i: (0, i))]
        + [whole((rows, 2 * head_size))] * 4
        + [
            whole(links.shape),
            pl.BlockSpec((4, 1, block, head_size), lambda i: (0, i, 0, 0)),
        ],
        [
            whole((4, rows, head_size)),
            pl.BlockSpec((rows, block), lambda i: (0, i)),
        ],
        [
            jax.ShapeDtypeStruct((4, rows, head_size), jnp.bfloat16),
            jax.ShapeDtypeStruct((rows, chip_width), jnp.bfloat16),
        ],
        cost=pl.CostEstimate(
            flops=2 * rows * head_size * (6 * head_size + 4 * chip_width),
            bytes_accessed=8 * chip_width * head_size + 12 * head_size * head_size,
            transcendentals=0,
        ),
    )(gradient, *flat, links, weights)


def solve_last(addends, links):
    rows, two = addends[0][0].shape
    head_size = two // 2
    flat = [array for pair in addends for array in pair]

    def kernel(low, low_got, high, high_got, m_ref, b_ref):
        solve((low, low_got, high, high_got), m_ref, b_ref)

    return call(
        kernel,
        (1,),
        [whole((rows, two))] * 4 + [whole(links.shape)],
        whole((4, rows, head_size)),
        jax.ShapeDtypeStruct((4, rows, head_size), jnp.bfloat16),
        cost=pl.CostEstimate(
            flops=12 * rows * head_size * head_size,
            bytes_accessed=12 * head_size * head_size,
            transcendentals=0,
        ),
    )(*flat, links)


def rebuild(gradient, backs, weights):
    rows, chip_width = gradient.shape
    count, share, head_size = weights.shape
    steps = 4
    block = chip_width // steps
    weights = weights.reshape(4, steps, block, head_size)

    def kernel(g_ref, b_ref, w_ref, out_ref):
        total = g_ref[...]
        out_ref[3, 0] = total
        for at in (3, 2, 1):
            total = (total.astype(jnp.float32) + dot_nt(b_ref[at], w_ref[at, 0])).astype(
                jnp.bfloat16
            )
            out_ref[at - 1, 0] = total

    return call(
        kernel,
        (steps,),
        [
            pl.BlockSpec((rows, block), lambda i: (0, i)),
            whole((4, rows, head_size)),
            pl.BlockSpec((4, 1, block, head_size), lambda i: (0, i, 0, 0)),
        ],
        pl.BlockSpec((4, 1, rows, block), lambda i: (0, i // 2, 0, i % 2)),
        jax.ShapeDtypeStruct((4, 2, rows, share), jnp.bfloat16),
        cost=pl.CostEstimate(
            flops=6 * rows * head_size * chip_width,
            bytes_accessed=8 * chip_width * head_size,
            transcendentals=0,
        ),
    )(gradient, backs, weights)


def averaged(picked, back, gradient, hidden, contributors):
    rows, share = picked.shape
    head_size = back.shape[1]
    steps = 4
    block = share // steps

    def kernel(count_ref, p_ref, b_ref, g_ref, h_ref, out_ref, sum_ref):
        value = dot(p_ref[...], b_ref[...], ((0,), (0,))) / count_ref[0]
        output = dot(g_ref[...], h_ref[...], ((0,), (0,))) / count_ref[0]
        out_ref[:, :head_size] = value
        out_ref[:, head_size:] = output
        square = jnp.sum(value * value + output * output)

        @pl.when(pl.program_id(0) == 0)
        def _():
            sum_ref[...] = jnp.zeros_like(sum_ref)

        sum_ref[...] += square

    return call(
        kernel,
        (steps,),
        [
            pl.BlockSpec(memory_space=pltpu.SMEM),
            pl.BlockSpec((rows, block), lambda i: (0, i)),
            whole((rows, head_size)),
            pl.BlockSpec((rows, block), lambda i: (0, i)),
            whole((rows, head_size)),
        ],
        [
            pl.BlockSpec((block, 2 * head_size), lambda i: (i, 0)),
            whole((8, 128)),
        ],
        [
            jax.ShapeDtypeStruct((share, 2 * head_size), jnp.float32),
            jax.ShapeDtypeStruct((8, 128), jnp.float32),
        ],
        cost=pl.CostEstimate(
            flops=4 * rows * share * head_size,
            bytes_accessed=4 * rows * (share + head_size) + 8 * share * head_size,
            transcendentals=0,
        ),
    )(contributors, picked, back, gradient, hidden)


def update(factor, grads, master, moment_one, moment_two):
    share, columns = grads.shape
    block = min(share, 128)

    def kernel(factor_ref, grad_ref, master_ref, one_ref, two_ref, out_ref, new_one_ref, new_two_ref):
        scaled = factor_ref[0] * grad_ref[...]
        new_one = beta_one * one_ref[0].astype(jnp.float32) + (1.0 - beta_one) * scaled
        new_two = beta_two * two_ref[0].astype(jnp.float32) + (1.0 - beta_two) * scaled * scaled
        hat_one = new_one / (1.0 - beta_one**step_count)
        hat_two = new_two / (1.0 - beta_two**step_count)
        old_master = master_ref[0]
        out_ref[0] = old_master - learn_rate * (
            hat_one / (jnp.sqrt(hat_two) + adam_eps) + weight_decay * old_master
        )
        new_one_ref[0] = new_one.astype(jnp.bfloat16)
        new_two_ref[0] = new_two.astype(jnp.bfloat16)

    tile = pl.BlockSpec((1, block, columns), lambda i: (0, i, 0))
    return call(
        kernel,
        (share // block,),
        [
            pl.BlockSpec(memory_space=pltpu.SMEM),
            pl.BlockSpec((block, columns), lambda i: (i, 0)),
            tile,
            tile,
            tile,
        ],
        [tile] * 3,
        [
            jax.ShapeDtypeStruct((1, share, columns), jnp.float32),
            jax.ShapeDtypeStruct((1, share, columns), jnp.bfloat16),
            jax.ShapeDtypeStruct((1, share, columns), jnp.bfloat16),
        ],
        cost=pl.CostEstimate(
            flops=20 * share * columns,
            bytes_accessed=20 * share * columns,
            transcendentals=share * columns,
        ),
    )(factor, grads, master, moment_one, moment_two)


def shards(
    acts, out_grad, w_value, w_output, order, alive, flags, clip_rms, master, moment_one, moment_two
):
    z, y, x, core = (lax.axis_index(axis) for axis in ("z", "y", "x", "core"))
    planes, columns, across = (lax.axis_size(axis) for axis in ("z", "y", "x"))
    replicas = across * lax.axis_size("core")
    own_value, own_output = w_value[0], w_output[0]
    share, head_size = own_value.shape
    micro, tok_rows, width = out_grad.shape
    rows = micro * tok_rows
    chip_width = 2 * share

    output_weight = lax.all_gather(own_output, PLANE, axis=0)
    value_weight = lax.all_gather(own_value, PLANE, axis=0)
    flag_row = lax.all_gather(flags[0, 0], DP)

    top = out_grad.reshape(rows, width)
    own_slice = lax.dynamic_slice(top, (0, x * chip_width), (rows, chip_width))
    gradient = jnp.where(
        jnp.logical_and(z == planes - 1, x == y), own_slice, jnp.zeros_like(own_slice)
    )
    for turn in range(1, across):
        other = lax.rem(x + turn, across)
        piece = lax.dynamic_slice(top, (0, other * chip_width), (rows, chip_width))
        base = (planes - 1) * columns * across
        pairs = [
            (base + i * across + i, base + i * across + (i + turn) % across) for i in range(columns)
        ]
        gradient = gradient + lax.ppermute(piece, ("z", "y", "x"), pairs)

    keep = alive * (1 - flag_row)
    replica = lax.axis_index(DP)
    own_keep = (alive[replica] * (1 - flags[0, 0])).astype(jnp.bfloat16)
    picked = jnp.take(acts[0], order[0], axis=0).reshape(rows, width) * own_keep
    picked = lax.all_to_all(picked, DP, split_axis=1, concat_axis=0, tiled=True)
    hidden_part = dot(picked, own_value, ((1,), (0,))).astype(jnp.bfloat16)
    hidden_part = lax.all_to_all(
        hidden_part.reshape(replicas, rows, head_size), DP, split_axis=0, concat_axis=0, tiled=True
    )
    hidden = jnp.sum(hidden_part.astype(jnp.float32), axis=0).astype(jnp.bfloat16)
    output_weight, hidden, gradient, keep = lax.optimization_barrier(
        (output_weight, hidden, gradient, keep)
    )
    hidden = lax.all_gather(hidden, DP, axis=0, tiled=True)

    eighth = head_size // replicas
    at_row = lax.axis_index(PLANE) * eighth
    link = []
    for at, other in PAIRS:
        total = 0.0
        for half in range(2):
            left = lax.dynamic_slice(output_weight[2 * at + half], (at_row, 0), (eighth, share))
            total = total + dot(left, value_weight[2 * other + half], ((1,), (0,)))
        link.append(total.astype(jnp.bfloat16))
    (low, low_got), (high, high_got) = addends_over_x((jnp.stack(link[:3]), jnp.stack(link[3:])))
    link = jnp.concatenate(
        [
            (low.astype(jnp.float32) + low_got.astype(jnp.float32)).astype(jnp.bfloat16),
            (high.astype(jnp.float32) + high_got.astype(jnp.float32)).astype(jnp.bfloat16),
        ]
    )
    links = lax.all_gather(link, PLANE, axis=0)

    kept_gradient, kept_back = gradient, None
    for turn in range(planes):
        high = project(gradient, output_weight, 2)
        low = project(gradient, output_weight, 0)
        addends = addends_over_x((low, high))
        if turn < planes - 1:
            backs, gradient = advance(gradient, addends, links, value_weight)
            gradient = lax.ppermute(gradient, "z", [(i, i - 1) for i in range(1, planes)])
            kept_gradient = kept_gradient + gradient
        else:
            backs = solve_last(addends, links)
        kept_back = backs if kept_back is None else kept_back + backs

    sent = rebuild(kept_gradient, kept_back, value_weight)
    grad_rows = lax.all_to_all(
        sent.reshape(replicas, rows, share), PLANE, split_axis=0, concat_axis=0, tiled=True
    )
    grad_rows = grad_rows.reshape(replicas * rows, share)
    backs = lax.all_to_all(kept_back, "y", split_axis=0, concat_axis=0, tiled=True)
    others = swap(backs, "core", 1)
    back_rows = jnp.stack(
        [jnp.where(core == 0, backs, others), jnp.where(core == 0, others, backs)], axis=1
    ).reshape(replicas * rows, head_size)

    contributors = jnp.maximum(jnp.sum(keep).astype(jnp.float32), 1.0)[None]
    grads, square = averaged(picked, back_rows, grad_rows, hidden, contributors)
    norm = jnp.sqrt(sum_over_all(square)[0, :1])
    sections = planes * columns
    threshold = clip_rms * math.sqrt(2 * width * head_size * sections)
    factor = jnp.minimum(1.0, threshold / (norm + 1e-06))
    return tuple(update(factor, grads, master, moment_one, moment_two))


def solution(mesh):
    physical = Mesh(mesh.devices.reshape(4, 4, 4, 2), ("z", "y", "x", "core"))
    in_specs = (
        P(SECTION, None, DP, None),
        P(None, DP, None),
        P(SECTION, DP, None),
        P(SECTION, None, DP),
        P(DP, None),
        P(),
        P(SECTION, DP),
        P(),
        P(SECTION, DP, None),
        P(SECTION, DP, None),
        P(SECTION, DP, None),
    )
    out_specs = (P(SECTION, DP, None), P(SECTION, DP, None), P(SECTION, DP, None))
    return jax.shard_map(
        shards, mesh=physical, in_specs=in_specs, out_specs=out_specs, check_vma=False
    )
```

time: 596 us -> 410 us (0.69); the launches traced: 586 us -> 409 us
  waiting for transfers between devices: 288 us -> 196 us
  starting transfers between devices: 121 us -> 57.5 us
  matrix products: 69.3 us -> 19.3 us
  Pallas kernels: 0 us -> 48.1 us
  local copies, waits for them, and re-layouts: 54.4 us -> 40.3 us
  other arithmetic: 24.4 us -> 11.3 us
  blocking collectives: 8.12 us -> 18.7 us
    ppermute x72 -> x22, waiting for transfers between devices: 153 us -> 71.9 us  [swap(): lax.ppermute(value, axis, [(i, i ^ mask) for i in range(lax.axis_size(axi...]
    ppermute x72 -> x22, starting transfers between devices: 96.6 us -> 19.8 us  [swap(): lax.ppermute(value, axis, [(i, i ^ mask) for i in range(lax.axis_size(axi...]
    dot_general x53 -> x13, matrix products: 69.3 us -> 19.3 us  [dot(): lax.dot_general(left, right, (dims, ((), ())), preferred_element_type=jnp...]
    pallas_call x0 -> x15, Pallas kernels: none -> 48.1 us  [the longest x3 15.6 us: advance(): call(kernel, (steps,), [pl.BlockSpec((rows, block), lambda i: (0, i))] +...]
    all_gather x1, waiting for transfers between devices: 45.2 us -> 0.01 us  [shards(): output_weight = lax.all_gather(own_output, PLANE, axis=0)]
    all_to_all x1, waiting for transfers between devices: 0.01 us -> 22.8 us  [shards(): picked = lax.all_to_all(picked, DP, split_axis=1, concat_axis=0, tiled=True)]
    all_gather x1, waiting for transfers between devices: 40.9 us -> 22.6 us  [shards(): value_weight = lax.all_gather(own_value, PLANE, axis=0)]
    convert_element_type x47 -> x12, other arithmetic: 14.8 us -> 0.85 us  [the longest x10 0.7 us: addends_over_x(): (part.astype(jnp.float32) + other.astype(jnp.float32)).astype(jnp.bfloat16)]
  transfers between devices with their start and end apart: 85 -> 45, of which waited for: 73 -> 33; matrix products, arithmetic and copies ran while one was open for 14% -> 9% of each run, Pallas kernels for 0% -> 4%
where the time goes in v2:
time: 410 us; the launch traced here: 409 us
  waiting for transfers between devices  196 us (48%)
  starting transfers between devices  57.5 us (14%)
  Pallas kernels  48.1 us (12%)
  local copies, waits for them, and re-layouts  40.3 us (10%)
  matrix products  19.3 us (5%)
  blocking collectives  18.7 us (5%)
  between operations  17.9 us (4%)
  other arithmetic  11.3 us (3%)
    ppermute x22, waiting for transfers between devices, swap(): lax.ppermute(value, axis, [(i, i ^ mask) for i in range(lax.axis_size(axi...  71.9 us
    ppermute x3, waiting for transfers between devices, shards(): lax.ppermute(gradient, 'z', [(i, i - 1) for i in range(1, planes)])  37.8 us
    unnamed x66, local copies, waits for them, and re-layouts  27.7 us
    all_to_all x1, waiting for transfers between devices, shards(): lax.all_to_all(sent.reshape(replicas, rows, share), PLANE, split_axis=0,...  27.4 us
    all_to_all x1, waiting for transfers between devices, shards(): picked = lax.all_to_all(picked, DP, split_axis=1, concat_axis=0, tiled=True)  22.8 us
    all_gather x1, waiting for transfers between devices, shards(): value_weight = lax.all_gather(own_value, PLANE, axis=0)  22.6 us
    ppermute x22, starting transfers between devices, swap(): lax.ppermute(value, axis, [(i, i ^ mask) for i in range(lax.axis_size(axi...  19.8 us
    dot_general x13, matrix products, dot(): lax.dot_general(left, right, (dims, ((), ())), preferred_element_type=jnp...  19.3 us
  transfers between devices with their start and end apart: 45, of which 33 were waited for; matrix products, arithmetic and copies ran while one was open for 9% of the time, Pallas kernels for 4%

profile of v2, /device:TPU:0, one launch (start us, length us, event | category | flops | bytes accessed | tf_op | source)
XLA Modules:
  0.0 409.1 jit_solution(16777641020234239939)
XLA Ops:
  11.9 2.2 gather_fusion
  14.1 3.3 copy.18
  17.6 4.1 %fusion = bf16[144,8,1024]{2,0,1:T(8,128)(2,1)} fusion(bf16[144,8,1024]{2,1,0:T(8,128)(2,1)S(1)} %bitcast.115, pred[144]{0:T(512)(128)(4,1)S(1)} %broadcast_in_dim.21, bf16[]{:T(256)S(6)} %convert_element_type.137), kind=kLoop, calls=%fused_computation.3 | loop fusion | flops 2359296 | bytes 4718738 | tf_op jit(solution)/shard_map/mul | solution.py:342
  21.7 4.4 %all-to-all-start = ((bf16[144,8,1024]{2,0,1:T(8,128)(2,1)}), bf16[144,8,1024]{2,0,1:T(8,128)(2,1)S(1)}, u32[]{:S(2)}, u32[]{:S(2)}) async-start(bf16[144,8,1024]{2,0,1:T(8,128)(2,1)} %fusion), calls=%async_computation | async-start | bytes 4718592 | tf_op jit(solution)/shard_map/all_to_all | solution.py:343
  26.1 2.8 constant_dynamic-slice_fusion.2
  33.3 22.8 %all-to-all-done = bf16[144,8,1024]{2,0,1:T(8,128)(2,1)S(1)} async-done(((bf16[144,8,1024]{2,0,1:T(8,128)(2,1)}), bf16[144,8,1024]{2,0,1:T(8,128)(2,1)S(1)}, u32[]{:S(2)}, u32[]{:S(2)}) %all-to-all-start) | async-done | bytes 2359328 | tf_op jit(solution)/shard_map/all_to_all | solution.py:343
  56.1 2.4 convolution_convert_fusion
  58.5 3.7 all-to-all-start.1
  63.7 18.7 %all-reduce = s32[8]{0:T(128)S(1)} all-reduce(s32[8]{0:T(128)S(1)} %bitcast_dynamic-update-slice_fusion), channel_id=2, replica_groups=mesh['z'=4,'y'=4,'x'=4,'core'=2] {'x','core'}, use_global_device_ids=true, to_apply=%add | all-reduce | flops 8 | bytes 64
  82.4 2.0 add_add_fusion.2.g_ref
  85.3 5.7 %fusion.57 = (bf16[1,512,1024]{2,1,0:T(8,128)(2,1)S(1)}, bf16[1,512,1024]{2,1,0:T(8,128)(2,1)}, bf16[1,512,1024]{2,1,0:T(8,128)(2,1)}, bf16[1,512,1024]{2,1,0:T(...) fusion(bf16[8,512,1024]{2,1,0:T(8,128)(2,1)} %all-gather.7.cloned.1.call-done.w_ref), kind=kLoop, calls=%fused_computation.105 | loop fusion | bytes 12582912 | tf_op jit(solution)/shard_map/slice | solution.py:360
  91.0 22.6 %all-gather.9.cloned.1.call-done = bf16[8,1024,512]{2,1,0:T(8,128)(2,1)} async-done(((bf16[1,1024,512]{2,1,0:T(8,128)(2,1)}), bf16[8,1024,512]{2,1,0:T(8,128)(2,1)}) %all-gather.9.cloned.1.call-update) | async-done | bytes 8388624 | tf_op jit(solution)/shard_map/all_gather | solution.py:322
  115.3 1.9 fusion.16
  132.2 2.2 collective-permute-start.9
  135.6 5.6 %collective-permute-done.9 = bf16[3,64,512]{2,1,0:T(8,128)(2,1)S(1)} collective-permute-done((bf16[3,64,512]{2,1,0:T(8,128)(2,1)S(1)}, bf16[3,64,512]{2,1,0:T(8,128)(2,1)S(1)}, u32[]{:S(2)}, u32[]{:S(2)}) %collective-permute-start.9) | collective-permute-done | bytes 196640 | tf_op jit(solution)/shard_map/ppermute | solution.py:53
  141.6 2.9 collective-permute-done.8
  144.5 2.7 collective-permute-done.10
  148.2 3.4 copy-done.2
  153.3 2.1 collective-permute-start.5
  155.4 1.7 shard_map.130
  157.2 4.0 collective-permute-done.5
  161.5 5.0 %collective-permute-done.3 = bf16[144,1024]{1,0:T(8,128)(2,1)S(1)} collective-permute-done((bf16[144,1024]{1,0:T(8,128)(2,1)S(1)}, bf16[144,1024]{1,0:T(8,128)(2,1)S(1)}, u32[]{:S(2)}, u32[]{:S(2)}) %collective-permute-start.3) | collective-permute-done | bytes 294944 | tf_op jit(solution)/shard_map/ppermute | solution.py:53
  169.7 4.9 %collective-permute-done.4.low_got = bf16[144,1024]{1,0:T(8,128)(2,1)S(1)} collective-permute-done((bf16[144,1024]{1,0:T(8,128)(2,1)S(1)}, bf16[144,1024]{1,0:T(8,128)(2,1)S(1)}, u32[]{:S(2)}, u32[]{:S(2)}) %collective-permute-start.4) | collective-permute-done | bytes 294944 | tf_op jit(solution)/shard_map/ppermute | solution.py:53
  175.3 3.4 copy-done.5
  178.7 1.9 copy-done.8
  180.6 5.2 %shard_map.132 = (bf16[4,144,512]{2,1,0:T(8,128)(2,1)S(1)}, bf16[144,2048]{1,0:T(8,128)(2,1)S(1)}) custom-call(bf16[144,2048]{1,0:T(8,128)(2,1)S(1)} %add_add_fusion.2.g_ref, bf16[144,1024]{1,0:T(8,128)(2,1)S(1)} %add_convert_fusion.7.low, bf16[144,1024]{1,0:T(8,128)(2,1)S(1)} %collective-permute-done.4.low_got, ...), custom_call_target="tpu_custom_call" | custom-call | flops 1660944384 | bytes 11534336 | tf_op jit(solution)/shard_map/pallas_call | solution.py:141
  187.1 16.1 %collective-permute-done.11.g_ref = bf16[144,2048]{1,0:T(8,128)(2,1)S(1)} collective-permute-done((bf16[144,2048]{1,0:T(8,128)(2,1)S(1)}, bf16[144,2048]{1,0:T(8,128)(2,1)S(1)}, u32[]{:S(2)}, u32[]{:S(2)}) %collective-permute-start.11) | collective-permute-done | bytes 589856 | tf_op jit(solution)/shard_map/ppermute | solution.py:379
  203.2 3.4 copy-done.3
  208.3 2.8 collective-permute-start.14
  211.1 1.7 shard_map.133
  213.1 4.8 %collective-permute-done.14 = bf16[144,1024]{1,0:T(8,128)(2,1)S(1)} collective-permute-done((bf16[144,1024]{1,0:T(8,128)(2,1)S(1)}, bf16[144,1024]{1,0:T(8,128)(2,1)S(1)}, u32[]{:S(2)}, u32[]{:S(2)}) %collective-permute-start.14) | collective-permute-done | bytes 294944 | tf_op jit(solution)/shard_map/ppermute | solution.py:53
  218.4 4.2 %collective-permute-done.12 = bf16[144,1024]{1,0:T(8,128)(2,1)S(1)} collective-permute-done((bf16[144,1024]{1,0:T(8,128)(2,1)S(1)}, bf16[144,1024]{1,0:T(8,128)(2,1)S(1)}, u32[]{:S(2)}, u32[]{:S(2)}) %collective-permute-start.12) | collective-permute-done | bytes 294944 | tf_op jit(solution)/shard_map/ppermute | solution.py:53
  222.8 4.5 %collective-permute-done.15.high_got = bf16[144,1024]{1,0:T(8,128)(2,1)S(1)} collective-permute-done((bf16[144,1024]{1,0:T(8,128)(2,1)S(1)}, bf16[144,1024]{1,0:T(8,128)(2,1)S(1)}, u32[]{:S(2)}, u32[]{:S(2)}) %collective-permute-start.15) | collective-permute-done | bytes 294944 | tf_op jit(solution)/shard_map/ppermute | solution.py:53
  227.3 3.5 collective-permute-done.13.low_got
  230.7 3.4 copy-done.6
  234.1 5.2 %shard_map.135 = (bf16[4,144,512]{2,1,0:T(8,128)(2,1)S(1)}, bf16[144,2048]{1,0:T(8,128)(2,1)S(1)}) custom-call(bf16[144,2048]{1,0:T(8,128)(2,1)S(1)} %collective-permute-done.11.g_ref, bf16[144,1024]{1,0:T(8,128)(2,1)S(1)} %add_convert_fusion.5.low, bf16[144,1024]{1,0:T(8,128)(2,1)S(1)} %collective-permute-done.13.low_got, ...), custom_call_target="tpu_custom_call" | custom-call | flops 1660944384 | bytes 11534336 | tf_op jit(solution)/shard_map/pallas_call | solution.py:141
  240.6 11.2 %collective-permute-done.16.g_ref = bf16[144,2048]{1,0:T(8,128)(2,1)S(1)} collective-permute-done((bf16[144,2048]{1,0:T(8,128)(2,1)S(1)}, bf16[144,2048]{1,0:T(8,128)(2,1)S(1)}, u32[]{:S(2)}, u32[]{:S(2)}) %collective-permute-start.16) | collective-permute-done | bytes 589856 | tf_op jit(solution)/shard_map/ppermute | solution.py:379
  251.9 1.7 shard_map.137
  254.3 1.7 shard_map.136
  256.1 6.7 %collective-permute-done.19 = bf16[144,1024]{1,0:T(8,128)(2,1)S(1)} collective-permute-done((bf16[144,1024]{1,0:T(8,128)(2,1)S(1)}, bf16[144,1024]{1,0:T(8,128)(2,1)S(1)}, u32[]{:S(2)}, u32[]{:S(2)}) %collective-permute-start.19) | collective-permute-done | bytes 294944 | tf_op jit(solution)/shard_map/ppermute | solution.py:53
  265.6 4.1 collective-permute-done.20.high_got
  269.7 2.4 collective-permute-done.18.low_got
  272.1 5.2 %shard_map.138 = (bf16[4,144,512]{2,1,0:T(8,128)(2,1)S(1)}, bf16[144,2048]{1,0:T(8,128)(2,1)S(1)}) custom-call(bf16[144,2048]{1,0:T(8,128)(2,1)S(1)} %collective-permute-done.16.g_ref, bf16[144,1024]{1,0:T(8,128)(2,1)S(1)} %add_convert_fusion.3.low, bf16[144,1024]{1,0:T(8,128)(2,1)S(1)} %collective-permute-done.18.low_got, ...), custom_call_target="tpu_custom_call" | custom-call | flops 1660944384 | bytes 11534336 | tf_op jit(solution)/shard_map/pallas_call | solution.py:141
  279.4 10.5 %collective-permute-done.21.g_ref = bf16[144,2048]{1,0:T(8,128)(2,1)S(1)} collective-permute-done((bf16[144,2048]{1,0:T(8,128)(2,1)S(1)}, bf16[144,2048]{1,0:T(8,128)(2,1)S(1)}, u32[]{:S(2)}, u32[]{:S(2)}) %collective-permute-start.21) | collective-permute-done | bytes 589856 | tf_op jit(solution)/shard_map/ppermute | solution.py:379
  289.9 1.7 shard_map.140
  291.7 1.7 collective-permute-start.24
  293.4 1.7 shard_map.139
  295.2 6.3 %collective-permute-done.24 = bf16[144,1024]{1,0:T(8,128)(2,1)S(1)} collective-permute-done((bf16[144,1024]{1,0:T(8,128)(2,1)S(1)}, bf16[144,1024]{1,0:T(8,128)(2,1)S(1)}, u32[]{:S(2)}, u32[]{:S(2)}) %collective-permute-start.24) | collective-permute-done | bytes 294944 | tf_op jit(solution)/shard_map/ppermute | solution.py:53
  302.0 2.3 collective-permute-start.23
  304.3 4.1 collective-permute-done.25.high_got
  310.0 1.9 copy-done.10
  314.3 3.5 all-to-all-start.2
  317.9 3.4 copy-done.7
  321.4 5.1 %shard_map.142 = bf16[4,2,144,1024]{3,2,1,0:T(8,128)(2,1)} custom-call(bf16[144,2048]{1,0:T(8,128)(2,1)S(1)} %add_add_fusion.g_ref, bf16[4,144,512]{2,1,0:T(8,128)(2,1)} %add_add_fusion.1.b_ref, bf16[4,4,512,512]{3,2,1,0:T(8,128)(2,1)S(1)} %bitcast.107), custom_call_target="tpu_custom_call" | custom-call | flops 905969664 | bytes 8388608 | tf_op jit(solution)/shard_map/pallas_call | solution.py:204
  326.5 4.7 %all-to-all-start.3 = ((bf16[8,144,1024]{2,1,0:T(8,128)(2,1)}), bf16[8,144,1024]{2,1,0:T(8,128)(2,1)}, u32[]{:S(2)}, u32[]{:S(2)}) async-start(bf16[8,144,1024]{2,1,0:T(8,128)(2,1)} %bitcast.37), calls=%async_computation.3 | async-start | bytes 4718592 | tf_op jit(solution)/shard_map/all_to_all | solution.py:386
  334.0 27.4 %all-to-all-done.3 = bf16[8,144,1024]{2,1,0:T(8,128)(2,1)} async-done(((bf16[8,144,1024]{2,1,0:T(8,128)(2,1)}), bf16[8,144,1024]{2,1,0:T(8,128)(2,1)}, u32[]{:S(2)}, u32[]{:S(2)}) %all-to-all-start.3) | async-done | bytes 2359328 | tf_op jit(solution)/shard_map/all_to_all | solution.py:386
  362.6 6.1 %shard_map.143 = (f32[1024,1024]{1,0:T(8,128)S(1)}, f32[8,128]{1,0:T(8,128)S(1)}) custom-call(f32[1]{0:T(128)} %bitcast.13.count_ref, bf16[1152,1024]{1,0:T(8,128)(2,1)S(1)} %bitcast.113, bf16[1152,512]{1,0:T(8,128)(2,1)S(1)} %bitcast.114, bf16[1152,1024]{1,0:T(8,128)(2,1)} %bitcast.38.g_ref, bf16[1152,512]{1,0:T(8,128)(2,1)S(1)} %copy-done.24), custom_call_target="tpu_custom_call" | custom-call | flops 2415919104 | bytes 11272192 | tf_op jit(solution)/shard_map/pallas_call | solution.py:241
  370.5 2.7 collective-permute-start.29
  374.8 3.5 collective-permute-done.30
  378.9 2.7 collective-permute-start.32
  383.1 3.5 collective-permute-done.33
  389.9 2.0 collective-permute-start.36
  392.6 2.4 collective-permute-done.36
  396.3 6.3 %shard_map.144 = (f32[1,1024,1024]{2,1,0:T(8,128)}, bf16[1,1024,1024]{2,1,0:T(8,128)(2,1)}, bf16[1,1024,1024]{2,1,0:T(8,128)(2,1)}) custom-call(f32[1]{0:T(128)S(6)} %min.3.factor_ref, f32[1024,1024]{1,0:T(8,128)S(1)} %get-tuple-element.26.grad_ref, f32[1,1024,1024]{2,1,0:T(8,128)S(1)} %copy-done.13, bf16[1,1024,1024]{2,1,0:T(8,128)(2,1)S(1)} %copy-done.16, ...), custom_call_target="tpu_custom_call" | custom-call | flops 20971520 | bytes 20971520 | tf_op jit(solution)/shard_map/pallas_call | solution.py:285
  (165 shorter events, 63.4 us)
Async XLA Ops:
  7.2 4.7 %copy-start = (bf16[1,3,48,8192]{3,2,1,0:T(8,128)(2,1)S(1)}, bf16[1,3,48,8192]{3,2,1,0:T(8,128)(2,1)}, u32[]{:S(2)}) copy-start(bf16[1,3,48,8192]{3,2,1,0:T(8,128)(2,1)} %param.11) | copy-start | bytes 7077892
  7.2 78.2 %all-gather.7.cloned.1.call-start = ((), (), s32[]{:S(2)}) async-start(), calls=%async_computation.4 | async-start | bytes 9437184 | tf_op jit(solution)/shard_map/all_gather | solution.py:321
  7.9 105.7 %all-gather.9.cloned.1.call-start = ((), (), s32[]{:S(2)}) async-start(), calls=%async_computation.5 | async-start | bytes 9437184 | tf_op jit(solution)/shard_map/all_gather | solution.py:322
  21.7 34.4 %all-to-all-start = ((bf16[144,8,1024]{2,0,1:T(8,128)(2,1)}), bf16[144,8,1024]{2,0,1:T(8,128)(2,1)S(1)}, u32[]{:S(2)}, u32[]{:S(2)}) async-start(bf16[144,8,1024]{2,0,1:T(8,128)(2,1)} %fusion), calls=%async_computation | async-start | bytes 4718592 | tf_op jit(solution)/shard_map/all_to_all | solution.py:343
  26.1 30.0 %copy-start.25 = (bf16[1,1024,512]{2,1,0:T(8,128)(2,1)S(1)}, bf16[1,1024,512]{2,1,0:T(8,128)(2,1)}, u32[]{:S(2)}) copy-start(bf16[1,1024,512]{2,1,0:T(8,128)(2,1)} %param.13) | copy-start | bytes 3145732
  28.9 53.5 %collective-permute-start = (bf16[144,2048]{1,0:T(8,128)(2,1)}, bf16[144,2048]{1,0:T(8,128)(2,1)}, u32[]{:S(2)}, u32[]{:S(2)}) collective-permute-start(bf16[144,2048]{1,0:T(8,128)(2,1)} %get-tuple-element.33), channel_id=1, source_target_pairs={{96,98},{106,108},{116,118},{126,120},{97,99},{107,109},{117,119},... | collective-permute-start | bytes 1769480 | tf_op jit(solution)/shard_map/ppermute | solution.py:337
  30.4 52.1 %collective-permute-start.1 = (bf16[144,2048]{1,0:T(8,128)(2,1)}, bf16[144,2048]{1,0:T(8,128)(2,1)}, u32[]{:S(2)}, u32[]{:S(2)}) collective-permute-start(bf16[144,2048]{1,0:T(8,128)(2,1)} %get-tuple-element.35), channel_id=1, source_target_pairs={{96,100},{106,110},{116,112},{126,122},{97,101},{107,111},{117,113... | collective-permute-start | bytes 1769480 | tf_op jit(solution)/shard_map/ppermute | solution.py:337
  31.8 50.6 %collective-permute-start.2 = (bf16[144,2048]{1,0:T(8,128)(2,1)}, bf16[144,2048]{1,0:T(8,128)(2,1)}, u32[]{:S(2)}, u32[]{:S(2)}) collective-permute-start(bf16[144,2048]{1,0:T(8,128)(2,1)} %get-tuple-element.34), channel_id=1, source_target_pairs={{96,102},{106,104},{116,114},{126,124},{97,103},{107,105},{117,115... | collective-permute-start | bytes 1769480 | tf_op jit(solution)/shard_map/ppermute | solution.py:337
  58.5 3.8 copy-start.28
  58.5 23.9 %copy-start.27 = (s32[8]{0:T(128)S(1)}, s32[8]{0:T(128)}, u32[]{:S(2)}) copy-start(s32[8]{0:T(128)} %param.16) | copy-start | bytes 100
  58.5 26.0 %all-to-all-start.1 = ((bf16[8,144,512]{2,1,0:T(8,128)(2,1)}), bf16[8,144,512]{2,1,0:T(8,128)(2,1)S(1)}, u32[]{:S(2)}, u32[]{:S(2)}) async-start(bf16[8,144,512]{2,1,0:T(8,128)(2,1)} %bitcast.9), calls=%async_computation.1 | async-start | bytes 2359296 | tf_op jit(solution)/shard_map/all_to_all | solution.py:345
  62.3 113.0 %all-gather.13.cloned.1.call-start = ((), (), s32[]{:S(2)}) async-start(), calls=%async_computation.7 | async-start | bytes 3538944 | tf_op jit(solution)/shard_map/all_gather | solution.py:370
  113.6 11.3 %copy-start.4 = (bf16[8,1024,512]{2,1,0:T(8,128)(2,1)S(1)}, bf16[8,1024,512]{2,1,0:T(8,128)(2,1)}, u32[]{:S(2)}) copy-start(bf16[8,1024,512]{2,1,0:T(8,128)(2,1)} %all-gather.9.cloned.1.call-done) | copy-start | bytes 25165828
  123.3 11.0 %collective-permute-start.7 = (bf16[3,64,512]{2,1,0:T(8,128)(2,1)S(1)}, bf16[3,64,512]{2,1,0:T(8,128)(2,1)S(1)}, u32[]{:S(2)}, u32[]{:S(2)}) collective-permute-start(bf16[3,64,512]{2,1,0:T(8,128)(2,1)S(1)} %pad_maximum_fusion.2), channel_id=1, source_target_pairs={{0,2},{2,0},{4,6},{6,4},{1,3},{3,1},{5,7},{7,5},{8,10},{10,8},{12,... | collective-permute-start | bytes 589832 | tf_op jit(solution)/shard_map/ppermute | solution.py:53
  132.2 9.1 %collective-permute-start.9 = (bf16[3,64,512]{2,1,0:T(8,128)(2,1)S(1)}, bf16[3,64,512]{2,1,0:T(8,128)(2,1)S(1)}, u32[]{:S(2)}, u32[]{:S(2)}) collective-permute-start(bf16[3,64,512]{2,1,0:T(8,128)(2,1)S(1)} %pad_maximum_fusion.3), channel_id=1, source_target_pairs={{0,6},{2,4},{4,2},{6,0},{1,7},{3,5},{5,3},{7,1},{8,14},{10,12},{12... | collective-permute-start | bytes 589832 | tf_op jit(solution)/shard_map/ppermute | solution.py:53
  134.4 10.1 %collective-permute-start.8 = (bf16[3,64,512]{2,1,0:T(8,128)(2,1)S(1)}, bf16[3,64,512]{2,1,0:T(8,128)(2,1)S(1)}, u32[]{:S(2)}, u32[]{:S(2)}) collective-permute-start(bf16[3,64,512]{2,1,0:T(8,128)(2,1)S(1)} %add_convert_fusion.11), channel_id=1, source_target_pairs={{0,6},{2,4},{4,2},{6,0},{1,7},{3,5},{5,3},{7,1},{8,14},{10,12},{12... | collective-permute-start | bytes 589832 | tf_op jit(solution)/shard_map/ppermute | solution.py:53
  141.3 5.9 %collective-permute-start.10 = (bf16[3,64,512]{2,1,0:T(8,128)(2,1)S(1)}, bf16[3,64,512]{2,1,0:T(8,128)(2,1)S(1)}, u32[]{:S(2)}, u32[]{:S(2)}) collective-permute-start(bf16[3,64,512]{2,1,0:T(8,128)(2,1)S(1)} %add_convert_fusion.9), channel_id=1, source_target_pairs={{0,2},{2,0},{4,6},{6,4},{1,3},{3,1},{5,7},{7,5},{8,10},{10,8},{12,... | collective-permute-start | bytes 589832 | tf_op jit(solution)/shard_map/ppermute | solution.py:53
  148.1 185.9 %all-gather.11.cloned.1.call-start = ((), (), s32[]{:S(2)}) async-start(), calls=%async_computation.6 | async-start | bytes 1327104 | tf_op jit(solution)/shard_map/all_gather | solution.py:352
  148.2 3.4 copy-start.2
  153.3 8.0 %collective-permute-start.5 = (bf16[144,1024]{1,0:T(8,128)(2,1)S(1)}, bf16[144,1024]{1,0:T(8,128)(2,1)S(1)}, u32[]{:S(2)}, u32[]{:S(2)}) collective-permute-start(bf16[144,1024]{1,0:T(8,128)(2,1)S(1)} %shard_map.131), channel_id=1, source_target_pairs={{0,6},{2,4},{4,2},{6,0},{1,7},{3,5},{5,3},{7,1},{8,14},{10,12},{12... | collective-permute-start | bytes 884744 | tf_op jit(solution)/shard_map/ppermute | solution.py:53
  157.1 9.3 %collective-permute-start.3 = (bf16[144,1024]{1,0:T(8,128)(2,1)S(1)}, bf16[144,1024]{1,0:T(8,128)(2,1)S(1)}, u32[]{:S(2)}, u32[]{:S(2)}) collective-permute-start(bf16[144,1024]{1,0:T(8,128)(2,1)S(1)} %shard_map.130), channel_id=1, source_target_pairs={{0,2},{2,0},{4,6},{6,4},{1,3},{3,1},{5,7},{7,5},{8,10},{10,8},{12,... | collective-permute-start | bytes 884744 | tf_op jit(solution)/shard_map/ppermute | solution.py:53
  161.4 8.3 %collective-permute-start.6 = (bf16[144,1024]{1,0:T(8,128)(2,1)S(1)}, bf16[144,1024]{1,0:T(8,128)(2,1)S(1)}, u32[]{:S(2)}, u32[]{:S(2)}) collective-permute-start(bf16[144,1024]{1,0:T(8,128)(2,1)S(1)} %add_convert_fusion.6.high), channel_id=1, source_target_pairs={{0,2},{2,0},{4,6},{6,4},{1,3},{3,1},{5,7},{7,5},{8,10},{10,8},{12,... | collective-permute-start | bytes 884744 | tf_op jit(solution)/shard_map/ppermute | solution.py:53
  166.6 8.0 %collective-permute-start.4 = (bf16[144,1024]{1,0:T(8,128)(2,1)S(1)}, bf16[144,1024]{1,0:T(8,128)(2,1)S(1)}, u32[]{:S(2)}, u32[]{:S(2)}) collective-permute-start(bf16[144,1024]{1,0:T(8,128)(2,1)S(1)} %add_convert_fusion.7.low), channel_id=1, source_target_pairs={{0,6},{2,4},{4,2},{6,0},{1,7},{3,5},{5,3},{7,1},{8,14},{10,12},{12... | collective-permute-start | bytes 884744 | tf_op jit(solution)/shard_map/ppermute | solution.py:53
  185.8 22.5 %copy-start.18 = (bf16[4,144,512]{2,1,0:T(8,128)(2,1)}, bf16[4,144,512]{2,1,0:T(8,128)(2,1)S(1)}, u32[]{:S(2)}) copy-start(bf16[4,144,512]{2,1,0:T(8,128)(2,1)S(1)} %get-tuple-element.18) | copy-start | bytes 1769476
  185.8 17.4 %collective-permute-start.11 = (bf16[144,2048]{1,0:T(8,128)(2,1)S(1)}, bf16[144,2048]{1,0:T(8,128)(2,1)S(1)}, u32[]{:S(2)}, u32[]{:S(2)}) collective-permute-start(bf16[144,2048]{1,0:T(8,128)(2,1)S(1)} %get-tuple-element.19), channel_id=1, source_target_pairs={{32,0},{64,32},{96,64},{33,1},{65,33},{97,65},{34,2},{66,34},{98,6... | collective-permute-start | bytes 1769480 | tf_op jit(solution)/shard_map/ppermute | solution.py:379
  208.3 9.6 %collective-permute-start.14 = (bf16[144,1024]{1,0:T(8,128)(2,1)S(1)}, bf16[144,1024]{1,0:T(8,128)(2,1)S(1)}, u32[]{:S(2)}, u32[]{:S(2)}) collective-permute-start(bf16[144,1024]{1,0:T(8,128)(2,1)S(1)} %shard_map.134), channel_id=1, source_target_pairs={{0,6},{2,4},{4,2},{6,0},{1,7},{3,5},{5,3},{7,1},{8,14},{10,12},{12... | collective-permute-start | bytes 884744 | tf_op jit(solution)/shard_map/ppermute | solution.py:53
  211.1 19.6 %copy-start.9 = (bf16[48,64,512]{2,1,0:T(8,128)(2,1)S(1)}, bf16[48,64,512]{2,1,0:T(8,128)(2,1)}, u32[]{:S(2)}) copy-start(bf16[48,64,512]{2,1,0:T(8,128)(2,1)} %all-gather.13.cloned.1.call-done) | copy-start | bytes 9437188
  211.1 40.8 %slice-start = ((s8[8388608]{0:T(1024)(128)(4,1)}), s8[4194304]{0:T(1024)(128)(4,1)S(1)}, s32[]{:S(2)}) async-start(s8[8388608]{0:T(1024)(128)(4,1)} %bitcast.102), calls=%async_computation.8 | async-start | bytes 8388608
  212.8 9.8 %collective-permute-start.12 = (bf16[144,1024]{1,0:T(8,128)(2,1)S(1)}, bf16[144,1024]{1,0:T(8,128)(2,1)S(1)}, u32[]{:S(2)}, u32[]{:S(2)}) collective-permute-start(bf16[144,1024]{1,0:T(8,128)(2,1)S(1)} %shard_map.133), channel_id=1, source_target_pairs={{0,2},{2,0},{4,6},{6,4},{1,3},{3,1},{5,7},{7,5},{8,10},{10,8},{12,... | collective-permute-start | bytes 884744 | tf_op jit(solution)/shard_map/ppermute | solution.py:53
  218.0 9.2 %collective-permute-start.15 = (bf16[144,1024]{1,0:T(8,128)(2,1)S(1)}, bf16[144,1024]{1,0:T(8,128)(2,1)S(1)}, u32[]{:S(2)}, u32[]{:S(2)}) collective-permute-start(bf16[144,1024]{1,0:T(8,128)(2,1)S(1)} %add_convert_fusion.4.high), channel_id=1, source_target_pairs={{0,2},{2,0},{4,6},{6,4},{1,3},{3,1},{5,7},{7,5},{8,10},{10,8},{12,... | collective-permute-start | bytes 884744 | tf_op jit(solution)/shard_map/ppermute | solution.py:53
  222.7 29.2 %slice-start.1 = ((s8[8388608]{0:T(1024)(128)(4,1)}), s8[4194304]{0:T(1024)(128)(4,1)S(1)}, s32[]{:S(2)}) async-start(s8[8388608]{0:T(1024)(128)(4,1)} %bitcast.102), calls=%async_computation.9 | async-start | bytes 8388608
  222.7 8.0 %collective-permute-start.13 = (bf16[144,1024]{1,0:T(8,128)(2,1)S(1)}, bf16[144,1024]{1,0:T(8,128)(2,1)S(1)}, u32[]{:S(2)}, u32[]{:S(2)}) collective-permute-start(bf16[144,1024]{1,0:T(8,128)(2,1)S(1)} %add_convert_fusion.5.low), channel_id=1, source_target_pairs={{0,6},{2,4},{4,2},{6,0},{1,7},{3,5},{5,3},{7,1},{8,14},{10,12},{12... | collective-permute-start | bytes 884744 | tf_op jit(solution)/shard_map/ppermute | solution.py:53
  239.3 14.3 %copy-start.20 = (bf16[4,144,512]{2,1,0:T(8,128)(2,1)}, bf16[4,144,512]{2,1,0:T(8,128)(2,1)S(1)}, u32[]{:S(2)}) copy-start(bf16[4,144,512]{2,1,0:T(8,128)(2,1)S(1)} %get-tuple-element.20) | copy-start | bytes 1769476
  239.3 12.5 %collective-permute-start.16 = (bf16[144,2048]{1,0:T(8,128)(2,1)S(1)}, bf16[144,2048]{1,0:T(8,128)(2,1)S(1)}, u32[]{:S(2)}, u32[]{:S(2)}) collective-permute-start(bf16[144,2048]{1,0:T(8,128)(2,1)S(1)} %get-tuple-element.21), channel_id=1, source_target_pairs={{32,0},{64,32},{96,64},{33,1},{65,33},{97,65},{34,2},{66,34},{98,6... | collective-permute-start | bytes 1769480 | tf_op jit(solution)/shard_map/ppermute | solution.py:379
  251.8 20.3 %copy-start.11 = (bf16[144,2048]{1,0:T(8,128)(2,1)}, bf16[144,2048]{1,0:T(8,128)(2,1)S(1)}, u32[]{:S(2)}) copy-start(bf16[144,2048]{1,0:T(8,128)(2,1)S(1)} %collective-permute-done.16.g_ref) | copy-start | bytes 1769476
  253.6 9.2 %collective-permute-start.19 = (bf16[144,1024]{1,0:T(8,128)(2,1)S(1)}, bf16[144,1024]{1,0:T(8,128)(2,1)S(1)}, u32[]{:S(2)}, u32[]{:S(2)}) collective-permute-start(bf16[144,1024]{1,0:T(8,128)(2,1)S(1)} %shard_map.137), channel_id=1, source_target_pairs={{0,6},{2,4},{4,2},{6,0},{1,7},{3,5},{5,3},{7,1},{8,14},{10,12},{12... | collective-permute-start | bytes 884744 | tf_op jit(solution)/shard_map/ppermute | solution.py:53
  256.0 8.0 %collective-permute-start.17 = (bf16[144,1024]{1,0:T(8,128)(2,1)S(1)}, bf16[144,1024]{1,0:T(8,128)(2,1)S(1)}, u32[]{:S(2)}, u32[]{:S(2)}) collective-permute-start(bf16[144,1024]{1,0:T(8,128)(2,1)S(1)} %shard_map.136), channel_id=1, source_target_pairs={{0,2},{2,0},{4,6},{6,4},{1,3},{3,1},{5,7},{7,5},{8,10},{10,8},{12,... | collective-permute-start | bytes 884744 | tf_op jit(solution)/shard_map/ppermute | solution.py:53
  262.9 6.8 %collective-permute-start.20 = (bf16[144,1024]{1,0:T(8,128)(2,1)S(1)}, bf16[144,1024]{1,0:T(8,128)(2,1)S(1)}, u32[]{:S(2)}, u32[]{:S(2)}) collective-permute-start(bf16[144,1024]{1,0:T(8,128)(2,1)S(1)} %add_convert_fusion.2.high), channel_id=1, source_target_pairs={{0,2},{2,0},{4,6},{6,4},{1,3},{3,1},{5,7},{7,5},{8,10},{10,8},{12,... | collective-permute-start | bytes 884744 | tf_op jit(solution)/shard_map/ppermute | solution.py:53
  264.1 8.0 %collective-permute-start.18 = (bf16[144,1024]{1,0:T(8,128)(2,1)S(1)}, bf16[144,1024]{1,0:T(8,128)(2,1)S(1)}, u32[]{:S(2)}, u32[]{:S(2)}) collective-permute-start(bf16[144,1024]{1,0:T(8,128)(2,1)S(1)} %add_convert_fusion.3.low), channel_id=1, source_target_pairs={{0,6},{2,4},{4,2},{6,0},{1,7},{3,5},{5,3},{7,1},{8,14},{10,12},{12... | collective-permute-start | bytes 884744 | tf_op jit(solution)/shard_map/ppermute | solution.py:53
  278.2 11.8 %collective-permute-start.21 = (bf16[144,2048]{1,0:T(8,128)(2,1)S(1)}, bf16[144,2048]{1,0:T(8,128)(2,1)S(1)}, u32[]{:S(2)}, u32[]{:S(2)}) collective-permute-start(bf16[144,2048]{1,0:T(8,128)(2,1)S(1)} %get-tuple-element.23), channel_id=1, source_target_pairs={{32,0},{64,32},{96,64},{33,1},{65,33},{97,65},{34,2},{66,34},{98,6... | collective-permute-start | bytes 1769480 | tf_op jit(solution)/shard_map/ppermute | solution.py:379
  291.7 9.9 %collective-permute-start.24 = (bf16[144,1024]{1,0:T(8,128)(2,1)S(1)}, bf16[144,1024]{1,0:T(8,128)(2,1)S(1)}, u32[]{:S(2)}, u32[]{:S(2)}) collective-permute-start(bf16[144,1024]{1,0:T(8,128)(2,1)S(1)} %shard_map.140), channel_id=1, source_target_pairs={{0,6},{2,4},{4,2},{6,0},{1,7},{3,5},{5,3},{7,1},{8,14},{10,12},{12... | collective-permute-start | bytes 884744 | tf_op jit(solution)/shard_map/ppermute | solution.py:53
  295.1 6.8 %collective-permute-start.22 = (bf16[144,1024]{1,0:T(8,128)(2,1)S(1)}, bf16[144,1024]{1,0:T(8,128)(2,1)S(1)}, u32[]{:S(2)}, u32[]{:S(2)}) collective-permute-start(bf16[144,1024]{1,0:T(8,128)(2,1)S(1)} %shard_map.139), channel_id=1, source_target_pairs={{0,2},{2,0},{4,6},{6,4},{1,3},{3,1},{5,7},{7,5},{8,10},{10,8},{12,... | collective-permute-start | bytes 884744 | tf_op jit(solution)/shard_map/ppermute | solution.py:53
  301.6 6.8 %collective-permute-start.25 = (bf16[144,1024]{1,0:T(8,128)(2,1)S(1)}, bf16[144,1024]{1,0:T(8,128)(2,1)S(1)}, u32[]{:S(2)}, u32[]{:S(2)}) collective-permute-start(bf16[144,1024]{1,0:T(8,128)(2,1)S(1)} %add_convert_fusion.high), channel_id=1, source_target_pairs={{0,2},{2,0},{4,6},{6,4},{1,3},{3,1},{5,7},{7,5},{8,10},{10,8},{12,... | collective-permute-start | bytes 884744 | tf_op jit(solution)/shard_map/ppermute | solution.py:53
  302.0 8.0 %collective-permute-start.23 = (bf16[144,1024]{1,0:T(8,128)(2,1)S(1)}, bf16[144,1024]{1,0:T(8,128)(2,1)S(1)}, u32[]{:S(2)}, u32[]{:S(2)}) collective-permute-start(bf16[144,1024]{1,0:T(8,128)(2,1)S(1)} %add_convert_fusion.1.low), channel_id=1, source_target_pairs={{0,6},{2,4},{4,2},{6,0},{1,7},{3,5},{5,3},{7,1},{8,14},{10,12},{12... | collective-permute-start | bytes 884744 | tf_op jit(solution)/shard_map/ppermute | solution.py:53
  313.2 4.6 %copy-start.12 = (bf16[144,2048]{1,0:T(8,128)(2,1)S(1)}, bf16[144,2048]{1,0:T(8,128)(2,1)}, u32[]{:S(2)}) copy-start(bf16[144,2048]{1,0:T(8,128)(2,1)} %copy-done.11) | copy-start | bytes 1769476
  314.3 12.2 %all-to-all-start.2 = ((bf16[4,144,512]{2,1,0:T(8,128)(2,1)}), bf16[4,144,512]{2,1,0:T(8,128)(2,1)S(1)}, u32[]{:S(2)}, u32[]{:S(2)}) async-start(bf16[4,144,512]{2,1,0:T(8,128)(2,1)} %add_add_fusion.1.b_ref), calls=%async_computation.2 | async-start | bytes 1179648 | tf_op jit(solution)/shard_map/all_to_all | solution.py:390
  317.9 3.5 copy-start.7
  326.5 34.9 %all-to-all-start.3 = ((bf16[8,144,1024]{2,1,0:T(8,128)(2,1)}), bf16[8,144,1024]{2,1,0:T(8,128)(2,1)}, u32[]{:S(2)}, u32[]{:S(2)}) async-start(bf16[8,144,1024]{2,1,0:T(8,128)(2,1)} %bitcast.37), calls=%async_computation.3 | async-start | bytes 4718592 | tf_op jit(solution)/shard_map/all_to_all | solution.py:386
  331.3 2.4 collective-permute-start.26
  333.8 27.6 %copy-start.15 = (bf16[144,8,1024]{2,0,1:T(8,128)(2,1)S(1)}, bf16[144,8,1024]{2,0,1:T(8,128)(2,1)}, u32[]{:S(2)}) copy-start(bf16[144,8,1024]{2,0,1:T(8,128)(2,1)} %copy-done.14) | copy-start | bytes 7077892
  362.6 33.6 %copy-start.13 = (f32[1,1024,1024]{2,1,0:T(8,128)S(1)}, f32[1,1024,1024]{2,1,0:T(8,128)}, u32[]{:S(2)}) copy-start(f32[1,1024,1024]{2,1,0:T(8,128)} %master_ref.1) | copy-start | bytes 12582916
  362.6 33.7 %copy-start.16 = (bf16[1,1024,1024]{2,1,0:T(8,128)(2,1)S(1)}, bf16[1,1024,1024]{2,1,0:T(8,128)(2,1)}, u32[]{:S(2)}) copy-start(bf16[1,1024,1024]{2,1,0:T(8,128)(2,1)} %one_ref.1) | copy-start | bytes 6291460
  362.6 33.7 %copy-start.17 = (bf16[1,1024,1024]{2,1,0:T(8,128)(2,1)S(1)}, bf16[1,1024,1024]{2,1,0:T(8,128)(2,1)}, u32[]{:S(2)}) copy-start(bf16[1,1024,1024]{2,1,0:T(8,128)(2,1)} %two_ref.1) | copy-start | bytes 6291460
  368.7 1.2 collective-permute-start.27
  370.0 4.8 %collective-permute-start.28 = (f32[8,128]{1,0:T(8,128)S(1)}, f32[8,128]{1,0:T(8,128)S(1)}, u32[]{:S(2)}, u32[]{:S(2)}) collective-permute-start(f32[8,128]{1,0:T(8,128)S(1)} %add.216), channel_id=1, source_target_pairs={{0,2},{2,4},{4,6},{6,0},{1,3},{3,5},{5,7},{7,1},{8,10},{10,12},{12... | collective-permute-start | bytes 12296 | tf_op jit(solution)/shard_map/ppermute | solution.py:58
  370.5 4.3 %collective-permute-start.29 = (f32[8,128]{1,0:T(8,128)S(1)}, f32[8,128]{1,0:T(8,128)S(1)}, u32[]{:S(2)}, u32[]{:S(2)}) collective-permute-start(f32[8,128]{1,0:T(8,128)S(1)} %add.216), channel_id=1, source_target_pairs={{0,6},{2,0},{4,2},{6,4},{1,7},{3,1},{5,3},{7,5},{8,14},{10,8},{12,... | collective-permute-start | bytes 12296 | tf_op jit(solution)/shard_map/ppermute | solution.py:58
  373.2 5.1 %collective-permute-start.30 = (f32[8,128]{1,0:T(8,128)S(1)}, f32[8,128]{1,0:T(8,128)S(1)}, u32[]{:S(2)}, u32[]{:S(2)}) collective-permute-start(f32[8,128]{1,0:T(8,128)S(1)} %add.216), channel_id=1, source_target_pairs={{0,4},{2,6},{4,0},{6,2},{1,5},{3,7},{5,1},{7,3},{8,12},{10,14},{12... | collective-permute-start | bytes 12296 | tf_op jit(solution)/shard_map/ppermute | solution.py:58
  378.3 4.8 %collective-permute-start.31 = (f32[8,128]{1,0:T(8,128)S(1)}, f32[8,128]{1,0:T(8,128)S(1)}, u32[]{:S(2)}, u32[]{:S(2)}) collective-permute-start(f32[8,128]{1,0:T(8,128)S(1)} %add_add_fusion.5), channel_id=1, source_target_pairs={{0,8},{8,16},{16,24},{24,0},{1,9},{9,17},{17,25},{25,1},{2,10},{10... | collective-permute-start | bytes 12296 | tf_op jit(solution)/shard_map/ppermute | solution.py:58
  378.9 4.3 %collective-permute-start.32 = (f32[8,128]{1,0:T(8,128)S(1)}, f32[8,128]{1,0:T(8,128)S(1)}, u32[]{:S(2)}, u32[]{:S(2)}) collective-permute-start(f32[8,128]{1,0:T(8,128)S(1)} %add_add_fusion.5), channel_id=1, source_target_pairs={{0,24},{8,0},{16,8},{24,16},{1,25},{9,1},{17,9},{25,17},{2,26},{10... | collective-permute-start | bytes 12296 | tf_op jit(solution)/shard_map/ppermute | solution.py:58
  381.6 5.1 %collective-permute-start.33 = (f32[8,128]{1,0:T(8,128)S(1)}, f32[8,128]{1,0:T(8,128)S(1)}, u32[]{:S(2)}, u32[]{:S(2)}) collective-permute-start(f32[8,128]{1,0:T(8,128)S(1)} %add_add_fusion.5), channel_id=1, source_target_pairs={{0,16},{8,24},{16,0},{24,8},{1,17},{9,25},{17,1},{25,9},{2,18},{10... | collective-permute-start | bytes 12296 | tf_op jit(solution)/shard_map/ppermute | solution.py:58
  386.7 5.9 %collective-permute-start.34 = (f32[8,128]{1,0:T(8,128)S(1)}, f32[8,128]{1,0:T(8,128)S(1)}, u32[]{:S(2)}, u32[]{:S(2)}) collective-permute-start(f32[8,128]{1,0:T(8,128)S(1)} %add_add_fusion.4), channel_id=1, source_target_pairs={{0,32},{32,64},{64,96},{96,0},{1,33},{33,65},{65,97},{97,1},{2,34}... | collective-permute-start | bytes 12296 | tf_op jit(solution)/shard_map/ppermute | solution.py:58
  388.3 4.3 %collective-permute-start.35 = (f32[8,128]{1,0:T(8,128)S(1)}, f32[8,128]{1,0:T(8,128)S(1)}, u32[]{:S(2)}, u32[]{:S(2)}) collective-permute-start(f32[8,128]{1,0:T(8,128)S(1)} %add_add_fusion.4), channel_id=1, source_target_pairs={{0,96},{32,0},{64,32},{96,64},{1,97},{33,1},{65,33},{97,65},{2,98}... | collective-permute-start | bytes 12296 | tf_op jit(solution)/shard_map/ppermute | solution.py:58
  389.9 5.1 %collective-permute-start.36 = (f32[8,128]{1,0:T(8,128)S(1)}, f32[8,128]{1,0:T(8,128)S(1)}, u32[]{:S(2)}, u32[]{:S(2)}) collective-permute-start(f32[8,128]{1,0:T(8,128)S(1)} %add_add_fusion.4), channel_id=1, source_target_pairs={{0,64},{32,96},{64,0},{96,32},{1,65},{33,97},{65,1},{97,33},{2,66}... | collective-permute-start | bytes 12296 | tf_op jit(solution)/shard_map/ppermute | solution.py:58
  396.3 6.3 %copy-start.1 = (bf16[1,3,48,8192]{3,2,1,0:T(8,128)(2,1)S(1)}, bf16[1,3,48,8192]{3,2,1,0:T(8,128)(2,1)}, u32[]{:S(2)}) copy-start(bf16[1,3,48,8192]{3,2,1,0:T(8,128)(2,1)} %param.11) | copy-start | bytes 7077892
  (12 other events, 25.7 us)
Sparse Core Ops, SparseCore 0:
  9.7 52.1 all-gather.6
  63.7 49.8 all-gather.8
  148.2 27.0 all-gather.12
  304.4 22.2 all-gather.10

commit v3 on v2

--- a/solution.py
+++ b/solution.py
@@ -20,8 +20,8 @@
 PLANE = ("y", "core")
 
 
-VMEM_LIMIT = 40 * 1024 * 1024
-PAIRS = ((0, 1), (0, 2), (0, 3), (1, 2), (1, 3), (2, 3))
+VMEM_LIMIT = 18 * 1024 * 1024
+PAIRS = ((0, 1), (0, 2), (1, 2), (0, 3), (1, 3), (2, 3))
 
 
 def dot(left, right, dims):
@@ -56,6 +56,78 @@
 def turn_by(value, axis, steps):
     count = lax.axis_size(axis)
     return lax.ppermute(value, axis, [(i, (i + steps) % count) for i in range(count)])
+
+
+def pack(own_value, own_output):
+    share, head_size = own_value.shape
+    blocks = share // head_size
+
+    def kernel(v_ref, o_ref, out_ref):
+        at = pl.program_id(0)
+
+        @pl.when(at < blocks)
+        def _():
+            out_ref[0] = v_ref[...]
+
+        @pl.when(at >= blocks)
+        def _():
+            out_ref[0] = o_ref[...]
+
+    return call(
+        kernel,
+        (2 * blocks,),
+        [
+            pl.BlockSpec((head_size, head_size), lambda i: (jnp.minimum(i, blocks - 1), 0)),
+            pl.BlockSpec((head_size, head_size), lambda i: (0, jnp.maximum(i - blocks, 0))),
+        ],
+        pl.BlockSpec((1, head_size, head_size), lambda i: (i, 0, 0)),
+        jax.ShapeDtypeStruct((2 * blocks, head_size, head_size), jnp.bfloat16),
+        cost=pl.CostEstimate(
+            flops=0, bytes_accessed=8 * share * head_size, transcendentals=0
+        ),
+    )(own_value, own_output)
+
+
+def link_parts(stack, place):
+    columns, cores, double, head_size, _ = stack.shape
+    blocks = double // 2
+    eighth = head_size // (columns * cores)
+    total = len(PAIRS)
+    table = jnp.array([pair[0] for pair in PAIRS] + [pair[1] for pair in PAIRS], jnp.int32)
+    table = jnp.concatenate([table, place[None].astype(jnp.int32)])
+
+    def kernel(table_ref, o_ref, v_ref, out_ref):
+        part = 0.0
+        for side in range(cores):
+            for k in range(blocks):
+                part = part + dot(o_ref[0, side, k], v_ref[0, side, k], ((1,), (0,)))
+        out_ref[0] = part.astype(jnp.bfloat16)
+
+    return pl.pallas_call(
+        kernel,
+        grid_spec=pltpu.PrefetchScalarGridSpec(
+            num_scalar_prefetch=1,
+            grid=(total,),
+            in_specs=[
+                pl.BlockSpec(
+                    (1, cores, blocks, eighth, head_size),
+                    lambda i, table: (table[i], 0, 1, table[2 * total], 0),
+                ),
+                pl.BlockSpec(
+                    (1, cores, blocks, head_size, head_size),
+                    lambda i, table: (table[total + i], 0, 0, 0, 0),
+                ),
+            ],
+            out_specs=pl.BlockSpec((1, eighth, head_size), lambda i, table: (i, 0, 0)),
+        ),
+        out_shape=jax.ShapeDtypeStruct((total, eighth, head_size), jnp.bfloat16),
+        cost_estimate=pl.CostEstimate(
+            flops=4 * total * eighth * blocks * head_size * head_size,
+            bytes_accessed=12 * blocks * head_size * head_size,
+            transcendentals=0,
+        ),
+        compiler_params=pltpu.CompilerParams(vmem_limit_bytes=VMEM_LIMIT),
+    )(table, stack, stack)
 
 
 def addends_over_x(parts, masks=((1, 3), (3, 1))):
@@ -78,12 +150,17 @@
     return value
 
 
-def project(gradient, weights, first):
+def project(gradient, stack, first):
     rows, chip_width = gradient.shape
-    _, head_size, share = weights.shape
+    columns, cores, double, head_size, _ = stack.shape
+    blocks = double // 2
 
     def kernel(g_ref, w_ref, out_ref):
-        part = dot_nt(g_ref[:, :share], w_ref[0]) + dot_nt(g_ref[:, share:], w_ref[1])
+        part = 0.0
+        for side in range(cores):
+            for k in range(blocks):
+                start = (side * blocks + k) * head_size
+                part = part + dot_nt(g_ref[:, start : start + head_size], w_ref[0, side, k])
         out_ref[...] = part.astype(jnp.bfloat16)
 
     return call(
@@ -91,7 +168,9 @@
         (2,),
         [
             whole((rows, chip_width)),
-            pl.BlockSpec((2, head_size, share), lambda i: (first + i, 0, 0)),
+            pl.BlockSpec(
+                (1, cores, blocks, head_size, head_size), lambda i: (first + i, 0, 1, 0, 0)
+            ),
         ],
         pl.BlockSpec((rows, head_size), lambda i: (0, i)),
         jax.ShapeDtypeStruct((rows, 2 * head_size), jnp.bfloat16),
@@ -100,7 +179,7 @@
             bytes_accessed=4 * chip_width * head_size,
             transcendentals=0,
         ),
-    )(gradient, weights)
+    )(gradient, stack)
 
 
 def solve(addends, links, b_ref):
@@ -122,10 +201,10 @@
 
 def advance(gradient, addends, links, weights):
     rows, chip_width = gradient.shape
-    count, share, head_size = weights.shape
-    steps = 4
-    block = chip_width // steps
-    weights = weights.reshape(4, steps, block, head_size)
+    _, cores, double, head_size, _ = weights.shape
+    blocks = double // 2
+    steps = cores * blocks
+    block = head_size
     flat = [array for pair in addends for array in pair]
 
     def kernel(g_ref, low, low_got, high, high_got, m_ref, w_ref, b_ref, out_ref):
@@ -135,7 +214,7 @@
 
         total = g_ref[...].astype(jnp.float32)
         for at in range(4):
-            total = total + dot_nt(b_ref[at], w_ref[at, 0])
+            total = total + dot_nt(b_ref[at], w_ref[at, 0, 0])
         out_ref[...] = total.astype(jnp.bfloat16)
 
     return call(
@@ -145,7 +224,9 @@
         + [whole((rows, 2 * head_size))] * 4
         + [
             whole(links.shape),
-            pl.BlockSpec((4, 1, block, head_size), lambda i: (0, i, 0, 0)),
+            pl.BlockSpec(
+                (4, 1, 1, block, head_size), lambda i: (0, i // blocks, i % blocks, 0, 0)
+            ),
         ],
         [
             whole((4, rows, head_size)),
@@ -187,30 +268,42 @@
 
 def rebuild(gradient, backs, weights):
     rows, chip_width = gradient.shape
-    count, share, head_size = weights.shape
-    steps = 4
-    block = chip_width // steps
-    weights = weights.reshape(4, steps, block, head_size)
+    _, cores, double, head_size, _ = weights.shape
+    blocks = double // 2
 
     def kernel(g_ref, b_ref, w_ref, out_ref):
-        total = g_ref[...]
-        out_ref[3, 0] = total
-        for at in (3, 2, 1):
-            total = (total.astype(jnp.float32) + dot_nt(b_ref[at], w_ref[at, 0])).astype(
-                jnp.bfloat16
-            )
-            out_ref[at - 1, 0] = total
-
-    return call(
-        kernel,
-        (steps,),
-        [
-            pl.BlockSpec((rows, block), lambda i: (0, i)),
+        at_block = pl.program_id(1)
+
+        @pl.when(at_block < blocks)
+        def _():
+            total = g_ref[...]
+            out_ref[3, 0] = total
+            for at in (3, 2, 1):
+                total = (total.astype(jnp.float32) + dot_nt(b_ref[at], w_ref[at, 0, 0])).astype(
+                    jnp.bfloat16
+                )
+                out_ref[at - 1, 0] = total
+
+        @pl.when(at_block == blocks)
+        def _():
+            for at in range(4):
+                out_ref[at, 0] = b_ref[at]
+
+    def inner(k):
+        return jnp.minimum(k, blocks - 1)
+
+    return call(
+        kernel,
+        (cores, blocks + 1),
+        [
+            pl.BlockSpec((rows, head_size), lambda i, k: (0, i * blocks + inner(k))),
             whole((4, rows, head_size)),
-            pl.BlockSpec((4, 1, block, head_size), lambda i: (0, i, 0, 0)),
-        ],
-        pl.BlockSpec((4, 1, rows, block), lambda i: (0, i // 2, 0, i % 2)),
-        jax.ShapeDtypeStruct((4, 2, rows, share), jnp.bfloat16),
+            pl.BlockSpec(
+                (4, 1, 1, head_size, head_size), lambda i, k: (0, i, inner(k), 0, 0)
+            ),
+        ],
+        pl.BlockSpec((4, 1, rows, head_size), lambda i, k: (0, i, 0, k)),
+        jax.ShapeDtypeStruct((4, cores, rows, chip_width // cores + head_size), jnp.bfloat16),
         cost=pl.CostEstimate(
             flops=6 * rows * head_size * chip_width,
             bytes_accessed=8 * chip_width * head_size,
@@ -219,9 +312,9 @@
     )(gradient, backs, weights)
 
 
-def averaged(picked, back, gradient, hidden, contributors):
+def averaged(picked, got, hidden, contributors):
     rows, share = picked.shape
-    head_size = back.shape[1]
+    head_size = hidden.shape[1]
     steps = 4
     block = share // steps
 
@@ -244,7 +337,7 @@
         [
             pl.BlockSpec(memory_space=pltpu.SMEM),
             pl.BlockSpec((rows, block), lambda i: (0, i)),
-            whole((rows, head_size)),
+            pl.BlockSpec((rows, head_size), lambda i: (0, share // head_size)),
             pl.BlockSpec((rows, block), lambda i: (0, i)),
             whole((rows, head_size)),
         ],
@@ -261,7 +354,7 @@
             bytes_accessed=4 * rows * (share + head_size) + 8 * share * head_size,
             transcendentals=0,
         ),
-    )(contributors, picked, back, gradient, hidden)
+    )(contributors, picked, got, got, hidden)
 
 
 def update(factor, grads, master, moment_one, moment_two):
@@ -318,49 +411,38 @@
     rows = micro * tok_rows
     chip_width = 2 * share
 
-    output_weight = lax.all_gather(own_output, PLANE, axis=0)
-    value_weight = lax.all_gather(own_value, PLANE, axis=0)
-    flag_row = lax.all_gather(flags[0, 0], DP)
+    bundle = pack(own_value, own_output)
+    stack = lax.all_gather(bundle, PLANE, axis=0).reshape((columns, 2) + bundle.shape)
 
     top = out_grad.reshape(rows, width)
-    own_slice = lax.dynamic_slice(top, (0, x * chip_width), (rows, chip_width))
-    gradient = jnp.where(
-        jnp.logical_and(z == planes - 1, x == y), own_slice, jnp.zeros_like(own_slice)
-    )
-    for turn in range(1, across):
-        other = lax.rem(x + turn, across)
-        piece = lax.dynamic_slice(top, (0, other * chip_width), (rows, chip_width))
-        base = (planes - 1) * columns * across
-        pairs = [
-            (base + i * across + i, base + i * across + (i + turn) % across) for i in range(columns)
-        ]
-        gradient = gradient + lax.ppermute(piece, ("z", "y", "x"), pairs)
-
-    keep = alive * (1 - flag_row)
+    piece = lax.dynamic_slice(top, (0, z * chip_width), (rows, chip_width))
+    base = (planes - 1) * columns * across
+    pairs = [
+        ((j * columns + i) * across + i, base + i * across + j)
+        for i in range(columns)
+        for j in range(across)
+    ]
+    gradient = lax.ppermute(piece, ("z", "y", "x"), pairs)
+
     replica = lax.axis_index(DP)
-    own_keep = (alive[replica] * (1 - flags[0, 0])).astype(jnp.bfloat16)
-    picked = jnp.take(acts[0], order[0], axis=0).reshape(rows, width) * own_keep
+    keep = (alive[replica] * (1 - flags[0, 0])).astype(jnp.float32)
+    count = jnp.full((8, 128), keep)
+    count = count + swap(count, "core", 1)
+    count = count + sum(turn_by(count, "x", steps) for steps in range(1, across))
+    picked = jnp.take(acts[0], order[0], axis=0).reshape(rows, width) * keep.astype(jnp.bfloat16)
     picked = lax.all_to_all(picked, DP, split_axis=1, concat_axis=0, tiled=True)
+
     hidden_part = dot(picked, own_value, ((1,), (0,))).astype(jnp.bfloat16)
     hidden_part = lax.all_to_all(
         hidden_part.reshape(replicas, rows, head_size), DP, split_axis=0, concat_axis=0, tiled=True
     )
+
     hidden = jnp.sum(hidden_part.astype(jnp.float32), axis=0).astype(jnp.bfloat16)
-    output_weight, hidden, gradient, keep = lax.optimization_barrier(
-        (output_weight, hidden, gradient, keep)
-    )
+    stack, hidden, gradient, count = lax.optimization_barrier((stack, hidden, gradient, count))
     hidden = lax.all_gather(hidden, DP, axis=0, tiled=True)
 
-    eighth = head_size // replicas
-    at_row = lax.axis_index(PLANE) * eighth
-    link = []
-    for at, other in PAIRS:
-        total = 0.0
-        for half in range(2):
-            left = lax.dynamic_slice(output_weight[2 * at + half], (at_row, 0), (eighth, share))
-            total = total + dot(left, value_weight[2 * other + half], ((1,), (0,)))
-        link.append(total.astype(jnp.bfloat16))
-    (low, low_got), (high, high_got) = addends_over_x((jnp.stack(link[:3]), jnp.stack(link[3:])))
+    link = link_parts(stack, lax.axis_index(PLANE))
+    (low, low_got), (high, high_got) = addends_over_x((link[:3], link[3:]))
     link = jnp.concatenate(
         [
             (low.astype(jnp.float32) + low_got.astype(jnp.float32)).astype(jnp.bfloat16),
@@ -371,30 +453,24 @@
 
     kept_gradient, kept_back = gradient, None
     for turn in range(planes):
-        high = project(gradient, output_weight, 2)
-        low = project(gradient, output_weight, 0)
+        high = project(gradient, stack, 2)
+        low = project(gradient, stack, 0)
         addends = addends_over_x((low, high))
         if turn < planes - 1:
-            backs, gradient = advance(gradient, addends, links, value_weight)
+            backs, gradient = advance(gradient, addends, links, stack)
             gradient = lax.ppermute(gradient, "z", [(i, i - 1) for i in range(1, planes)])
             kept_gradient = kept_gradient + gradient
         else:
             backs = solve_last(addends, links)
         kept_back = backs if kept_back is None else kept_back + backs
 
-    sent = rebuild(kept_gradient, kept_back, value_weight)
-    grad_rows = lax.all_to_all(
-        sent.reshape(replicas, rows, share), PLANE, split_axis=0, concat_axis=0, tiled=True
-    )
-    grad_rows = grad_rows.reshape(replicas * rows, share)
-    backs = lax.all_to_all(kept_back, "y", split_axis=0, concat_axis=0, tiled=True)
-    others = swap(backs, "core", 1)
-    back_rows = jnp.stack(
-        [jnp.where(core == 0, backs, others), jnp.where(core == 0, others, backs)], axis=1
-    ).reshape(replicas * rows, head_size)
-
-    contributors = jnp.maximum(jnp.sum(keep).astype(jnp.float32), 1.0)[None]
-    grads, square = averaged(picked, back_rows, grad_rows, hidden, contributors)
+    sent = rebuild(kept_gradient, kept_back, stack)
+    got = lax.all_to_all(
+        sent.reshape(replicas, rows, share + head_size), PLANE, split_axis=0, concat_axis=0, tiled=True
+    ).reshape(replicas * rows, share + head_size)
+
+    contributors = jnp.maximum(count[0, :1], 1.0)
+    grads, square = averaged(picked, got, hidden, contributors)
     norm = jnp.sqrt(sum_over_all(square)[0, :1])
     sections = planes * columns
     threshold = clip_rms * math.sqrt(2 * width * head_size * sections)

time: 410 us -> 394 us (0.961)
  waiting for transfers between devices: 196 us -> 175 us
  matrix products: 19.3 us -> 2.4 us
  blocking collectives: 18.7 us -> 34.7 us
  other arithmetic: 11.3 us -> 5.52 us
  starting transfers between devices: 57.5 us -> 62.9 us
  Pallas kernels: 48.1 us -> 52.3 us
    all_to_all x0 -> x1, blocking collectives: none -> 34.7 us  [shards(): picked = lax.all_to_all(picked, DP, split_axis=1, concat_axis=0, tiled=True)]
    all_to_all x3 -> x1, waiting for transfers between devices: 50.1 us -> 16.3 us  [shards(): lax.all_to_all(sent.reshape(replicas, rows, share + head_size), PLANE, sp...]
    all_gather x1, waiting for transfers between devices: 0.02 us -> 24.4 us  [shards(): hidden = lax.all_gather(hidden, DP, axis=0, tiled=True)]
    unnamed x1 -> x0, blocking collectives: 18.7 us -> none
    dot_general x13 -> x1, matrix products: 19.3 us -> 2.4 us  [dot(): lax.dot_general(left, right, (dims, ((), ())), preferred_element_type=jnp...]
    ppermute x22, waiting for transfers between devices: 71.9 us -> 57.6 us  [swap(): lax.ppermute(value, axis, [(i, i ^ mask) for i in range(lax.axis_size(axi...]
    ppermute x22, starting transfers between devices: 19.8 us -> 32.3 us  [swap(): lax.ppermute(value, axis, [(i, i ^ mask) for i in range(lax.axis_size(axi...]
    unnamed x66 -> x53, local copies, waits for them, and re-layouts: 27.7 us -> 36.9 us
  transfers between devices with their start and end apart: 45 -> 43, of which waited for: 33 -> 37; matrix products, arithmetic and copies ran while one was open for 9% -> 4% of each run, Pallas kernels for 4% -> 3%
where the time goes in v3:
time: 394 us; the launch traced here: 393 us
  waiting for transfers between devices  175 us (44%)
  starting transfers between devices  62.9 us (16%)
  Pallas kernels  52.3 us (13%)
  local copies, waits for them, and re-layouts  42 us (11%)
  blocking collectives  34.7 us (9%)
  between operations  17.7 us (4%)
  other arithmetic  5.52 us (1%)
    ppermute x22, waiting for transfers between devices, swap(): lax.ppermute(value, axis, [(i, i ^ mask) for i in range(lax.axis_size(axi...  57.6 us
    ppermute x3, waiting for transfers between devices, shards(): lax.ppermute(gradient, 'z', [(i, i - 1) for i in range(1, planes)])  38.2 us
    unnamed x53, local copies, waits for them, and re-layouts  36.9 us
    all_to_all x1, blocking collectives, shards(): picked = lax.all_to_all(picked, DP, split_axis=1, concat_axis=0, tiled=True)  34.7 us
    ppermute x22, starting transfers between devices, swap(): lax.ppermute(value, axis, [(i, i ^ mask) for i in range(lax.axis_size(axi...  32.3 us
    all_gather x1, waiting for transfers between devices, shards(): hidden = lax.all_gather(hidden, DP, axis=0, tiled=True)  24.4 us
    ppermute x12, waiting for transfers between devices, turn_by(): lax.ppermute(value, axis, [(i, (i + steps) % count) for i in range(count)])  19.6 us
    all_to_all x1, waiting for transfers between devices, shards(): lax.all_to_all(sent.reshape(replicas, rows, share + head_size), PLANE, sp...  16.3 us
  transfers between devices with their start and end apart: 43, of which 37 were waited for; matrix products, arithmetic and copies ran while one was open for 4% of the time, Pallas kernels for 3%

profile of v3, /device:TPU:0, one launch (start us, length us, event | category | flops | bytes accessed | tf_op | source)
XLA Modules:
  0.0 393.0 jit_solution(13142000497657462918)
XLA Ops:
  11.6 2.2 gather_fusion
  13.7 3.3 copy.17
  19.1 2.7 fusion
  21.9 34.7 %all_to_all.26 = bf16[144,8,1024]{2,0,1:T(8,128)(2,1)S(1)} all-to-all(bf16[144,8,1024]{2,0,1:T(8,128)(2,1)S(1)} %fusion), channel_id=1, replica_groups=mesh['z'=4,'y'=4,'x'=4,'core'=2] {'x','core'}, dimensions={1} | all-to-all | bytes 4718592 | tf_op jit(solution)/shard_map/all_to_all | solution.py:433
  56.6 2.4 convolution_convert_fusion
  59.0 3.7 all-to-all-start.1
  63.8 6.1 %collective-permute-start = (bf16[144,2048]{1,0:T(8,128)(2,1)S(1)}, bf16[144,2048]{1,0:T(8,128)(2,1)S(1)}, u32[]{:S(2)}, u32[]{:S(2)}) collective-permute-start(bf16[144,2048]{1,0:T(8,128)(2,1)S(1)} %constant_dynamic-slice_fusion), channel_id=1, source_target_pairs={{0,96},{32,98},{64,100},{96,102},{10,104},{42,106},{74,108},{106,1... | collective-permute-start | bytes 1769480 | tf_op jit(solution)/shard_map/ppermute | solution.py:425
  71.2 2.0 collective-permute-start.2
  73.4 5.2 %collective-permute-done.4 = f32[8,128]{1,0:T(8,128)S(1)} collective-permute-done((f32[8,128]{1,0:T(8,128)S(1)}, f32[8,128]{1,0:T(8,128)S(1)}, u32[]{:S(2)}, u32[]{:S(2)}) %collective-permute-start.4) | collective-permute-done | bytes 4128 | tf_op jit(solution)/shard_map/ppermute | solution.py:58
  82.9 16.2 %all-gather.8.cloned.1.call-done = bf16[32,512,512]{2,1,0:T(8,128)(2,1)} async-done(((bf16[4,512,512]{2,1,0:T(8,128)(2,1)}), bf16[32,512,512]{2,1,0:T(8,128)(2,1)}) %all-gather.8.cloned.1.call-update) | async-done | bytes 16777232 | tf_op jit(solution)/shard_map/all_gather | solution.py:415
  99.1 5.8 %copy-done.2 = bf16[32,512,512]{2,1,0:T(8,128)(2,1)S(1)} copy-done((bf16[32,512,512]{2,1,0:T(8,128)(2,1)S(1)}, bf16[32,512,512]{2,1,0:T(8,128)(2,1)}, u32[]{:S(2)}) %copy-start.2) | copy-done | bytes 16777240
  104.9 4.1 %shard_map.142 = bf16[6,64,512]{2,1,0:T(8,128)(2,1)S(1)} custom-call(s32[13]{0:T(128)S(1)} %pad_add_fusion.table_ref, bf16[4,2,4,512,512]{4,3,2,1,0:T(8,128)(2,1)S(1)} %bitcast.30, bf16[4,2,4,512,512]{4,3,2,1,0:T(8,128)(2,1)S(1)} %bitcast.31), custom_call_target="tpu_custom_call" | custom-call | flops 805306368 | bytes 6291456 | tf_op jit(solution)/shard_map/pallas_call | solution.py:106
  110.5 2.1 collective-permute-start.11
  112.6 3.5 collective-permute-done.9
  116.1 2.4 collective-permute-done.11
  118.7 2.2 collective-permute-start.10
  120.9 3.8 collective-permute-done.12
  126.8 5.8 %copy-done.3 = bf16[32,512,512]{2,1,0:T(8,128)(2,1)S(1)} copy-done((bf16[32,512,512]{2,1,0:T(8,128)(2,1)S(1)}, bf16[32,512,512]{2,1,0:T(8,128)(2,1)}, u32[]{:S(2)}) %copy-start.3) | copy-done | bytes 16777240
  137.1 2.1 collective-permute-start.7
  139.2 2.5 collective-permute-done.5
  141.8 2.3 collective-permute-start.6
  144.2 2.8 collective-permute-done.7
  148.8 2.6 collective-permute-done.6.low_got
  151.4 2.5 collective-permute-done.8.high_got
  154.4 5.8 %copy-done.4 = bf16[32,512,512]{2,1,0:T(8,128)(2,1)S(1)} copy-done((bf16[32,512,512]{2,1,0:T(8,128)(2,1)S(1)}, bf16[32,512,512]{2,1,0:T(8,128)(2,1)}, u32[]{:S(2)}) %copy-start.4) | copy-done | bytes 16777240
  162.1 5.3 %shard_map.143 = (bf16[4,144,512]{2,1,0:T(8,128)(2,1)S(1)}, bf16[144,2048]{1,0:T(8,128)(2,1)S(1)}) custom-call(bf16[144,2048]{1,0:T(8,128)(2,1)S(1)} %collective-permute-done.g_ref, bf16[144,1024]{1,0:T(8,128)(2,1)S(1)} %add_convert_fusion.7.low, bf16[144,1024]{1,0:T(8,128)(2,1)S(1)} %collective-permute-done.6.low_got, ...), custom_call_target="tpu_custom_call" | custom-call | flops 1660944384 | bytes 11534336 | tf_op jit(solution)/shard_map/pallas_call | solution.py:220
  168.7 16.1 %collective-permute-done.13.g_ref = bf16[144,2048]{1,0:T(8,128)(2,1)S(1)} collective-permute-done((bf16[144,2048]{1,0:T(8,128)(2,1)S(1)}, bf16[144,2048]{1,0:T(8,128)(2,1)S(1)}, u32[]{:S(2)}, u32[]{:S(2)}) %collective-permute-start.13) | collective-permute-done | bytes 589856 | tf_op jit(solution)/shard_map/ppermute | solution.py:461
  184.8 5.8 %copy-done.5 = bf16[32,512,512]{2,1,0:T(8,128)(2,1)S(1)} copy-done((bf16[32,512,512]{2,1,0:T(8,128)(2,1)S(1)}, bf16[32,512,512]{2,1,0:T(8,128)(2,1)}, u32[]{:S(2)}) %copy-start.5) | copy-done | bytes 16777240
  196.0 2.2 collective-permute-start.16
  198.2 2.7 collective-permute-done.14
  201.0 2.8 collective-permute-start.15
  203.8 3.5 collective-permute-done.16
  207.4 4.3 %collective-permute-done.15.low_got = bf16[144,1024]{1,0:T(8,128)(2,1)S(1)} collective-permute-done((bf16[144,1024]{1,0:T(8,128)(2,1)S(1)}, bf16[144,1024]{1,0:T(8,128)(2,1)S(1)}, u32[]{:S(2)}, u32[]{:S(2)}) %collective-permute-start.15) | collective-permute-done | bytes 294944 | tf_op jit(solution)/shard_map/ppermute | solution.py:53
  211.7 2.4 collective-permute-done.17.high_got
  214.2 5.3 %shard_map.146 = (bf16[4,144,512]{2,1,0:T(8,128)(2,1)S(1)}, bf16[144,2048]{1,0:T(8,128)(2,1)S(1)}) custom-call(bf16[144,2048]{1,0:T(8,128)(2,1)S(1)} %collective-permute-done.13.g_ref, bf16[144,1024]{1,0:T(8,128)(2,1)S(1)} %add_convert_fusion.5.low, bf16[144,1024]{1,0:T(8,128)(2,1)S(1)} %collective-permute-done.15.low_got, ...), custom_call_target="tpu_custom_call" | custom-call | flops 1660944384 | bytes 11534336 | tf_op jit(solution)/shard_map/pallas_call | solution.py:220
  220.8 11.6 %collective-permute-done.18.g_ref = bf16[144,2048]{1,0:T(8,128)(2,1)S(1)} collective-permute-done((bf16[144,2048]{1,0:T(8,128)(2,1)S(1)}, bf16[144,2048]{1,0:T(8,128)(2,1)S(1)}, u32[]{:S(2)}, u32[]{:S(2)}) %collective-permute-start.18) | collective-permute-done | bytes 589856 | tf_op jit(solution)/shard_map/ppermute | solution.py:461
  234.6 2.0 shard_map.148
  236.6 2.5 collective-permute-start.21
  239.2 2.0 collective-permute-done.19
  241.2 2.7 collective-permute-start.20
  244.0 2.0 collective-permute-done.21
  246.8 2.5 collective-permute-done.20.low_got
  249.3 3.6 collective-permute-done.22.high_got
  252.8 5.3 %shard_map.149 = (bf16[4,144,512]{2,1,0:T(8,128)(2,1)S(1)}, bf16[144,2048]{1,0:T(8,128)(2,1)S(1)}) custom-call(bf16[144,2048]{1,0:T(8,128)(2,1)S(1)} %collective-permute-done.18.g_ref, bf16[144,1024]{1,0:T(8,128)(2,1)S(1)} %add_convert_fusion.3.low, bf16[144,1024]{1,0:T(8,128)(2,1)S(1)} %collective-permute-done.20.low_got, ...), custom_call_target="tpu_custom_call" | custom-call | flops 1660944384 | bytes 11534336 | tf_op jit(solution)/shard_map/pallas_call | solution.py:220
  259.5 10.5 %collective-permute-done.23.g_ref = bf16[144,2048]{1,0:T(8,128)(2,1)S(1)} collective-permute-done((bf16[144,2048]{1,0:T(8,128)(2,1)S(1)}, bf16[144,2048]{1,0:T(8,128)(2,1)S(1)}, u32[]{:S(2)}, u32[]{:S(2)}) %collective-permute-start.23) | collective-permute-done | bytes 589856 | tf_op jit(solution)/shard_map/ppermute | solution.py:461
  272.6 2.0 shard_map.151
  274.6 2.4 collective-permute-start.26
  277.1 4.5 %collective-permute-done.24 = bf16[144,1024]{1,0:T(8,128)(2,1)S(1)} collective-permute-done((bf16[144,1024]{1,0:T(8,128)(2,1)S(1)}, bf16[144,1024]{1,0:T(8,128)(2,1)S(1)}, u32[]{:S(2)}, u32[]{:S(2)}) %collective-permute-start.24) | collective-permute-done | bytes 294944 | tf_op jit(solution)/shard_map/ppermute | solution.py:53
  281.6 3.1 collective-permute-start.25
  285.3 4.3 %collective-permute-done.25.low_got = bf16[144,1024]{1,0:T(8,128)(2,1)S(1)} collective-permute-done((bf16[144,1024]{1,0:T(8,128)(2,1)S(1)}, bf16[144,1024]{1,0:T(8,128)(2,1)S(1)}, u32[]{:S(2)}, u32[]{:S(2)}) %collective-permute-start.25) | collective-permute-done | bytes 294944 | tf_op jit(solution)/shard_map/ppermute | solution.py:53
  289.6 2.2 collective-permute-done.27.high_got
  293.3 3.8 shard_map.153
  298.9 3.7 all-to-all-start.2
  304.5 24.4 %all-gather.6.cloned.1.call-done.h_ref = bf16[1152,512]{1,0:T(8,128)(2,1)} async-done(((bf16[144,512]{1,0:T(8,128)(2,1)}), bf16[1152,512]{1,0:T(8,128)(2,1)}) %all-gather.6.cloned.1.call-update) | async-done | bytes 1179664 | tf_op jit(solution)/shard_map/all_gather | solution.py:442
  328.9 16.3 %all-to-all-done.2 = bf16[8,144,1536]{2,1,0:T(8,128)(2,1)S(1)} async-done(((bf16[8,144,1536]{2,1,0:T(8,128)(2,1)}), bf16[8,144,1536]{2,1,0:T(8,128)(2,1)S(1)}, u32[]{:S(2)}, u32[]{:S(2)}) %all-to-all-start.2) | async-done | bytes 3538976 | tf_op jit(solution)/shard_map/all_to_all | solution.py:468
  348.1 4.9 %shard_map.154 = (f32[1024,1024]{1,0:T(8,128)S(1)}, f32[8,128]{1,0:T(8,128)S(1)}) custom-call(f32[1]{0:T(128)} %bitcast.13.count_ref, bf16[1152,1024]{1,0:T(8,128)(2,1)S(1)} %bitcast.54, bf16[1152,1536]{1,0:T(8,128)(2,1)S(1)} %bitcast.50, bf16[1152,1536]{1,0:T(8,128)(2,1)S(1)} %bitcast.51, bf16[1152,512]{1,0:T(8,128)(2,1)S(1)} %copy-done.15), custom_call_target="tpu_custom_call" | custom-call | flops 2415919104 | bytes 11272192 | tf_op jit(solution)/shard_map/pallas_call | solution.py:334
  354.7 2.3 collective-permute-start.30
  357.0 2.4 collective-permute-done.31
  359.4 2.4 collective-permute-done.29
  362.1 2.9 collective-permute-start.33
  366.9 2.9 collective-permute-done.32
  369.9 3.2 collective-permute-start.37
  376.6 2.3 collective-permute-done.35
  380.2 6.3 %shard_map.155 = (f32[1,1024,1024]{2,1,0:T(8,128)}, bf16[1,1024,1024]{2,1,0:T(8,128)(2,1)}, bf16[1,1024,1024]{2,1,0:T(8,128)(2,1)}) custom-call(f32[1]{0:T(128)S(6)} %min.3.factor_ref, f32[1024,1024]{1,0:T(8,128)S(1)} %get-tuple-element.26.grad_ref, f32[1,1024,1024]{2,1,0:T(8,128)S(1)} %copy-done.12, bf16[1,1024,1024]{2,1,0:T(8,128)(2,1)S(1)} %copy-done.13, ...), custom_call_target="tpu_custom_call" | custom-call | flops 20971520 | bytes 20971520 | tf_op jit(solution)/shard_map/pallas_call | solution.py:378
  (133 shorter events, 55.3 us)
Async XLA Ops:
  7.2 4.4 %copy-start = (bf16[1,3,48,8192]{3,2,1,0:T(8,128)(2,1)S(1)}, bf16[1,3,48,8192]{3,2,1,0:T(8,128)(2,1)}, u32[]{:S(2)}) copy-start(bf16[1,3,48,8192]{3,2,1,0:T(8,128)(2,1)} %param.12) | copy-start | bytes 7077892
  7.2 91.9 %all-gather.8.cloned.1.call-start = ((), (), s32[]{:S(2)}) async-start(), calls=%async_computation.4 | async-start | bytes 18874368 | tf_op jit(solution)/shard_map/all_gather | solution.py:415
  9.8 1.7 copy-start.19
  13.7 4.1 %copy-start.20 = (s32[8]{0:T(128)S(1)}, s32[8]{0:T(128)}, u32[]{:S(2)}) copy-start(s32[8]{0:T(128)} %param.17) | copy-start | bytes 100
  21.9 34.7 %copy-start.18 = (bf16[1,1024,512]{2,1,0:T(8,128)(2,1)S(1)}, bf16[1,1024,512]{2,1,0:T(8,128)(2,1)}, u32[]{:S(2)}) copy-start(bf16[1,1024,512]{2,1,0:T(8,128)(2,1)} %param.14) | copy-start | bytes 3145732
  56.6 2.4 copy-start.9
  59.0 14.3 %copy-start.21 = (s32[12]{0:T(128)S(1)}, s32[12]{0:T(128)}, u32[]{:S(2)}) copy-start(s32[12]{0:T(128)} %constant.56.clone) | copy-start | bytes 148
  59.0 21.2 %all-to-all-start.1 = ((bf16[8,144,512]{2,1,0:T(8,128)(2,1)}), bf16[8,144,512]{2,1,0:T(8,128)(2,1)S(1)}, u32[]{:S(2)}, u32[]{:S(2)}) async-start(bf16[8,144,512]{2,1,0:T(8,128)(2,1)} %bitcast.11), calls=%async_computation.1 | async-start | bytes 2359296 | tf_op jit(solution)/shard_map/all_to_all | solution.py:436
  62.7 91.7 %all-gather.10.cloned.1.call-start = ((), (), s32[]{:S(2)}) async-start(), calls=%async_computation.5 | async-start | bytes 3538944 | tf_op jit(solution)/shard_map/all_gather | solution.py:452
  63.8 19.0 %collective-permute-start = (bf16[144,2048]{1,0:T(8,128)(2,1)S(1)}, bf16[144,2048]{1,0:T(8,128)(2,1)S(1)}, u32[]{:S(2)}, u32[]{:S(2)}) collective-permute-start(bf16[144,2048]{1,0:T(8,128)(2,1)S(1)} %constant_dynamic-slice_fusion), channel_id=1, source_target_pairs={{0,96},{32,98},{64,100},{96,102},{10,104},{42,106},{74,108},{106,1... | collective-permute-start | bytes 1769480 | tf_op jit(solution)/shard_map/ppermute | solution.py:425
  70.0 1.2 collective-permute-start.1
  71.2 7.3 %collective-permute-start.4 = (f32[8,128]{1,0:T(8,128)S(1)}, f32[8,128]{1,0:T(8,128)S(1)}, u32[]{:S(2)}, u32[]{:S(2)}) collective-permute-start(f32[8,128]{1,0:T(8,128)S(1)} %broadcast_add_fusion), channel_id=1, source_target_pairs={{0,6},{2,0},{4,2},{6,4},{1,7},{3,1},{5,3},{7,5},{8,14},{10,8},{12,... | collective-permute-start | bytes 12296 | tf_op jit(solution)/shard_map/ppermute | solution.py:58
  71.2 7.3 %collective-permute-start.2 = (f32[8,128]{1,0:T(8,128)S(1)}, f32[8,128]{1,0:T(8,128)S(1)}, u32[]{:S(2)}, u32[]{:S(2)}) collective-permute-start(f32[8,128]{1,0:T(8,128)S(1)} %broadcast_add_fusion), channel_id=1, source_target_pairs={{0,2},{2,4},{4,6},{6,0},{1,3},{3,5},{5,7},{7,1},{8,10},{10,12},{12... | collective-permute-start | bytes 12296 | tf_op jit(solution)/shard_map/ppermute | solution.py:58
  73.3 6.9 %collective-permute-start.3 = (f32[8,128]{1,0:T(8,128)S(1)}, f32[8,128]{1,0:T(8,128)S(1)}, u32[]{:S(2)}, u32[]{:S(2)}) collective-permute-start(f32[8,128]{1,0:T(8,128)S(1)} %broadcast_add_fusion), channel_id=1, source_target_pairs={{0,4},{2,6},{4,0},{6,2},{1,5},{3,7},{5,1},{7,3},{8,12},{10,14},{12... | collective-permute-start | bytes 12296 | tf_op jit(solution)/shard_map/ppermute | solution.py:58
  99.1 5.8 %copy-start.2 = (bf16[32,512,512]{2,1,0:T(8,128)(2,1)S(1)}, bf16[32,512,512]{2,1,0:T(8,128)(2,1)}, u32[]{:S(2)}) copy-start(bf16[32,512,512]{2,1,0:T(8,128)(2,1)} %all-gather.8.cloned.1.call-done) | copy-start | bytes 50331652
  109.0 7.1 %collective-permute-start.9 = (bf16[3,64,512]{2,1,0:T(8,128)(2,1)S(1)}, bf16[3,64,512]{2,1,0:T(8,128)(2,1)S(1)}, u32[]{:S(2)}, u32[]{:S(2)}) collective-permute-start(bf16[3,64,512]{2,1,0:T(8,128)(2,1)S(1)} %get-tuple-element.29), channel_id=1, source_target_pairs={{0,2},{2,0},{4,6},{6,4},{1,3},{3,1},{5,7},{7,5},{8,10},{10,8},{12,... | collective-permute-start | bytes 589832 | tf_op jit(solution)/shard_map/ppermute | solution.py:53
  110.5 8.0 %collective-permute-start.11 = (bf16[3,64,512]{2,1,0:T(8,128)(2,1)S(1)}, bf16[3,64,512]{2,1,0:T(8,128)(2,1)S(1)}, u32[]{:S(2)}, u32[]{:S(2)}) collective-permute-start(bf16[3,64,512]{2,1,0:T(8,128)(2,1)S(1)} %get-tuple-element.30), channel_id=1, source_target_pairs={{0,6},{2,4},{4,2},{6,0},{1,7},{3,5},{5,3},{7,1},{8,14},{10,12},{12... | collective-permute-start | bytes 589832 | tf_op jit(solution)/shard_map/ppermute | solution.py:53
  118.6 6.0 %collective-permute-start.12 = (bf16[3,64,512]{2,1,0:T(8,128)(2,1)S(1)}, bf16[3,64,512]{2,1,0:T(8,128)(2,1)S(1)}, u32[]{:S(2)}, u32[]{:S(2)}) collective-permute-start(bf16[3,64,512]{2,1,0:T(8,128)(2,1)S(1)} %get-tuple-element.28), channel_id=1, source_target_pairs={{0,2},{2,0},{4,6},{6,4},{1,3},{3,1},{5,7},{7,5},{8,10},{10,8},{12,... | collective-permute-start | bytes 589832 | tf_op jit(solution)/shard_map/ppermute | solution.py:53
  118.7 7.2 %collective-permute-start.10 = (bf16[3,64,512]{2,1,0:T(8,128)(2,1)S(1)}, bf16[3,64,512]{2,1,0:T(8,128)(2,1)S(1)}, u32[]{:S(2)}, u32[]{:S(2)}) collective-permute-start(bf16[3,64,512]{2,1,0:T(8,128)(2,1)S(1)} %get-tuple-element.27), channel_id=1, source_target_pairs={{0,6},{2,4},{4,2},{6,0},{1,7},{3,5},{5,3},{7,1},{8,14},{10,12},{12... | collective-permute-start | bytes 589832 | tf_op jit(solution)/shard_map/ppermute | solution.py:53
  126.8 5.8 %copy-start.3 = (bf16[32,512,512]{2,1,0:T(8,128)(2,1)S(1)}, bf16[32,512,512]{2,1,0:T(8,128)(2,1)}, u32[]{:S(2)}) copy-start(bf16[32,512,512]{2,1,0:T(8,128)(2,1)} %all-gather.8.cloned.1.call-done) | copy-start | bytes 50331652
  134.6 7.2 %collective-permute-start.5 = (bf16[144,1024]{1,0:T(8,128)(2,1)S(1)}, bf16[144,1024]{1,0:T(8,128)(2,1)S(1)}, u32[]{:S(2)}, u32[]{:S(2)}) collective-permute-start(bf16[144,1024]{1,0:T(8,128)(2,1)S(1)} %shard_map.140), channel_id=1, source_target_pairs={{0,2},{2,0},{4,6},{6,4},{1,3},{3,1},{5,7},{7,5},{8,10},{10,8},{12,... | collective-permute-start | bytes 884744 | tf_op jit(solution)/shard_map/ppermute | solution.py:53
  137.1 9.9 %collective-permute-start.7 = (bf16[144,1024]{1,0:T(8,128)(2,1)S(1)}, bf16[144,1024]{1,0:T(8,128)(2,1)S(1)}, u32[]{:S(2)}, u32[]{:S(2)}) collective-permute-start(bf16[144,1024]{1,0:T(8,128)(2,1)S(1)} %shard_map.141), channel_id=1, source_target_pairs={{0,6},{2,4},{4,2},{6,0},{1,7},{3,5},{5,3},{7,1},{8,14},{10,12},{12... | collective-permute-start | bytes 884744 | tf_op jit(solution)/shard_map/ppermute | solution.py:53
  141.8 9.6 %collective-permute-start.6 = (bf16[144,1024]{1,0:T(8,128)(2,1)S(1)}, bf16[144,1024]{1,0:T(8,128)(2,1)S(1)}, u32[]{:S(2)}, u32[]{:S(2)}) collective-permute-start(bf16[144,1024]{1,0:T(8,128)(2,1)S(1)} %add_convert_fusion.7.low), channel_id=1, source_target_pairs={{0,6},{2,4},{4,2},{6,0},{1,7},{3,5},{5,3},{7,1},{8,14},{10,12},{12... | collective-permute-start | bytes 884744 | tf_op jit(solution)/shard_map/ppermute | solution.py:53
  147.1 6.8 %collective-permute-start.8 = (bf16[144,1024]{1,0:T(8,128)(2,1)S(1)}, bf16[144,1024]{1,0:T(8,128)(2,1)S(1)}, u32[]{:S(2)}, u32[]{:S(2)}) collective-permute-start(bf16[144,1024]{1,0:T(8,128)(2,1)S(1)} %add_convert_fusion.6.high), channel_id=1, source_target_pairs={{0,2},{2,0},{4,6},{6,4},{1,3},{3,1},{5,7},{7,5},{8,10},{10,8},{12,... | collective-permute-start | bytes 884744 | tf_op jit(solution)/shard_map/ppermute | solution.py:53
  154.4 5.8 %copy-start.4 = (bf16[32,512,512]{2,1,0:T(8,128)(2,1)S(1)}, bf16[32,512,512]{2,1,0:T(8,128)(2,1)}, u32[]{:S(2)}) copy-start(bf16[32,512,512]{2,1,0:T(8,128)(2,1)} %all-gather.8.cloned.1.call-done) | copy-start | bytes 50331652
  160.2 1.9 copy-start.6
  167.4 17.4 %collective-permute-start.13 = (bf16[144,2048]{1,0:T(8,128)(2,1)S(1)}, bf16[144,2048]{1,0:T(8,128)(2,1)S(1)}, u32[]{:S(2)}, u32[]{:S(2)}) collective-permute-start(bf16[144,2048]{1,0:T(8,128)(2,1)S(1)} %get-tuple-element.18), channel_id=1, source_target_pairs={{32,0},{64,32},{96,64},{33,1},{65,33},{97,65},{34,2},{66,34},{98,6... | collective-permute-start | bytes 1769480 | tf_op jit(solution)/shard_map/ppermute | solution.py:461
  184.7 5.8 %copy-start.5 = (bf16[32,512,512]{2,1,0:T(8,128)(2,1)S(1)}, bf16[32,512,512]{2,1,0:T(8,128)(2,1)}, u32[]{:S(2)}) copy-start(bf16[32,512,512]{2,1,0:T(8,128)(2,1)} %all-gather.8.cloned.1.call-done) | copy-start | bytes 50331652
  192.5 8.4 %collective-permute-start.14 = (bf16[144,1024]{1,0:T(8,128)(2,1)S(1)}, bf16[144,1024]{1,0:T(8,128)(2,1)S(1)}, u32[]{:S(2)}, u32[]{:S(2)}) collective-permute-start(bf16[144,1024]{1,0:T(8,128)(2,1)S(1)} %shard_map.144), channel_id=1, source_target_pairs={{0,2},{2,0},{4,6},{6,4},{1,3},{3,1},{5,7},{7,5},{8,10},{10,8},{12,... | collective-permute-start | bytes 884744 | tf_op jit(solution)/shard_map/ppermute | solution.py:53
  194.0 20.1 %copy-start.7 = (bf16[48,64,512]{2,1,0:T(8,128)(2,1)S(1)}, bf16[48,64,512]{2,1,0:T(8,128)(2,1)}, u32[]{:S(2)}) copy-start(bf16[48,64,512]{2,1,0:T(8,128)(2,1)} %all-gather.10.cloned.1.call-done) | copy-start | bytes 9437188
  196.0 11.2 %collective-permute-start.16 = (bf16[144,1024]{1,0:T(8,128)(2,1)S(1)}, bf16[144,1024]{1,0:T(8,128)(2,1)S(1)}, u32[]{:S(2)}, u32[]{:S(2)}) collective-permute-start(bf16[144,1024]{1,0:T(8,128)(2,1)S(1)} %shard_map.145), channel_id=1, source_target_pairs={{0,6},{2,4},{4,2},{6,0},{1,7},{3,5},{5,3},{7,1},{8,14},{10,12},{12... | collective-permute-start | bytes 884744 | tf_op jit(solution)/shard_map/ppermute | solution.py:53
  201.0 10.7 %collective-permute-start.15 = (bf16[144,1024]{1,0:T(8,128)(2,1)S(1)}, bf16[144,1024]{1,0:T(8,128)(2,1)S(1)}, u32[]{:S(2)}, u32[]{:S(2)}) collective-permute-start(bf16[144,1024]{1,0:T(8,128)(2,1)S(1)} %add_convert_fusion.5.low), channel_id=1, source_target_pairs={{0,6},{2,4},{4,2},{6,0},{1,7},{3,5},{5,3},{7,1},{8,14},{10,12},{12... | collective-permute-start | bytes 884744 | tf_op jit(solution)/shard_map/ppermute | solution.py:53
  207.3 6.8 %collective-permute-start.17 = (bf16[144,1024]{1,0:T(8,128)(2,1)S(1)}, bf16[144,1024]{1,0:T(8,128)(2,1)S(1)}, u32[]{:S(2)}, u32[]{:S(2)}) collective-permute-start(bf16[144,1024]{1,0:T(8,128)(2,1)S(1)} %add_convert_fusion.4.high), channel_id=1, source_target_pairs={{0,2},{2,0},{4,6},{6,4},{1,3},{3,1},{5,7},{7,5},{8,10},{10,8},{12,... | collective-permute-start | bytes 884744 | tf_op jit(solution)/shard_map/ppermute | solution.py:53
  219.5 12.9 %collective-permute-start.18 = (bf16[144,2048]{1,0:T(8,128)(2,1)S(1)}, bf16[144,2048]{1,0:T(8,128)(2,1)S(1)}, u32[]{:S(2)}, u32[]{:S(2)}) collective-permute-start(bf16[144,2048]{1,0:T(8,128)(2,1)S(1)} %get-tuple-element.19), channel_id=1, source_target_pairs={{32,0},{64,32},{96,64},{33,1},{65,33},{97,65},{34,2},{66,34},{98,6... | collective-permute-start | bytes 1769480 | tf_op jit(solution)/shard_map/ppermute | solution.py:461
  234.4 6.8 %collective-permute-start.19 = (bf16[144,1024]{1,0:T(8,128)(2,1)S(1)}, bf16[144,1024]{1,0:T(8,128)(2,1)S(1)}, u32[]{:S(2)}, u32[]{:S(2)}) collective-permute-start(bf16[144,1024]{1,0:T(8,128)(2,1)S(1)} %shard_map.147), channel_id=1, source_target_pairs={{0,2},{2,0},{4,6},{6,4},{1,3},{3,1},{5,7},{7,5},{8,10},{10,8},{12,... | collective-permute-start | bytes 884744 | tf_op jit(solution)/shard_map/ppermute | solution.py:53
  236.6 9.3 %collective-permute-start.21 = (bf16[144,1024]{1,0:T(8,128)(2,1)S(1)}, bf16[144,1024]{1,0:T(8,128)(2,1)S(1)}, u32[]{:S(2)}, u32[]{:S(2)}) collective-permute-start(bf16[144,1024]{1,0:T(8,128)(2,1)S(1)} %shard_map.148), channel_id=1, source_target_pairs={{0,6},{2,4},{4,2},{6,0},{1,7},{3,5},{5,3},{7,1},{8,14},{10,12},{12... | collective-permute-start | bytes 884744 | tf_op jit(solution)/shard_map/ppermute | solution.py:53
  241.2 8.0 %collective-permute-start.20 = (bf16[144,1024]{1,0:T(8,128)(2,1)S(1)}, bf16[144,1024]{1,0:T(8,128)(2,1)S(1)}, u32[]{:S(2)}, u32[]{:S(2)}) collective-permute-start(bf16[144,1024]{1,0:T(8,128)(2,1)S(1)} %add_convert_fusion.3.low), channel_id=1, source_target_pairs={{0,6},{2,4},{4,2},{6,0},{1,7},{3,5},{5,3},{7,1},{8,14},{10,12},{12... | collective-permute-start | bytes 884744 | tf_op jit(solution)/shard_map/ppermute | solution.py:53
  246.0 6.8 %collective-permute-start.22 = (bf16[144,1024]{1,0:T(8,128)(2,1)S(1)}, bf16[144,1024]{1,0:T(8,128)(2,1)S(1)}, u32[]{:S(2)}, u32[]{:S(2)}) collective-permute-start(bf16[144,1024]{1,0:T(8,128)(2,1)S(1)} %add_convert_fusion.2.high), channel_id=1, source_target_pairs={{0,2},{2,0},{4,6},{6,4},{1,3},{3,1},{5,7},{7,5},{8,10},{10,8},{12,... | collective-permute-start | bytes 884744 | tf_op jit(solution)/shard_map/ppermute | solution.py:53
  258.2 11.8 %collective-permute-start.23 = (bf16[144,2048]{1,0:T(8,128)(2,1)S(1)}, bf16[144,2048]{1,0:T(8,128)(2,1)S(1)}, u32[]{:S(2)}, u32[]{:S(2)}) collective-permute-start(bf16[144,2048]{1,0:T(8,128)(2,1)S(1)} %get-tuple-element.20), channel_id=1, source_target_pairs={{32,0},{64,32},{96,64},{33,1},{65,33},{97,65},{34,2},{66,34},{98,6... | collective-permute-start | bytes 1769480 | tf_op jit(solution)/shard_map/ppermute | solution.py:461
  271.9 9.6 %collective-permute-start.24 = (bf16[144,1024]{1,0:T(8,128)(2,1)S(1)}, bf16[144,1024]{1,0:T(8,128)(2,1)S(1)}, u32[]{:S(2)}, u32[]{:S(2)}) collective-permute-start(bf16[144,1024]{1,0:T(8,128)(2,1)S(1)} %shard_map.150), channel_id=1, source_target_pairs={{0,2},{2,0},{4,6},{6,4},{1,3},{3,1},{5,7},{7,5},{8,10},{10,8},{12,... | collective-permute-start | bytes 884744 | tf_op jit(solution)/shard_map/ppermute | solution.py:53
  272.6 20.6 %slice-start = ((s8[16777216]{0:T(1024)(128)(4,1)}), s8[4194304]{0:T(1024)(128)(4,1)S(1)}, s32[]{:S(2)}) async-start(s8[16777216]{0:T(1024)(128)(4,1)} %bitcast.43), calls=%async_computation.6 | async-start | bytes 8388608
  272.6 20.7 %slice-start.1 = ((s8[16777216]{0:T(1024)(128)(4,1)}), s8[4194304]{0:T(1024)(128)(4,1)S(1)}, s32[]{:S(2)}) async-start(s8[16777216]{0:T(1024)(128)(4,1)} %bitcast.43), calls=%async_computation.7 | async-start | bytes 8388608
  272.6 20.7 %slice-start.2 = ((s8[16777216]{0:T(1024)(128)(4,1)}), s8[4194304]{0:T(1024)(128)(4,1)S(1)}, s32[]{:S(2)}) async-start(s8[16777216]{0:T(1024)(128)(4,1)} %bitcast.43), calls=%async_computation.8 | async-start | bytes 8388608
  274.6 10.2 %collective-permute-start.26 = (bf16[144,1024]{1,0:T(8,128)(2,1)S(1)}, bf16[144,1024]{1,0:T(8,128)(2,1)S(1)}, u32[]{:S(2)}, u32[]{:S(2)}) collective-permute-start(bf16[144,1024]{1,0:T(8,128)(2,1)S(1)} %shard_map.151), channel_id=1, source_target_pairs={{0,6},{2,4},{4,2},{6,0},{1,7},{3,5},{5,3},{7,1},{8,14},{10,12},{12... | collective-permute-start | bytes 884744 | tf_op jit(solution)/shard_map/ppermute | solution.py:53
  281.6 8.0 %collective-permute-start.25 = (bf16[144,1024]{1,0:T(8,128)(2,1)S(1)}, bf16[144,1024]{1,0:T(8,128)(2,1)S(1)}, u32[]{:S(2)}, u32[]{:S(2)}) collective-permute-start(bf16[144,1024]{1,0:T(8,128)(2,1)S(1)} %add_convert_fusion.1.low), channel_id=1, source_target_pairs={{0,6},{2,4},{4,2},{6,0},{1,7},{3,5},{5,3},{7,1},{8,14},{10,12},{12... | collective-permute-start | bytes 884744 | tf_op jit(solution)/shard_map/ppermute | solution.py:53
  284.9 7.0 %collective-permute-start.27 = (bf16[144,1024]{1,0:T(8,128)(2,1)S(1)}, bf16[144,1024]{1,0:T(8,128)(2,1)S(1)}, u32[]{:S(2)}, u32[]{:S(2)}) collective-permute-start(bf16[144,1024]{1,0:T(8,128)(2,1)S(1)} %add_convert_fusion.high), channel_id=1, source_target_pairs={{0,2},{2,0},{4,6},{6,4},{1,3},{3,1},{5,7},{7,5},{8,10},{10,8},{12,... | collective-permute-start | bytes 884744 | tf_op jit(solution)/shard_map/ppermute | solution.py:53
  285.3 8.0 %slice-start.3 = ((s8[16777216]{0:T(1024)(128)(4,1)}), s8[4194304]{0:T(1024)(128)(4,1)S(1)}, s32[]{:S(2)}) async-start(s8[16777216]{0:T(1024)(128)(4,1)} %bitcast.43), calls=%async_computation.9 | async-start | bytes 8388608
  297.1 1.8 copy-start.8
  298.9 46.2 %all-to-all-start.2 = ((bf16[8,144,1536]{2,1,0:T(8,128)(2,1)}), bf16[8,144,1536]{2,1,0:T(8,128)(2,1)S(1)}, u32[]{:S(2)}, u32[]{:S(2)}) async-start(bf16[8,144,1536]{2,1,0:T(8,128)(2,1)} %bitcast.52), calls=%async_computation.2 | async-start | bytes 7077888 | tf_op jit(solution)/shard_map/all_to_all | solution.py:468
  302.6 26.3 %all-gather.6.cloned.1.call-start = ((), (), s32[]{:S(2)}) async-start(), calls=%async_computation.3 | async-start | bytes 1327104 | tf_op jit(solution)/shard_map/all_gather | solution.py:442
  348.1 32.1 %copy-start.12 = (f32[1,1024,1024]{2,1,0:T(8,128)S(1)}, f32[1,1024,1024]{2,1,0:T(8,128)}, u32[]{:S(2)}) copy-start(f32[1,1024,1024]{2,1,0:T(8,128)} %master_ref.1) | copy-start | bytes 12582916
  348.1 32.1 %copy-start.13 = (bf16[1,1024,1024]{2,1,0:T(8,128)(2,1)S(1)}, bf16[1,1024,1024]{2,1,0:T(8,128)(2,1)}, u32[]{:S(2)}) copy-start(bf16[1,1024,1024]{2,1,0:T(8,128)(2,1)} %one_ref.1) | copy-start | bytes 6291460
  348.1 32.1 %copy-start.14 = (bf16[1,1024,1024]{2,1,0:T(8,128)(2,1)S(1)}, bf16[1,1024,1024]{2,1,0:T(8,128)(2,1)}, u32[]{:S(2)}) copy-start(bf16[1,1024,1024]{2,1,0:T(8,128)(2,1)} %two_ref.1) | copy-start | bytes 6291460
  353.0 1.2 collective-permute-start.28
  354.3 5.1 %collective-permute-start.31 = (f32[8,128]{1,0:T(8,128)S(1)}, f32[8,128]{1,0:T(8,128)S(1)}, u32[]{:S(2)}, u32[]{:S(2)}) collective-permute-start(f32[8,128]{1,0:T(8,128)S(1)} %add.157), channel_id=1, source_target_pairs={{0,4},{2,6},{4,0},{6,2},{1,5},{3,7},{5,1},{7,3},{8,12},{10,14},{12... | collective-permute-start | bytes 12296 | tf_op jit(solution)/shard_map/ppermute | solution.py:58
  354.7 4.7 %collective-permute-start.30 = (f32[8,128]{1,0:T(8,128)S(1)}, f32[8,128]{1,0:T(8,128)S(1)}, u32[]{:S(2)}, u32[]{:S(2)}) collective-permute-start(f32[8,128]{1,0:T(8,128)S(1)} %add.157), channel_id=1, source_target_pairs={{0,6},{2,0},{4,2},{6,4},{1,7},{3,1},{5,3},{7,5},{8,14},{10,8},{12,... | collective-permute-start | bytes 12296 | tf_op jit(solution)/shard_map/ppermute | solution.py:58
  357.0 4.8 %collective-permute-start.29 = (f32[8,128]{1,0:T(8,128)S(1)}, f32[8,128]{1,0:T(8,128)S(1)}, u32[]{:S(2)}, u32[]{:S(2)}) collective-permute-start(f32[8,128]{1,0:T(8,128)S(1)} %add.157), channel_id=1, source_target_pairs={{0,2},{2,4},{4,6},{6,0},{1,3},{3,5},{5,7},{7,1},{8,10},{10,12},{12... | collective-permute-start | bytes 12296 | tf_op jit(solution)/shard_map/ppermute | solution.py:58
  361.8 5.1 %collective-permute-start.34 = (f32[8,128]{1,0:T(8,128)S(1)}, f32[8,128]{1,0:T(8,128)S(1)}, u32[]{:S(2)}, u32[]{:S(2)}) collective-permute-start(f32[8,128]{1,0:T(8,128)S(1)} %add_add_fusion.4), channel_id=1, source_target_pairs={{0,16},{8,24},{16,0},{24,8},{1,17},{9,25},{17,1},{25,9},{2,18},{10... | collective-permute-start | bytes 12296 | tf_op jit(solution)/shard_map/ppermute | solution.py:58
  362.1 4.8 %collective-permute-start.33 = (f32[8,128]{1,0:T(8,128)S(1)}, f32[8,128]{1,0:T(8,128)S(1)}, u32[]{:S(2)}, u32[]{:S(2)}) collective-permute-start(f32[8,128]{1,0:T(8,128)S(1)} %add_add_fusion.4), channel_id=1, source_target_pairs={{0,24},{8,0},{16,8},{24,16},{1,25},{9,1},{17,9},{25,17},{2,26},{10... | collective-permute-start | bytes 12296 | tf_op jit(solution)/shard_map/ppermute | solution.py:58
  365.0 4.8 %collective-permute-start.32 = (f32[8,128]{1,0:T(8,128)S(1)}, f32[8,128]{1,0:T(8,128)S(1)}, u32[]{:S(2)}, u32[]{:S(2)}) collective-permute-start(f32[8,128]{1,0:T(8,128)S(1)} %add_add_fusion.4), channel_id=1, source_target_pairs={{0,8},{8,16},{16,24},{24,0},{1,9},{9,17},{17,25},{25,1},{2,10},{10... | collective-permute-start | bytes 12296 | tf_op jit(solution)/shard_map/ppermute | solution.py:58
  369.9 5.8 %collective-permute-start.37 = (f32[8,128]{1,0:T(8,128)S(1)}, f32[8,128]{1,0:T(8,128)S(1)}, u32[]{:S(2)}, u32[]{:S(2)}) collective-permute-start(f32[8,128]{1,0:T(8,128)S(1)} %add_add_fusion.3), channel_id=1, source_target_pairs={{0,64},{32,96},{64,0},{96,32},{1,65},{33,97},{65,1},{97,33},{2,66}... | collective-permute-start | bytes 12296 | tf_op jit(solution)/shard_map/ppermute | solution.py:58
  373.0 3.6 collective-permute-start.36
  374.1 4.8 %collective-permute-start.35 = (f32[8,128]{1,0:T(8,128)S(1)}, f32[8,128]{1,0:T(8,128)S(1)}, u32[]{:S(2)}, u32[]{:S(2)}) collective-permute-start(f32[8,128]{1,0:T(8,128)S(1)} %add_add_fusion.3), channel_id=1, source_target_pairs={{0,32},{32,64},{64,96},{96,0},{1,33},{33,65},{65,97},{97,1},{2,34}... | collective-permute-start | bytes 12296 | tf_op jit(solution)/shard_map/ppermute | solution.py:58
  380.2 6.3 %copy-start.1 = (bf16[1,3,48,8192]{3,2,1,0:T(8,128)(2,1)S(1)}, bf16[1,3,48,8192]{3,2,1,0:T(8,128)(2,1)}, u32[]{:S(2)}) copy-start(bf16[1,3,48,8192]{3,2,1,0:T(8,128)(2,1)} %param.12) | copy-start | bytes 7077892
  (5 other events, 6.9 us)
Sparse Core Ops, SparseCore 0:
  11.6 87.4 all-gather.7
  126.9 27.4 all-gather.9
  305.7 23.1 all-gather.5

commit v4 on v3

--- a/solution.py
+++ b/solution.py
@@ -21,6 +21,7 @@
 
 
 VMEM_LIMIT = 18 * 1024 * 1024
+STREAM_LIMIT = 60 * 1024 * 1024
 PAIRS = ((0, 1), (0, 2), (1, 2), (0, 3), (1, 3), (2, 3))
 
 
@@ -32,7 +33,7 @@
     return dot(left, right, ((1,), (1,)))
 
 
-def call(kernel, grid, in_specs, out_specs, out_shape, scratch=(), cost=None):
+def call(kernel, grid, in_specs, out_specs, out_shape, scratch=(), cost=None, limit=VMEM_LIMIT):
     return pl.pallas_call(
         kernel,
         grid=grid,
@@ -41,7 +42,7 @@
         out_shape=out_shape,
         scratch_shapes=list(scratch),
         cost_estimate=cost,
-        compiler_params=pltpu.CompilerParams(vmem_limit_bytes=VMEM_LIMIT),
+        compiler_params=pltpu.CompilerParams(vmem_limit_bytes=limit),
     )
 
 
@@ -126,7 +127,7 @@
             bytes_accessed=12 * blocks * head_size * head_size,
             transcendentals=0,
         ),
-        compiler_params=pltpu.CompilerParams(vmem_limit_bytes=VMEM_LIMIT),
+        compiler_params=pltpu.CompilerParams(vmem_limit_bytes=STREAM_LIMIT),
     )(table, stack, stack)
 
 
@@ -199,7 +200,7 @@
         b_ref[at] = backs[at]
 
 
-def advance(gradient, addends, links, weights):
+def advance(gradient, addends, links, weights, ready=(), limit=VMEM_LIMIT):
     rows, chip_width = gradient.shape
     _, cores, double, head_size, _ = weights.shape
     blocks = double // 2
@@ -207,7 +208,9 @@
     block = head_size
     flat = [array for pair in addends for array in pair]
 
-    def kernel(g_ref, low, low_got, high, high_got, m_ref, w_ref, b_ref, out_ref):
+    def kernel(g_ref, low, low_got, high, high_got, m_ref, w_ref, *others):
+        b_ref, out_ref = others[-2:]
+
         @pl.when(pl.program_id(0) == 0)
         def _():
             solve((low, low_got, high, high_got), m_ref, b_ref)
@@ -227,7 +230,8 @@
             pl.BlockSpec(
                 (4, 1, 1, block, head_size), lambda i: (0, i // blocks, i % blocks, 0, 0)
             ),
-        ],
+        ]
+        + [pl.BlockSpec(memory_space=pl.ANY)] * len(ready),
         [
             whole((4, rows, head_size)),
             pl.BlockSpec((rows, block), lambda i: (0, i)),
@@ -241,7 +245,8 @@
             bytes_accessed=8 * chip_width * head_size + 12 * head_size * head_size,
             transcendentals=0,
         ),
-    )(gradient, *flat, links, weights)
+        limit=limit,
+    )(gradient, *flat, links, weights, *ready)
 
 
 def solve_last(addends, links):
@@ -457,7 +462,9 @@
         low = project(gradient, stack, 0)
         addends = addends_over_x((low, high))
         if turn < planes - 1:
-            backs, gradient = advance(gradient, addends, links, stack)
+            ready = (hidden,) if turn == planes - 2 else ()
+            limit = STREAM_LIMIT if turn == 0 else VMEM_LIMIT
+            backs, gradient = advance(gradient, addends, links, stack, ready, limit)
             gradient = lax.ppermute(gradient, "z", [(i, i - 1) for i in range(1, planes)])
             kept_gradient = kept_gradient + gradient
         else:

time: 394 us -> 408 us (1.036)
  Pallas kernels: 52.3 us -> 62.2 us
    all_to_all x1, waiting for transfers between devices: 16.3 us -> 41.4 us  [shards(): lax.all_to_all(sent.reshape(replicas, rows, share + head_size), PLANE, sp...]
    all_gather x1, waiting for transfers between devices: 24.4 us -> 0.01 us  [shards(): hidden = lax.all_gather(hidden, DP, axis=0, tiled=True)]
    pallas_call x3, Pallas kernels: 15.9 us -> 22 us  [advance(): call(kernel, (steps,), [pl.BlockSpec((rows, block), lambda i: (0, i))] +...]
    unnamed x53 -> x83, local copies, waits for them, and re-layouts: 36.9 us -> 39.4 us
  transfers between devices with their start and end apart: 43 -> 43, of which waited for: 37 -> 35; matrix products, arithmetic and copies ran while one was open for 4% -> 4% of each run, Pallas kernels for 3% -> 4%
where the time goes in v4:
time: 408 us; the launch traced here: 406 us
  waiting for transfers between devices  174 us (43%)
  Pallas kernels  62.2 us (15%)
  starting transfers between devices  61.4 us (15%)
  local copies, waits for them, and re-layouts  45.5 us (11%)
  blocking collectives  34.7 us (9%)
  between operations  17.7 us (4%)
  other arithmetic  8.6 us (2%)
    ppermute x22, waiting for transfers between devices, swap(): lax.ppermute(value, axis, [(i, i ^ mask) for i in range(lax.axis_size(axi...  57.7 us
    all_to_all x1, waiting for transfers between devices, shards(): lax.all_to_all(sent.reshape(replicas, rows, share + head_size), PLANE, sp...  41.4 us
    unnamed x83, local copies, waits for them, and re-layouts  39.4 us
    ppermute x3, waiting for transfers between devices, shards(): lax.ppermute(gradient, 'z', [(i, i - 1) for i in range(1, planes)])  37.5 us
    all_to_all x1, blocking collectives, shards(): picked = lax.all_to_all(picked, DP, split_axis=1, concat_axis=0, tiled=True)  34.7 us
    ppermute x22, starting transfers between devices, swap(): lax.ppermute(value, axis, [(i, i ^ mask) for i in range(lax.axis_size(axi...  30.9 us
    pallas_call x3, Pallas kernels, advance(): call(kernel, (steps,), [pl.BlockSpec((rows, block), lambda i: (0, i))] +...  22 us
    ppermute x12, waiting for transfers between devices, turn_by(): lax.ppermute(value, axis, [(i, (i + steps) % count) for i in range(count)])  19.1 us
  transfers between devices with their start and end apart: 43, of which 35 were waited for; matrix products, arithmetic and copies ran while one was open for 4% of the time, Pallas kernels for 4%

profile of v4, /device:TPU:0, one launch (start us, length us, event | category | flops | bytes accessed | tf_op | source)
XLA Modules:
  0.0 406.5 jit_solution(2998428779549611954)
XLA Ops:
  13.6 2.2 gather_fusion
  15.8 3.3 copy.17
  19.1 2.7 fusion
  21.9 34.7 %all_to_all.26 = bf16[144,8,1024]{2,0,1:T(8,128)(2,1)S(1)} all-to-all(bf16[144,8,1024]{2,0,1:T(8,128)(2,1)S(1)} %fusion), channel_id=1, replica_groups=mesh['z'=4,'y'=4,'x'=4,'core'=2] {'x','core'}, dimensions={1} | all-to-all | bytes 4718592 | tf_op jit(solution)/shard_map/all_to_all | solution.py:438
  56.5 2.4 convolution_convert_fusion
  59.0 3.7 all-to-all-start.1
  63.8 6.1 %collective-permute-start = (bf16[144,2048]{1,0:T(8,128)(2,1)S(1)}, bf16[144,2048]{1,0:T(8,128)(2,1)S(1)}, u32[]{:S(2)}, u32[]{:S(2)}) collective-permute-start(bf16[144,2048]{1,0:T(8,128)(2,1)S(1)} %constant_dynamic-slice_fusion), channel_id=1, source_target_pairs={{0,96},{32,98},{64,100},{96,102},{10,104},{42,106},{74,108},{106,1... | collective-permute-start | bytes 1769480 | tf_op jit(solution)/shard_map/ppermute | solution.py:430
  71.2 2.0 collective-permute-start.2
  73.9 4.7 %collective-permute-done.4 = f32[8,128]{1,0:T(8,128)S(1)} collective-permute-done((f32[8,128]{1,0:T(8,128)S(1)}, f32[8,128]{1,0:T(8,128)S(1)}, u32[]{:S(2)}, u32[]{:S(2)}) %collective-permute-start.4) | collective-permute-done | bytes 4128 | tf_op jit(solution)/shard_map/ppermute | solution.py:59
  82.9 16.3 %all-gather.8.cloned.1.call-done = bf16[32,512,512]{2,1,0:T(8,128)(2,1)} async-done(((bf16[4,512,512]{2,1,0:T(8,128)(2,1)}), bf16[32,512,512]{2,1,0:T(8,128)(2,1)}) %all-gather.8.cloned.1.call-update) | async-done | bytes 16777232 | tf_op jit(solution)/shard_map/all_gather | solution.py:420
  99.1 7.8 %shard_map.142 = bf16[6,64,512]{2,1,0:T(8,128)(2,1)} custom-call(s32[13]{0:T(128)} %pad_add_fusion.table_ref, bf16[4,2,4,512,512]{4,3,2,1,0:T(8,128)(2,1)} %bitcast.30, bf16[4,2,4,512,512]{4,3,2,1,0:T(8,128)(2,1)} %bitcast.31), custom_call_target="tpu_custom_call" | custom-call | flops 805306368 | bytes 6291456 | tf_op jit(solution)/shard_map/pallas_call | solution.py:107
  109.5 2.1 collective-permute-start.11
  111.6 3.5 collective-permute-done.9
  115.1 2.4 collective-permute-done.11
  118.6 2.2 collective-permute-start.10
  120.8 5.1 %collective-permute-done.10 = bf16[3,64,512]{2,1,0:T(8,128)(2,1)S(1)} collective-permute-done((bf16[3,64,512]{2,1,0:T(8,128)(2,1)S(1)}, bf16[3,64,512]{2,1,0:T(8,128)(2,1)S(1)}, u32[]{:S(2)}, u32[]{:S(2)}) %collective-permute-start.10) | collective-permute-done | bytes 196640 | tf_op jit(solution)/shard_map/ppermute | solution.py:54
  127.4 5.8 %copy-done.2 = bf16[32,512,512]{2,1,0:T(8,128)(2,1)S(1)} copy-done((bf16[32,512,512]{2,1,0:T(8,128)(2,1)S(1)}, bf16[32,512,512]{2,1,0:T(8,128)(2,1)}, u32[]{:S(2)}) %copy-start.2) | copy-done | bytes 16777240
  133.1 2.0 shard_map.140
  135.5 2.0 shard_map.141
  138.8 3.3 collective-permute-done.5
  142.2 2.0 collective-permute-start.6
  144.2 3.6 collective-permute-done.7
  149.3 2.6 collective-permute-done.6.low_got
  151.9 2.8 collective-permute-done.8.high_got
  155.4 9.3 %shard_map.143 = (bf16[4,144,512]{2,1,0:T(8,128)(2,1)}, bf16[144,2048]{1,0:T(8,128)(2,1)}) custom-call(bf16[144,2048]{1,0:T(8,128)(2,1)} %copy-done.13, bf16[144,1024]{1,0:T(8,128)(2,1)} %copy-done.29, bf16[144,1024]{1,0:T(8,128)(2,1)} %copy-done.32, bf16[144,1024]{1,0:T(8,128)(2,1)} %copy-done.30, bf16[144,1024]{1,0:T(8,128)(2,1)} %copy-done.33, ...), custom_call_target="tpu_custom_call" | custom-call | flops 1660944384 | bytes 11534336 | tf_op jit(solution)/shard_map/pallas_call | solution.py:223
  166.0 15.3 %collective-permute-done.13.g_ref = bf16[144,2048]{1,0:T(8,128)(2,1)S(1)} collective-permute-done((bf16[144,2048]{1,0:T(8,128)(2,1)}, bf16[144,2048]{1,0:T(8,128)(2,1)S(1)}, u32[]{:S(2)}, u32[]{:S(2)}) %collective-permute-start.13) | collective-permute-done | bytes 589856 | tf_op jit(solution)/shard_map/ppermute | solution.py:468
  181.3 5.8 %copy-done.3 = bf16[32,512,512]{2,1,0:T(8,128)(2,1)S(1)} copy-done((bf16[32,512,512]{2,1,0:T(8,128)(2,1)S(1)}, bf16[32,512,512]{2,1,0:T(8,128)(2,1)}, u32[]{:S(2)}) %copy-start.3) | copy-done | bytes 16777240
  187.1 2.0 shard_map.144
  190.6 2.0 shard_map.145
  192.6 2.1 collective-permute-start.16
  196.5 3.8 collective-permute-start.15
  200.3 2.0 collective-permute-done.16
  204.1 3.4 collective-permute-done.15.low_got
  207.5 2.7 collective-permute-done.17.high_got
  210.2 6.0 %copy-done.4 = bf16[32,512,512]{2,1,0:T(8,128)(2,1)S(1)} copy-done((bf16[32,512,512]{2,1,0:T(8,128)(2,1)S(1)}, bf16[32,512,512]{2,1,0:T(8,128)(2,1)}, u32[]{:S(2)}) %copy-start.4) | copy-done | bytes 16777240
  217.2 6.3 %shard_map.146 = (bf16[4,144,512]{2,1,0:T(8,128)(2,1)S(1)}, bf16[144,2048]{1,0:T(8,128)(2,1)S(1)}) custom-call(bf16[144,2048]{1,0:T(8,128)(2,1)S(1)} %copy-done.16, bf16[144,1024]{1,0:T(8,128)(2,1)S(1)} %add_convert_fusion.5.low, bf16[144,1024]{1,0:T(8,128)(2,1)} %collective-permute-done.15.low_got, bf16[144,1024]{1,0:T(8,128)(2,1)} %add_convert_fusion.4.high, ...), custom_call_target="tpu_custom_call" | custom-call | flops 1660944384 | bytes 11534336 | tf_op jit(solution)/shard_map/pallas_call | solution.py:223
  224.9 11.8 %collective-permute-done.18.g_ref = bf16[144,2048]{1,0:T(8,128)(2,1)S(1)} collective-permute-done((bf16[144,2048]{1,0:T(8,128)(2,1)S(1)}, bf16[144,2048]{1,0:T(8,128)(2,1)S(1)}, u32[]{:S(2)}, u32[]{:S(2)}) %collective-permute-start.18) | collective-permute-done | bytes 589856 | tf_op jit(solution)/shard_map/ppermute | solution.py:468
  236.6 2.0 shard_map.147
  239.5 2.0 shard_map.148
  241.5 2.1 collective-permute-start.21
  245.5 2.5 collective-permute-start.20
  250.7 3.0 collective-permute-done.20.low_got
  253.6 3.8 collective-permute-done.22.high_got
  257.5 5.8 %copy-done.5 = bf16[32,512,512]{2,1,0:T(8,128)(2,1)S(1)} copy-done((bf16[32,512,512]{2,1,0:T(8,128)(2,1)S(1)}, bf16[32,512,512]{2,1,0:T(8,128)(2,1)}, u32[]{:S(2)}) %copy-start.5) | copy-done | bytes 16777240
  265.6 6.3 %shard_map.149 = (bf16[4,144,512]{2,1,0:T(8,128)(2,1)S(1)}, bf16[144,2048]{1,0:T(8,128)(2,1)S(1)}) custom-call(bf16[144,2048]{1,0:T(8,128)(2,1)S(1)} %copy-done.9, bf16[144,1024]{1,0:T(8,128)(2,1)S(1)} %add_convert_fusion.3.low, bf16[144,1024]{1,0:T(8,128)(2,1)} %collective-permute-done.20.low_got, bf16[144,1024]{1,0:T(8,128)(2,1)} %add_convert_fusion.2.high, ...), custom_call_target="tpu_custom_call" | custom-call | flops 1660944384 | bytes 11534336 | tf_op jit(solution)/shard_map/pallas_call | solution.py:223
  273.2 10.5 %collective-permute-done.23.g_ref = bf16[144,2048]{1,0:T(8,128)(2,1)S(1)} collective-permute-done((bf16[144,2048]{1,0:T(8,128)(2,1)S(1)}, bf16[144,2048]{1,0:T(8,128)(2,1)S(1)}, u32[]{:S(2)}, u32[]{:S(2)}) %collective-permute-start.23) | collective-permute-done | bytes 589856 | tf_op jit(solution)/shard_map/ppermute | solution.py:468
  283.7 2.0 shard_map.150
  286.0 2.0 shard_map.151
  288.0 2.5 collective-permute-start.26
  290.4 5.2 %collective-permute-done.24 = bf16[144,1024]{1,0:T(8,128)(2,1)S(1)} collective-permute-done((bf16[144,1024]{1,0:T(8,128)(2,1)S(1)}, bf16[144,1024]{1,0:T(8,128)(2,1)S(1)}, u32[]{:S(2)}, u32[]{:S(2)}) %collective-permute-start.24) | collective-permute-done | bytes 294944 | tf_op jit(solution)/shard_map/ppermute | solution.py:54
  295.7 2.4 collective-permute-start.25
  298.7 5.0 %collective-permute-done.25.low_got = bf16[144,1024]{1,0:T(8,128)(2,1)S(1)} collective-permute-done((bf16[144,1024]{1,0:T(8,128)(2,1)S(1)}, bf16[144,1024]{1,0:T(8,128)(2,1)S(1)}, u32[]{:S(2)}, u32[]{:S(2)}) %collective-permute-start.25) | collective-permute-done | bytes 294944 | tf_op jit(solution)/shard_map/ppermute | solution.py:54
  306.7 3.8 shard_map.153
  312.3 3.7 all-to-all-start.2
  317.1 41.4 %all-to-all-done.2 = bf16[8,144,1536]{2,1,0:T(8,128)(2,1)S(1)} async-done(((bf16[8,144,1536]{2,1,0:T(8,128)(2,1)}), bf16[8,144,1536]{2,1,0:T(8,128)(2,1)S(1)}, u32[]{:S(2)}, u32[]{:S(2)}) %all-to-all-start.2) | async-done | bytes 3538976 | tf_op jit(solution)/shard_map/all_to_all | solution.py:475
  361.5 4.9 %shard_map.154 = (f32[1024,1024]{1,0:T(8,128)S(1)}, f32[8,128]{1,0:T(8,128)S(1)}) custom-call(f32[1]{0:T(128)} %bitcast.13.count_ref, bf16[1152,1024]{1,0:T(8,128)(2,1)S(1)} %bitcast.54, bf16[1152,1536]{1,0:T(8,128)(2,1)S(1)} %bitcast.50, bf16[1152,1536]{1,0:T(8,128)(2,1)S(1)} %bitcast.51, bf16[1152,512]{1,0:T(8,128)(2,1)S(1)} %copy-done.20), custom_call_target="tpu_custom_call" | custom-call | flops 2415919104 | bytes 11272192 | tf_op jit(solution)/shard_map/pallas_call | solution.py:339
  368.1 2.3 collective-permute-start.30
  370.4 2.4 collective-permute-done.31
  372.8 2.4 collective-permute-done.29
  375.5 2.9 collective-permute-start.33
  380.3 2.9 collective-permute-done.32
  383.2 3.2 collective-permute-start.37
  390.0 2.3 collective-permute-done.35
  393.6 6.3 %shard_map.155 = (f32[1,1024,1024]{2,1,0:T(8,128)}, bf16[1,1024,1024]{2,1,0:T(8,128)(2,1)}, bf16[1,1024,1024]{2,1,0:T(8,128)(2,1)}) custom-call(f32[1]{0:T(128)S(6)} %min.3.factor_ref, f32[1024,1024]{1,0:T(8,128)S(1)} %get-tuple-element.26.grad_ref, f32[1,1024,1024]{2,1,0:T(8,128)S(1)} %copy-done.21, bf16[1,1024,1024]{2,1,0:T(8,128)(2,1)S(1)} %copy-done.22, ...), custom_call_target="tpu_custom_call" | custom-call | flops 20971520 | bytes 20971520 | tf_op jit(solution)/shard_map/pallas_call | solution.py:383
  (163 shorter events, 55.7 us)
Async XLA Ops:
  7.2 6.5 %copy-start = (bf16[1,3,48,8192]{3,2,1,0:T(8,128)(2,1)S(1)}, bf16[1,3,48,8192]{3,2,1,0:T(8,128)(2,1)}, u32[]{:S(2)}) copy-start(bf16[1,3,48,8192]{3,2,1,0:T(8,128)(2,1)} %param.12) | copy-start | bytes 7077892
  7.2 91.9 %all-gather.8.cloned.1.call-start = ((), (), s32[]{:S(2)}) async-start(), calls=%async_computation.4 | async-start | bytes 18874368 | tf_op jit(solution)/shard_map/all_gather | solution.py:420
  21.8 34.7 %copy-start.26 = (bf16[1,1024,512]{2,1,0:T(8,128)(2,1)S(1)}, bf16[1,1024,512]{2,1,0:T(8,128)(2,1)}, u32[]{:S(2)}) copy-start(bf16[1,1024,512]{2,1,0:T(8,128)(2,1)} %param.14) | copy-start | bytes 3145732
  58.9 14.3 %copy-start.36 = (s32[12]{0:T(128)S(1)}, s32[12]{0:T(128)}, u32[]{:S(2)}) copy-start(s32[12]{0:T(128)} %constant.56.clone) | copy-start | bytes 148
  59.0 21.2 %all-to-all-start.1 = ((bf16[8,144,512]{2,1,0:T(8,128)(2,1)}), bf16[8,144,512]{2,1,0:T(8,128)(2,1)S(1)}, u32[]{:S(2)}, u32[]{:S(2)}) async-start(bf16[8,144,512]{2,1,0:T(8,128)(2,1)} %bitcast.11), calls=%async_computation.1 | async-start | bytes 2359296 | tf_op jit(solution)/shard_map/all_to_all | solution.py:441
  62.7 92.1 %all-gather.10.cloned.1.call-start = ((), (), s32[]{:S(2)}) async-start(), calls=%async_computation.5 | async-start | bytes 3538944 | tf_op jit(solution)/shard_map/all_gather | solution.py:457
  63.8 19.0 %collective-permute-start = (bf16[144,2048]{1,0:T(8,128)(2,1)S(1)}, bf16[144,2048]{1,0:T(8,128)(2,1)S(1)}, u32[]{:S(2)}, u32[]{:S(2)}) collective-permute-start(bf16[144,2048]{1,0:T(8,128)(2,1)S(1)} %constant_dynamic-slice_fusion), channel_id=1, source_target_pairs={{0,96},{32,98},{64,100},{96,102},{10,104},{42,106},{74,108},{106,1... | collective-permute-start | bytes 1769480 | tf_op jit(solution)/shard_map/ppermute | solution.py:430
  69.9 1.2 collective-permute-start.1
  71.2 7.4 %collective-permute-start.4 = (f32[8,128]{1,0:T(8,128)S(1)}, f32[8,128]{1,0:T(8,128)S(1)}, u32[]{:S(2)}, u32[]{:S(2)}) collective-permute-start(f32[8,128]{1,0:T(8,128)S(1)} %broadcast_add_fusion), channel_id=1, source_target_pairs={{0,6},{2,0},{4,2},{6,4},{1,7},{3,1},{5,3},{7,5},{8,14},{10,8},{12,... | collective-permute-start | bytes 12296 | tf_op jit(solution)/shard_map/ppermute | solution.py:59
  71.2 8.9 %collective-permute-start.3 = (f32[8,128]{1,0:T(8,128)S(1)}, f32[8,128]{1,0:T(8,128)S(1)}, u32[]{:S(2)}, u32[]{:S(2)}) collective-permute-start(f32[8,128]{1,0:T(8,128)S(1)} %broadcast_add_fusion), channel_id=1, source_target_pairs={{0,4},{2,6},{4,0},{6,2},{1,5},{3,7},{5,1},{7,3},{8,12},{10,14},{12... | collective-permute-start | bytes 12296 | tf_op jit(solution)/shard_map/ppermute | solution.py:59
  71.2 8.9 %collective-permute-start.2 = (f32[8,128]{1,0:T(8,128)S(1)}, f32[8,128]{1,0:T(8,128)S(1)}, u32[]{:S(2)}, u32[]{:S(2)}) collective-permute-start(f32[8,128]{1,0:T(8,128)S(1)} %broadcast_add_fusion), channel_id=1, source_target_pairs={{0,2},{2,4},{4,6},{6,0},{1,3},{3,5},{5,7},{7,1},{8,10},{10,12},{12... | collective-permute-start | bytes 12296 | tf_op jit(solution)/shard_map/ppermute | solution.py:59
  82.9 52.6 %copy-start.13 = (bf16[144,2048]{1,0:T(8,128)(2,1)}, bf16[144,2048]{1,0:T(8,128)(2,1)S(1)}, u32[]{:S(2)}) copy-start(bf16[144,2048]{1,0:T(8,128)(2,1)S(1)} %collective-permute-done.g_ref) | copy-start | bytes 1769476
  108.0 7.1 %collective-permute-start.9 = (bf16[3,64,512]{2,1,0:T(8,128)(2,1)S(1)}, bf16[3,64,512]{2,1,0:T(8,128)(2,1)S(1)}, u32[]{:S(2)}, u32[]{:S(2)}) collective-permute-start(bf16[3,64,512]{2,1,0:T(8,128)(2,1)S(1)} %get-tuple-element.29), channel_id=1, source_target_pairs={{0,2},{2,0},{4,6},{6,4},{1,3},{3,1},{5,7},{7,5},{8,10},{10,8},{12,... | collective-permute-start | bytes 589832 | tf_op jit(solution)/shard_map/ppermute | solution.py:54
  109.5 8.0 %collective-permute-start.11 = (bf16[3,64,512]{2,1,0:T(8,128)(2,1)S(1)}, bf16[3,64,512]{2,1,0:T(8,128)(2,1)S(1)}, u32[]{:S(2)}, u32[]{:S(2)}) collective-permute-start(bf16[3,64,512]{2,1,0:T(8,128)(2,1)S(1)} %get-tuple-element.30), channel_id=1, source_target_pairs={{0,6},{2,4},{4,2},{6,0},{1,7},{3,5},{5,3},{7,1},{8,14},{10,12},{12... | collective-permute-start | bytes 589832 | tf_op jit(solution)/shard_map/ppermute | solution.py:54
  118.6 7.2 %collective-permute-start.10 = (bf16[3,64,512]{2,1,0:T(8,128)(2,1)S(1)}, bf16[3,64,512]{2,1,0:T(8,128)(2,1)S(1)}, u32[]{:S(2)}, u32[]{:S(2)}) collective-permute-start(bf16[3,64,512]{2,1,0:T(8,128)(2,1)S(1)} %get-tuple-element.27), channel_id=1, source_target_pairs={{0,6},{2,4},{4,2},{6,0},{1,7},{3,5},{5,3},{7,1},{8,14},{10,12},{12... | collective-permute-start | bytes 589832 | tf_op jit(solution)/shard_map/ppermute | solution.py:54
  120.8 5.7 %collective-permute-start.12 = (bf16[3,64,512]{2,1,0:T(8,128)(2,1)S(1)}, bf16[3,64,512]{2,1,0:T(8,128)(2,1)S(1)}, u32[]{:S(2)}, u32[]{:S(2)}) collective-permute-start(bf16[3,64,512]{2,1,0:T(8,128)(2,1)S(1)} %get-tuple-element.28), channel_id=1, source_target_pairs={{0,2},{2,0},{4,6},{6,4},{1,3},{3,1},{5,7},{7,5},{8,10},{10,8},{12,... | collective-permute-start | bytes 589832 | tf_op jit(solution)/shard_map/ppermute | solution.py:54
  127.3 123.3 %all-gather.6.cloned.1.call-start = ((), (), s32[]{:S(2)}) async-start(), calls=%async_computation.3 | async-start | bytes 1327104 | tf_op jit(solution)/shard_map/all_gather | solution.py:447
  135.1 7.0 %collective-permute-start.5 = (bf16[144,1024]{1,0:T(8,128)(2,1)S(1)}, bf16[144,1024]{1,0:T(8,128)(2,1)S(1)}, u32[]{:S(2)}, u32[]{:S(2)}) collective-permute-start(bf16[144,1024]{1,0:T(8,128)(2,1)S(1)} %shard_map.140), channel_id=1, source_target_pairs={{0,2},{2,0},{4,6},{6,4},{1,3},{3,1},{5,7},{7,5},{8,10},{10,8},{12,... | collective-permute-start | bytes 884744 | tf_op jit(solution)/shard_map/ppermute | solution.py:54
  137.5 10.4 %collective-permute-start.7 = (bf16[144,1024]{1,0:T(8,128)(2,1)S(1)}, bf16[144,1024]{1,0:T(8,128)(2,1)S(1)}, u32[]{:S(2)}, u32[]{:S(2)}) collective-permute-start(bf16[144,1024]{1,0:T(8,128)(2,1)S(1)} %shard_map.141), channel_id=1, source_target_pairs={{0,6},{2,4},{4,2},{6,0},{1,7},{3,5},{5,3},{7,1},{8,14},{10,12},{12... | collective-permute-start | bytes 884744 | tf_op jit(solution)/shard_map/ppermute | solution.py:54
  142.2 12.6 %copy-start.29 = (bf16[144,1024]{1,0:T(8,128)(2,1)}, bf16[144,1024]{1,0:T(8,128)(2,1)S(1)}, u32[]{:S(2)}) copy-start(bf16[144,1024]{1,0:T(8,128)(2,1)S(1)} %add_convert_fusion.7.low) | copy-start | bytes 884740
  142.2 9.7 %collective-permute-start.6 = (bf16[144,1024]{1,0:T(8,128)(2,1)S(1)}, bf16[144,1024]{1,0:T(8,128)(2,1)S(1)}, u32[]{:S(2)}, u32[]{:S(2)}) collective-permute-start(bf16[144,1024]{1,0:T(8,128)(2,1)S(1)} %add_convert_fusion.7.low), channel_id=1, source_target_pairs={{0,6},{2,4},{4,2},{6,0},{1,7},{3,5},{5,3},{7,1},{8,14},{10,12},{12... | collective-permute-start | bytes 884744 | tf_op jit(solution)/shard_map/ppermute | solution.py:54
  147.9 6.8 %copy-start.30 = (bf16[144,1024]{1,0:T(8,128)(2,1)}, bf16[144,1024]{1,0:T(8,128)(2,1)S(1)}, u32[]{:S(2)}) copy-start(bf16[144,1024]{1,0:T(8,128)(2,1)S(1)} %add_convert_fusion.6.high) | copy-start | bytes 884740
  147.9 6.8 %collective-permute-start.8 = (bf16[144,1024]{1,0:T(8,128)(2,1)S(1)}, bf16[144,1024]{1,0:T(8,128)(2,1)S(1)}, u32[]{:S(2)}, u32[]{:S(2)}) collective-permute-start(bf16[144,1024]{1,0:T(8,128)(2,1)S(1)} %add_convert_fusion.6.high), channel_id=1, source_target_pairs={{0,2},{2,0},{4,6},{6,4},{1,3},{3,1},{5,7},{7,5},{8,10},{10,8},{12,... | collective-permute-start | bytes 884744 | tf_op jit(solution)/shard_map/ppermute | solution.py:54
  164.8 16.6 %collective-permute-start.13 = (bf16[144,2048]{1,0:T(8,128)(2,1)}, bf16[144,2048]{1,0:T(8,128)(2,1)S(1)}, u32[]{:S(2)}, u32[]{:S(2)}) collective-permute-start(bf16[144,2048]{1,0:T(8,128)(2,1)} %get-tuple-element.18), channel_id=1, source_target_pairs={{32,0},{64,32},{96,64},{33,1},{65,33},{97,65},{34,2},{66,34},{98,6... | collective-permute-start | bytes 1769480 | tf_op jit(solution)/shard_map/ppermute | solution.py:468
  189.1 7.3 %collective-permute-start.14 = (bf16[144,1024]{1,0:T(8,128)(2,1)S(1)}, bf16[144,1024]{1,0:T(8,128)(2,1)S(1)}, u32[]{:S(2)}, u32[]{:S(2)}) collective-permute-start(bf16[144,1024]{1,0:T(8,128)(2,1)S(1)} %shard_map.144), channel_id=1, source_target_pairs={{0,2},{2,0},{4,6},{6,4},{1,3},{3,1},{5,7},{7,5},{8,10},{10,8},{12,... | collective-permute-start | bytes 884744 | tf_op jit(solution)/shard_map/ppermute | solution.py:54
  190.6 19.5 %copy-start.6 = (bf16[48,64,512]{2,1,0:T(8,128)(2,1)S(1)}, bf16[48,64,512]{2,1,0:T(8,128)(2,1)}, u32[]{:S(2)}) copy-start(bf16[48,64,512]{2,1,0:T(8,128)(2,1)} %all-gather.10.cloned.1.call-done) | copy-start | bytes 9437188
  192.6 9.7 %collective-permute-start.16 = (bf16[144,1024]{1,0:T(8,128)(2,1)S(1)}, bf16[144,1024]{1,0:T(8,128)(2,1)S(1)}, u32[]{:S(2)}, u32[]{:S(2)}) collective-permute-start(bf16[144,1024]{1,0:T(8,128)(2,1)S(1)} %shard_map.145), channel_id=1, source_target_pairs={{0,6},{2,4},{4,2},{6,0},{1,7},{3,5},{5,3},{7,1},{8,14},{10,12},{12... | collective-permute-start | bytes 884744 | tf_op jit(solution)/shard_map/ppermute | solution.py:54
  196.5 11.0 %collective-permute-start.15 = (bf16[144,1024]{1,0:T(8,128)(2,1)S(1)}, bf16[144,1024]{1,0:T(8,128)(2,1)}, u32[]{:S(2)}, u32[]{:S(2)}) collective-permute-start(bf16[144,1024]{1,0:T(8,128)(2,1)S(1)} %add_convert_fusion.5.low), channel_id=1, source_target_pairs={{0,6},{2,4},{4,2},{6,0},{1,7},{3,5},{5,3},{7,1},{8,14},{10,12},{12... | collective-permute-start | bytes 884744 | tf_op jit(solution)/shard_map/ppermute | solution.py:54
  203.1 7.0 %collective-permute-start.17 = (bf16[144,1024]{1,0:T(8,128)(2,1)}, bf16[144,1024]{1,0:T(8,128)(2,1)}, u32[]{:S(2)}, u32[]{:S(2)}) collective-permute-start(bf16[144,1024]{1,0:T(8,128)(2,1)} %add_convert_fusion.4.high), channel_id=1, source_target_pairs={{0,2},{2,0},{4,6},{6,4},{1,3},{3,1},{5,7},{7,5},{8,10},{10,8},{12,... | collective-permute-start | bytes 884744 | tf_op jit(solution)/shard_map/ppermute | solution.py:54
  223.6 15.1 %copy-start.27 = (bf16[4,144,512]{2,1,0:T(8,128)(2,1)}, bf16[4,144,512]{2,1,0:T(8,128)(2,1)S(1)}, u32[]{:S(2)}) copy-start(bf16[4,144,512]{2,1,0:T(8,128)(2,1)S(1)} %get-tuple-element.23) | copy-start | bytes 1769476
  223.6 13.1 %collective-permute-start.18 = (bf16[144,2048]{1,0:T(8,128)(2,1)S(1)}, bf16[144,2048]{1,0:T(8,128)(2,1)S(1)}, u32[]{:S(2)}, u32[]{:S(2)}) collective-permute-start(bf16[144,2048]{1,0:T(8,128)(2,1)S(1)} %get-tuple-element.19), channel_id=1, source_target_pairs={{32,0},{64,32},{96,64},{33,1},{65,33},{97,65},{34,2},{66,34},{98,6... | collective-permute-start | bytes 1769480 | tf_op jit(solution)/shard_map/ppermute | solution.py:468
  238.6 6.8 %collective-permute-start.19 = (bf16[144,1024]{1,0:T(8,128)(2,1)S(1)}, bf16[144,1024]{1,0:T(8,128)(2,1)S(1)}, u32[]{:S(2)}, u32[]{:S(2)}) collective-permute-start(bf16[144,1024]{1,0:T(8,128)(2,1)S(1)} %shard_map.147), channel_id=1, source_target_pairs={{0,2},{2,0},{4,6},{6,4},{1,3},{3,1},{5,7},{7,5},{8,10},{10,8},{12,... | collective-permute-start | bytes 884744 | tf_op jit(solution)/shard_map/ppermute | solution.py:54
  241.5 8.1 %collective-permute-start.21 = (bf16[144,1024]{1,0:T(8,128)(2,1)S(1)}, bf16[144,1024]{1,0:T(8,128)(2,1)S(1)}, u32[]{:S(2)}, u32[]{:S(2)}) collective-permute-start(bf16[144,1024]{1,0:T(8,128)(2,1)S(1)} %shard_map.148), channel_id=1, source_target_pairs={{0,6},{2,4},{4,2},{6,0},{1,7},{3,5},{5,3},{7,1},{8,14},{10,12},{12... | collective-permute-start | bytes 884744 | tf_op jit(solution)/shard_map/ppermute | solution.py:54
  245.5 8.1 %collective-permute-start.20 = (bf16[144,1024]{1,0:T(8,128)(2,1)S(1)}, bf16[144,1024]{1,0:T(8,128)(2,1)}, u32[]{:S(2)}, u32[]{:S(2)}) collective-permute-start(bf16[144,1024]{1,0:T(8,128)(2,1)S(1)} %add_convert_fusion.3.low), channel_id=1, source_target_pairs={{0,6},{2,4},{4,2},{6,0},{1,7},{3,5},{5,3},{7,1},{8,14},{10,12},{12... | collective-permute-start | bytes 884744 | tf_op jit(solution)/shard_map/ppermute | solution.py:54
  250.4 7.0 %collective-permute-start.22 = (bf16[144,1024]{1,0:T(8,128)(2,1)}, bf16[144,1024]{1,0:T(8,128)(2,1)}, u32[]{:S(2)}, u32[]{:S(2)}) collective-permute-start(bf16[144,1024]{1,0:T(8,128)(2,1)} %add_convert_fusion.2.high), channel_id=1, source_target_pairs={{0,2},{2,0},{4,6},{6,4},{1,3},{3,1},{5,7},{7,5},{8,10},{10,8},{12,... | collective-permute-start | bytes 884744 | tf_op jit(solution)/shard_map/ppermute | solution.py:54
  271.9 11.8 %collective-permute-start.23 = (bf16[144,2048]{1,0:T(8,128)(2,1)S(1)}, bf16[144,2048]{1,0:T(8,128)(2,1)S(1)}, u32[]{:S(2)}, u32[]{:S(2)}) collective-permute-start(bf16[144,2048]{1,0:T(8,128)(2,1)S(1)} %get-tuple-element.21), channel_id=1, source_target_pairs={{32,0},{64,32},{96,64},{33,1},{65,33},{97,65},{34,2},{66,34},{98,6... | collective-permute-start | bytes 1769480 | tf_op jit(solution)/shard_map/ppermute | solution.py:468
  285.6 12.9 %copy-start.10 = (bf16[144,2048]{1,0:T(8,128)(2,1)S(1)}, bf16[144,2048]{1,0:T(8,128)(2,1)}, u32[]{:S(2)}) copy-start(bf16[144,2048]{1,0:T(8,128)(2,1)} %copy-done.8) | copy-start | bytes 1769476
  285.7 12.9 %copy-start.14 = (bf16[144,2048]{1,0:T(8,128)(2,1)S(1)}, bf16[144,2048]{1,0:T(8,128)(2,1)}, u32[]{:S(2)}) copy-start(bf16[144,2048]{1,0:T(8,128)(2,1)} %copy-done.13) | copy-start | bytes 1769476
  285.7 12.9 %copy-start.17 = (bf16[144,2048]{1,0:T(8,128)(2,1)S(1)}, bf16[144,2048]{1,0:T(8,128)(2,1)}, u32[]{:S(2)}) copy-start(bf16[144,2048]{1,0:T(8,128)(2,1)} %copy-done.15) | copy-start | bytes 1769476
  285.7 9.9 %collective-permute-start.24 = (bf16[144,1024]{1,0:T(8,128)(2,1)S(1)}, bf16[144,1024]{1,0:T(8,128)(2,1)S(1)}, u32[]{:S(2)}, u32[]{:S(2)}) collective-permute-start(bf16[144,1024]{1,0:T(8,128)(2,1)S(1)} %shard_map.150), channel_id=1, source_target_pairs={{0,2},{2,0},{4,6},{6,4},{1,3},{3,1},{5,7},{7,5},{8,10},{10,8},{12,... | collective-permute-start | bytes 884744 | tf_op jit(solution)/shard_map/ppermute | solution.py:54
  286.0 20.7 %slice-start = ((s8[16777216]{0:T(1024)(128)(4,1)}), s8[4194304]{0:T(1024)(128)(4,1)S(1)}, s32[]{:S(2)}) async-start(s8[16777216]{0:T(1024)(128)(4,1)} %bitcast.43), calls=%async_computation.6 | async-start | bytes 8388608
  286.0 20.7 %slice-start.1 = ((s8[16777216]{0:T(1024)(128)(4,1)}), s8[4194304]{0:T(1024)(128)(4,1)S(1)}, s32[]{:S(2)}) async-start(s8[16777216]{0:T(1024)(128)(4,1)} %bitcast.43), calls=%async_computation.7 | async-start | bytes 8388608
  286.0 20.7 %slice-start.2 = ((s8[16777216]{0:T(1024)(128)(4,1)}), s8[4194304]{0:T(1024)(128)(4,1)S(1)}, s32[]{:S(2)}) async-start(s8[16777216]{0:T(1024)(128)(4,1)} %bitcast.43), calls=%async_computation.8 | async-start | bytes 8388608
  288.0 10.2 %collective-permute-start.26 = (bf16[144,1024]{1,0:T(8,128)(2,1)S(1)}, bf16[144,1024]{1,0:T(8,128)(2,1)S(1)}, u32[]{:S(2)}, u32[]{:S(2)}) collective-permute-start(bf16[144,1024]{1,0:T(8,128)(2,1)S(1)} %shard_map.151), channel_id=1, source_target_pairs={{0,6},{2,4},{4,2},{6,0},{1,7},{3,5},{5,3},{7,1},{8,14},{10,12},{12... | collective-permute-start | bytes 884744 | tf_op jit(solution)/shard_map/ppermute | solution.py:54
  295.7 8.0 %collective-permute-start.25 = (bf16[144,1024]{1,0:T(8,128)(2,1)S(1)}, bf16[144,1024]{1,0:T(8,128)(2,1)S(1)}, u32[]{:S(2)}, u32[]{:S(2)}) collective-permute-start(bf16[144,1024]{1,0:T(8,128)(2,1)S(1)} %add_convert_fusion.1.low), channel_id=1, source_target_pairs={{0,6},{2,4},{4,2},{6,0},{1,7},{3,5},{5,3},{7,1},{8,14},{10,12},{12... | collective-permute-start | bytes 884744 | tf_op jit(solution)/shard_map/ppermute | solution.py:54
  298.2 7.0 %collective-permute-start.27 = (bf16[144,1024]{1,0:T(8,128)(2,1)S(1)}, bf16[144,1024]{1,0:T(8,128)(2,1)S(1)}, u32[]{:S(2)}, u32[]{:S(2)}) collective-permute-start(bf16[144,1024]{1,0:T(8,128)(2,1)S(1)} %add_convert_fusion.high), channel_id=1, source_target_pairs={{0,2},{2,0},{4,6},{6,4},{1,3},{3,1},{5,7},{7,5},{8,10},{10,8},{12,... | collective-permute-start | bytes 884744 | tf_op jit(solution)/shard_map/ppermute | solution.py:54
  298.6 7.9 %copy-start.31 = (bf16[4,144,512]{2,1,0:T(8,128)(2,1)S(1)}, bf16[4,144,512]{2,1,0:T(8,128)(2,1)}, u32[]{:S(2)}) copy-start(bf16[4,144,512]{2,1,0:T(8,128)(2,1)} %get-tuple-element.22) | copy-start | bytes 1769476
  298.7 7.8 %copy-start.28 = (bf16[4,144,512]{2,1,0:T(8,128)(2,1)S(1)}, bf16[4,144,512]{2,1,0:T(8,128)(2,1)}, u32[]{:S(2)}) copy-start(bf16[4,144,512]{2,1,0:T(8,128)(2,1)} %copy-done.27) | copy-start | bytes 1769476
  298.7 8.0 %slice-start.3 = ((s8[16777216]{0:T(1024)(128)(4,1)}), s8[4194304]{0:T(1024)(128)(4,1)S(1)}, s32[]{:S(2)}) async-start(s8[16777216]{0:T(1024)(128)(4,1)} %bitcast.43), calls=%async_computation.9 | async-start | bytes 8388608
  312.3 46.2 %all-to-all-start.2 = ((bf16[8,144,1536]{2,1,0:T(8,128)(2,1)}), bf16[8,144,1536]{2,1,0:T(8,128)(2,1)S(1)}, u32[]{:S(2)}, u32[]{:S(2)}) async-start(bf16[8,144,1536]{2,1,0:T(8,128)(2,1)} %bitcast.52), calls=%async_computation.2 | async-start | bytes 7077888 | tf_op jit(solution)/shard_map/all_to_all | solution.py:475
  361.5 32.1 %copy-start.21 = (f32[1,1024,1024]{2,1,0:T(8,128)S(1)}, f32[1,1024,1024]{2,1,0:T(8,128)}, u32[]{:S(2)}) copy-start(f32[1,1024,1024]{2,1,0:T(8,128)} %master_ref.1) | copy-start | bytes 12582916
  361.5 32.1 %copy-start.22 = (bf16[1,1024,1024]{2,1,0:T(8,128)(2,1)S(1)}, bf16[1,1024,1024]{2,1,0:T(8,128)(2,1)}, u32[]{:S(2)}) copy-start(bf16[1,1024,1024]{2,1,0:T(8,128)(2,1)} %one_ref.1) | copy-start | bytes 6291460
  361.5 32.1 %copy-start.23 = (bf16[1,1024,1024]{2,1,0:T(8,128)(2,1)S(1)}, bf16[1,1024,1024]{2,1,0:T(8,128)(2,1)}, u32[]{:S(2)}) copy-start(bf16[1,1024,1024]{2,1,0:T(8,128)(2,1)} %two_ref.1) | copy-start | bytes 6291460
  366.4 1.2 collective-permute-start.28
  367.7 5.1 %collective-permute-start.31 = (f32[8,128]{1,0:T(8,128)S(1)}, f32[8,128]{1,0:T(8,128)S(1)}, u32[]{:S(2)}, u32[]{:S(2)}) collective-permute-start(f32[8,128]{1,0:T(8,128)S(1)} %add.157), channel_id=1, source_target_pairs={{0,4},{2,6},{4,0},{6,2},{1,5},{3,7},{5,1},{7,3},{8,12},{10,14},{12... | collective-permute-start | bytes 12296 | tf_op jit(solution)/shard_map/ppermute | solution.py:59
  368.1 4.7 %collective-permute-start.30 = (f32[8,128]{1,0:T(8,128)S(1)}, f32[8,128]{1,0:T(8,128)S(1)}, u32[]{:S(2)}, u32[]{:S(2)}) collective-permute-start(f32[8,128]{1,0:T(8,128)S(1)} %add.157), channel_id=1, source_target_pairs={{0,6},{2,0},{4,2},{6,4},{1,7},{3,1},{5,3},{7,5},{8,14},{10,8},{12,... | collective-permute-start | bytes 12296 | tf_op jit(solution)/shard_map/ppermute | solution.py:59
  370.4 4.8 %collective-permute-start.29 = (f32[8,128]{1,0:T(8,128)S(1)}, f32[8,128]{1,0:T(8,128)S(1)}, u32[]{:S(2)}, u32[]{:S(2)}) collective-permute-start(f32[8,128]{1,0:T(8,128)S(1)} %add.157), channel_id=1, source_target_pairs={{0,2},{2,4},{4,6},{6,0},{1,3},{3,5},{5,7},{7,1},{8,10},{10,12},{12... | collective-permute-start | bytes 12296 | tf_op jit(solution)/shard_map/ppermute | solution.py:59
  375.2 5.1 %collective-permute-start.34 = (f32[8,128]{1,0:T(8,128)S(1)}, f32[8,128]{1,0:T(8,128)S(1)}, u32[]{:S(2)}, u32[]{:S(2)}) collective-permute-start(f32[8,128]{1,0:T(8,128)S(1)} %add_add_fusion.4), channel_id=1, source_target_pairs={{0,16},{8,24},{16,0},{24,8},{1,17},{9,25},{17,1},{25,9},{2,18},{10... | collective-permute-start | bytes 12296 | tf_op jit(solution)/shard_map/ppermute | solution.py:59
  375.5 4.8 %collective-permute-start.33 = (f32[8,128]{1,0:T(8,128)S(1)}, f32[8,128]{1,0:T(8,128)S(1)}, u32[]{:S(2)}, u32[]{:S(2)}) collective-permute-start(f32[8,128]{1,0:T(8,128)S(1)} %add_add_fusion.4), channel_id=1, source_target_pairs={{0,24},{8,0},{16,8},{24,16},{1,25},{9,1},{17,9},{25,17},{2,26},{10... | collective-permute-start | bytes 12296 | tf_op jit(solution)/shard_map/ppermute | solution.py:59
  378.4 4.8 %collective-permute-start.32 = (f32[8,128]{1,0:T(8,128)S(1)}, f32[8,128]{1,0:T(8,128)S(1)}, u32[]{:S(2)}, u32[]{:S(2)}) collective-permute-start(f32[8,128]{1,0:T(8,128)S(1)} %add_add_fusion.4), channel_id=1, source_target_pairs={{0,8},{8,16},{16,24},{24,0},{1,9},{9,17},{17,25},{25,1},{2,10},{10... | collective-permute-start | bytes 12296 | tf_op jit(solution)/shard_map/ppermute | solution.py:59
  383.2 5.8 %collective-permute-start.37 = (f32[8,128]{1,0:T(8,128)S(1)}, f32[8,128]{1,0:T(8,128)S(1)}, u32[]{:S(2)}, u32[]{:S(2)}) collective-permute-start(f32[8,128]{1,0:T(8,128)S(1)} %add_add_fusion.3), channel_id=1, source_target_pairs={{0,64},{32,96},{64,0},{96,32},{1,65},{33,97},{65,1},{97,33},{2,66}... | collective-permute-start | bytes 12296 | tf_op jit(solution)/shard_map/ppermute | solution.py:59
  386.4 3.6 collective-permute-start.36
  387.5 4.8 %collective-permute-start.35 = (f32[8,128]{1,0:T(8,128)S(1)}, f32[8,128]{1,0:T(8,128)S(1)}, u32[]{:S(2)}, u32[]{:S(2)}) collective-permute-start(f32[8,128]{1,0:T(8,128)S(1)} %add_add_fusion.3), channel_id=1, source_target_pairs={{0,32},{32,64},{64,96},{96,0},{1,33},{33,65},{65,97},{97,1},{2,34}... | collective-permute-start | bytes 12296 | tf_op jit(solution)/shard_map/ppermute | solution.py:59
  393.6 6.3 %copy-start.1 = (bf16[1,3,48,8192]{3,2,1,0:T(8,128)(2,1)S(1)}, bf16[1,3,48,8192]{3,2,1,0:T(8,128)(2,1)}, u32[]{:S(2)}) copy-start(bf16[1,3,48,8192]{3,2,1,0:T(8,128)(2,1)} %param.12) | copy-start | bytes 7077892
  (20 other events, 53.7 us)
Sparse Core Ops, SparseCore 0:
  11.6 87.4 all-gather.7
  127.5 26.9 all-gather.9
  204.2 23.8 all-gather.5
